TPU v7x, 128 devices: a whole 4x4x4 slice. The times are simulated.
128 devices in a mesh: dp: 16 (over x, y_hi, core), tensor: 8 (over y_lo, z).
Axes of the slice: x: 4, y: 4 (y_hi: 2, y_lo: 2; y = y_hi * 2 + y_lo), z: 4, core: 2. Of those that a mesh axis runs over, the one named last changes fastest.
Arguments:
- wide_up: bfloat16 [4096, 16384], P(None, 'dp'), may hold values from -0.09375 to 0.09375
- wide_down: bfloat16 [16384, 4096], P('dp'), may hold values from -0.046875 to 0.046875
- narrow_up: bfloat16 [4096, 4096], P('dp', 'tensor'), may hold values from -0.09375 to 0.09375
- narrow_down: bfloat16 [4096, 4096], P('tensor', 'dp'), may hold values from -0.09375 to 0.09375
- wide_input: bfloat16 [2048, 4096], P('tensor'), may hold values from -6 to 6
- wide_preact: bfloat16 [2048, 16384], P('tensor', 'dp'), may hold values from -8 to 8
- narrow_input: bfloat16 [2048, 4096], P('dp'), may hold values from -6 to 6
- narrow_preact: bfloat16 [2048, 4096], P('dp', 'tensor'), may hold values from -8 to 8
- cotangent: bfloat16 [2048, 4096], P('dp', 'tensor'), may hold values from -6 to 6
Outputs:
- wide_input_grad: bfloat16 [2048, 4096], P('tensor', 'dp')
- wide_up_grad: bfloat16 [4096, 16384], P('tensor', 'dp')
- wide_down_grad: bfloat16 [16384, 4096], P('dp', 'tensor')
- narrow_up_grad: bfloat16 [4096, 4096], P('dp', 'tensor')
- narrow_down_grad: bfloat16 [4096, 4096], P('tensor', 'dp')
All inputs are finite; a program needn't handle non-finite values.
Results may differ from a plain program's by a relative error of at most 0.025.
Values may be sent and summed in bfloat16 or wider, within the bound.
No kernel may reach another device: no remote copies, remote signals or barrier semaphores. Data moves between devices by JAX's collectives and lax.ppermute only.
A program may use at most 128 MiB of HBM per device.

v0:
```python
import jax
import jax.numpy as jnp
from jax import lax
from jax.sharding import PartitionSpec as P


def silu_slope(values):
    sig = jax.nn.sigmoid(values)
    return sig * (1.0 + values * (1.0 - sig))


def contract_rows(left, right):
    return lax.dot_general(
        left, right, (((0,), (0,)), ((), ())), preferred_element_type=jnp.float32
    )


def contract_cols(left, right):
    return lax.dot_general(
        left, right, (((1,), (1,)), ((), ())), preferred_element_type=jnp.float32
    )


def body(
    wide_up,
    wide_down,
    narrow_up,
    narrow_down,
    wide_input,
    wide_preact,
    narrow_input,
    narrow_preact,
    cotangent,
):
    cot_full = lax.all_gather(cotangent, "tensor", axis=1, tiled=True)
    full_width = cot_full.shape[1]
    sliced = cot_full
    narrow_hidden_grad = contract_cols(
        sliced, lax.all_gather(narrow_down, "dp", axis=1, tiled=True)
    )
    narrow_pre = narrow_preact.astype(jnp.float32)
    narrow_act = jax.nn.silu(narrow_pre).astype(jnp.bfloat16)
    narrow_down_term = contract_rows(narrow_act, cot_full)
    narrow_down_grad = lax.psum_scatter(
        narrow_down_term.astype(jnp.bfloat16), "dp", scatter_dimension=1, tiled=True
    )
    narrow_pre_grad = (narrow_hidden_grad * silu_slope(narrow_pre)).astype(jnp.bfloat16)
    sliced = narrow_input
    narrow_up_grad = lax.psum_scatter(
        contract_rows(sliced, narrow_pre_grad).astype(jnp.bfloat16),
        "dp",
        scatter_dimension=0,
        tiled=True,
    )
    branch_part = contract_cols(
        narrow_pre_grad, lax.all_gather(narrow_up, "dp", axis=0, tiled=True)
    )
    shard_sum = lax.psum_scatter(
        branch_part.astype(jnp.bfloat16), "tensor", scatter_dimension=1, tiled=True
    ).astype(jnp.float32)
    local_grad = (cotangent.astype(jnp.float32) + shard_sum).astype(jnp.bfloat16)
    gathered = lax.all_gather(local_grad, "dp", axis=0, tiled=True)
    boundary_grad = lax.all_to_all(gathered, "tensor", split_axis=0, concat_axis=1, tiled=True)
    wide_hidden_grad = contract_cols(boundary_grad, wide_down)
    wide_pre = wide_preact.astype(jnp.float32)
    wide_act = jax.nn.silu(wide_pre).astype(jnp.bfloat16)
    wide_down_term = contract_rows(wide_act, boundary_grad)
    wide_down_grad = lax.psum_scatter(
        wide_down_term.astype(jnp.bfloat16), "tensor", scatter_dimension=1, tiled=True
    )
    wide_pre_grad = (wide_hidden_grad * silu_slope(wide_pre)).astype(jnp.bfloat16)
    sliced = wide_input
    wide_up_grad = lax.psum_scatter(
        contract_rows(sliced, wide_pre_grad).astype(jnp.bfloat16),
        "tensor",
        scatter_dimension=0,
        tiled=True,
    )
    input_term = contract_cols(wide_pre_grad, wide_up)
    input_share = lax.psum_scatter(
        input_term.astype(jnp.bfloat16), "dp", scatter_dimension=1, tiled=True
    ).astype(jnp.float32)
    share_width = full_width // lax.axis_size("dp")
    own_cols = lax.dynamic_slice_in_dim(
        boundary_grad, lax.axis_index("dp") * share_width, share_width, 1
    )
    wide_input_grad = (own_cols.astype(jnp.float32) + input_share).astype(jnp.bfloat16)
    return (wide_input_grad, wide_up_grad, wide_down_grad, narrow_up_grad, narrow_down_grad)


def solution(mesh):
    in_specs = (
        P(None, "dp"),
        P("dp", None),
        P("dp", "tensor"),
        P("tensor", "dp"),
        P("tensor", None),
        P("tensor", "dp"),
        P("dp", None),
        P("dp", "tensor"),
        P("dp", "tensor"),
    )
    out_specs = (
        P("tensor", "dp"),
        P("tensor", "dp"),
        P("dp", "tensor"),
        P("dp", "tensor"),
        P("tensor", "dp"),
    )
    return jax.shard_map(body, mesh=mesh, in_specs=in_specs, out_specs=out_specs, check_vma=False)
```

profile of v0, /device:TPU:0, one launch (start us, length us, event | category | flops | bytes accessed | tf_op | source)
XLA Modules:
  0.0 699.2 jit_solution(919450871897239223)
XLA Ops:
  7.2 0.7 all-gather.5.cloned.1.call-update
  8.0 0.7 all-gather.7.cloned.1.call-update
  8.7 0.7 all-gather.9.cloned.1.call-update
  9.4 41.9 %all-gather.5.cloned.1.call-done = bf16[128,4096]{1,0:T(8,128)(2,1)} async-done(((bf16[128,512]{1,0:T(8,128)(2,1)}), bf16[128,4096]{1,0:T(8,128)(2,1)}) %all-gather.5.cloned.1.call-update) | async-done | bytes 1048592 | tf_op jit(solution)/shard_map/all_gather | solution.py:35
  51.3 60.4 %all-gather.7.cloned.1.call-done = bf16[512,4096]{1,0:T(8,128)(2,1)} async-done(((bf16[512,256]{1,0:T(8,128)(2,1)}), bf16[512,4096]{1,0:T(8,128)(2,1)}) %all-gather.7.cloned.1.call-update) | async-done | bytes 4194320 | tf_op jit(solution)/shard_map/all_gather | solution.py:39
  111.7 4.0 fusion.2
  115.8 53.1 %all-gather.9.cloned.1.call-done = bf16[4096,512]{1,0:T(8,128)(2,1)} async-done(((bf16[256,512]{1,0:T(8,128)(2,1)}), bf16[4096,512]{1,0:T(8,128)(2,1)}) %all-gather.9.cloned.1.call-update) | async-done | bytes 4194320 | tf_op jit(solution)/shard_map/all_gather | solution.py:56
  168.8 4.6 convolution_convert_fusion.4
  173.5 0.0 all-gather.11.cloned.1.call-start
  173.5 38.2 %reduce-scatter.7.cloned.1.call-done = bf16[128,512]{1,0:T(8,128)(2,1)} async-done(((bf16[128,4096]{1,0:T(8,128)(2,1)}), bf16[128,512]{1,0:T(8,128)(2,1)}) %reduce-scatter.7.cloned.1.call-update) | async-done | bytes 131088 | tf_op jit(solution)/shard_map/reduce_scatter | solution.py:58
  211.7 1.6 add_convert_fusion.1
  213.4 3.2 fusion
  216.7 44.9 %all-gather.11.cloned.1.call-done = bf16[2048,512]{1,0:T(8,128)(2,1)} async-done(((bf16[128,512]{1,0:T(8,128)(2,1)}), bf16[2048,512]{1,0:T(8,128)(2,1)}) %all-gather.11.cloned.1.call-update) | async-done | bytes 2097168 | tf_op jit(solution)/shard_map/all_gather | solution.py:62
  261.6 31.9 %all_to_all.19 = bf16[8,256,512]{2,1,0:T(8,128)(2,1)S(1)} all-to-all(bf16[8,256,512]{2,1,0:T(8,128)(2,1)} %bitcast.26), channel_id=1, replica_groups=mesh['dp'=16,'tensor'=8] {'tensor'}, dimensions={0} | all-to-all | bytes 4194304 | tf_op jit(solution)/shard_map/all_to_all | solution.py:63
  293.5 0.3 copy.17
  293.7 1.4 copy-done.1
  295.1 6.3 fusion.1
  301.4 3.8 convolution_convert_fusion.3
  305.3 5.6 convert_bitcast_fusion
  311.0 0.2 reduce-scatter.17.cloned.1.call-start
  311.2 1.0 copy-done.3
  312.2 3.3 convolution_convert_fusion.1
  315.5 1.0 copy-done.7
  316.5 7.3 %convolution_convert_fusion = bf16[1024,4096]{1,0:T(8,128)(2,1)} fusion(bf16[256,4096]{1,0:T(8,128)(2,1)} %bitcast.24, bf16[256,1024]{1,0:T(8,128)(2,1)S(1)} %copy-done.7), kind=kOutput, calls=%fused_computation.1 | convolution fusion | flops 2153250816 | bytes 11010048 | tf_op jit(solution)/shard_map/dot_general | solution.py:13
  323.8 21.0 %reduce-scatter.15.cloned.1.call-done = bf16[256,512]{0,1:T(8,128)(2,1)} async-done(((bf16[4096,512]{0,1:T(8,128)(2,1)}), bf16[256,512]{0,1:T(8,128)(2,1)}) %reduce-scatter.15.cloned.1.call-update) | async-done | bytes 262160 | tf_op jit(solution)/shard_map/reduce_scatter | solution.py:49
  344.8 1.8 copy.16
  346.6 72.2 %reduce-scatter.9.cloned.1.call-done = bf16[256,256]{1,0:T(8,128)(2,1)} async-done(((bf16[256,4096]{1,0:T(8,128)(2,1)}), bf16[256,256]{1,0:T(8,128)(2,1)}) %reduce-scatter.9.cloned.1.call-update) | async-done | bytes 131088 | tf_op jit(solution)/shard_map/reduce_scatter | solution.py:80
  418.8 1.7 add_convert_fusion
  420.5 93.0 %reduce-scatter.11.cloned.1.call-done = bf16[512,1024]{0,1:T(8,128)(2,1)} async-done(((bf16[4096,1024]{0,1:T(8,128)(2,1)}), bf16[512,1024]{0,1:T(8,128)(2,1)}) %reduce-scatter.11.cloned.1.call-update) | async-done | bytes 1048592 | tf_op jit(solution)/shard_map/reduce_scatter | solution.py:73
  513.5 2.3 copy.15
  515.7 82.0 %reduce-scatter.17.cloned.1.call-done = bf16[512,256]{1,0:T(8,128)(2,1)} async-done(((bf16[512,4096]{1,0:T(8,128)(2,1)}), bf16[512,256]{1,0:T(8,128)(2,1)}) %reduce-scatter.17.cloned.1.call-update) | async-done | bytes 262160 | tf_op jit(solution)/shard_map/reduce_scatter | solution.py:44
  597.8 94.6 %reduce-scatter.13.cloned.1.call-done = bf16[1024,512]{1,0:T(8,128)(2,1)} async-done(((bf16[1024,4096]{1,0:T(8,128)(2,1)}), bf16[1024,512]{1,0:T(8,128)(2,1)}) %reduce-scatter.13.cloned.1.call-update) | async-done | bytes 1048592 | tf_op jit(solution)/shard_map/reduce_scatter | solution.py:68
  (33 shorter events, 0.5 us)
Async XLA Ops:
  7.2 298.1 %copy-start = (bf16[256,4096]{1,0:T(8,128)(2,1)S(1)}, bf16[256,4096]{1,0:T(8,128)(2,1)}, u32[]{:S(2)}) copy-start(bf16[256,4096]{1,0:T(8,128)(2,1)} %param.13) | copy-start | bytes 6291460
  7.2 44.2 %all-gather.5.cloned.1.call-start = ((), (), s32[]{:S(2)}) async-start(), calls=%async_computation.7 | async-start | bytes 1179648 | tf_op jit(solution)/shard_map/all_gather | solution.py:35
  7.9 103.8 %all-gather.7.cloned.1.call-start = ((), (), s32[]{:S(2)}) async-start(), calls=%async_computation.8 | async-start | bytes 4456448 | tf_op jit(solution)/shard_map/all_gather | solution.py:39
  8.7 160.1 %all-gather.9.cloned.1.call-start = ((), (), s32[]{:S(2)}) async-start(), calls=%async_computation.9 | async-start | bytes 4456448 | tf_op jit(solution)/shard_map/all_gather | solution.py:56
  9.4 202.3 %reduce-scatter.7.cloned.1.call-start = ((), (), s32[]{:S(2)}) async-start(), calls=%async_computation.10 | async-start | bytes 1179648 | tf_op jit(solution)/shard_map/reduce_scatter | solution.py:58
  115.7 96.0 %copy-start.4 = (bf16[128,512]{1,0:T(8,128)(2,1)S(1)}, bf16[128,512]{1,0:T(8,128)(2,1)}, u32[]{:S(2)}) copy-start(bf16[128,512]{1,0:T(8,128)(2,1)} %param.17) | copy-start | bytes 393220
  115.7 97.7 %copy-start.2 = (bf16[128,4096]{1,0:T(8,128)(2,1)S(1)}, bf16[128,4096]{1,0:T(8,128)(2,1)}, u32[]{:S(2)}) copy-start(bf16[128,4096]{1,0:T(8,128)(2,1)} %param.15) | copy-start | bytes 3145732
  173.5 88.1 %all-gather.11.cloned.1.call-start = ((), (), s32[]{:S(2)}) async-start(), calls=%async_computation.11 | async-start | bytes 2228224 | tf_op jit(solution)/shard_map/all_gather | solution.py:62
  213.4 131.5 %reduce-scatter.15.cloned.1.call-start = ((), (), s32[]{:S(2)}) async-start(), calls=%async_computation.15 | async-start | bytes 4456448 | tf_op jit(solution)/shard_map/reduce_scatter | solution.py:49
  216.7 202.2 %reduce-scatter.9.cloned.1.call-start = ((), (), s32[]{:S(2)}) async-start(), calls=%async_computation.12 | async-start | bytes 2228224 | tf_op jit(solution)/shard_map/reduce_scatter | solution.py:80
  261.6 33.5 %copy-start.6 = (bf16[256,1024]{1,0:T(8,128)(2,1)S(1)}, bf16[256,1024]{1,0:T(8,128)(2,1)}, u32[]{:S(2)}) copy-start(bf16[256,1024]{1,0:T(8,128)(2,1)} %param.14) | copy-start | bytes 1572868
  293.5 8.0 %slice-start = ((s8[8388608]{0:T(1024)(128)(4,1)}), s8[4194304]{0:T(1024)(128)(4,1)S(1)}, s32[]{:S(2)}) async-start(s8[8388608]{0:T(1024)(128)(4,1)} %bitcast.27), calls=%async_computation.17 | async-start | bytes 8388608
  293.7 1.4 copy-start.1
  295.1 6.3 slice-start.1
  305.3 208.2 %reduce-scatter.11.cloned.1.call-start = ((), (), s32[]{:S(2)}) async-start(), calls=%async_computation.13 | async-start | bytes 9437184 | tf_op jit(solution)/shard_map/reduce_scatter | solution.py:73
  311.0 1.2 copy-start.3
  311.0 1.2 copy-start.5
  311.0 286.8 %reduce-scatter.17.cloned.1.call-start = ((), (), s32[]{:S(2)}) async-start(), calls=%async_computation.16 | async-start | bytes 4456448 | tf_op jit(solution)/shard_map/reduce_scatter | solution.py:44
  315.5 1.1 copy-start.7
  315.5 376.8 %reduce-scatter.13.cloned.1.call-start = ((), (), s32[]{:S(2)}) async-start(), calls=%async_computation.14 | async-start | bytes 9437184 | tf_op jit(solution)/shard_map/reduce_scatter | solution.py:68
Sparse Core Ops, SparseCore 0:
  9.7 41.6 all-gather.4
  53.6 58.0 all-gather.6
  114.1 54.6 all-gather.8
  173.6 38.0 reduce-scatter.6
  214.6 46.9 all-gather.10
  265.5 79.2 reduce-scatter.14
  349.3 69.5 reduce-scatter.8
  421.4 92.0 reduce-scatter.10
  518.7 79.0 reduce-scatter.16
  600.6 91.6 reduce-scatter.12
where the time goes:
time: 700 us; the launch traced here: 699 us
  waiting for transfers between devices  603 us (86%)
  matrix products  38.2 us (5%)
  blocking collectives  31.9 us (5%)
  between operations  14.3 us (2%)
  local copies, waits for them, and re-layouts  7.7 us (1%)
    reduce_scatter x1, waiting for transfers between devices, body(): lax.psum_scatter(wide_down_term.astype(jnp.bfloat16), 'tensor', scatter_d...  94.6 us
    reduce_scatter x1, waiting for transfers between devices, body(): lax.psum_scatter(contract_rows(sliced, wide_pre_grad).astype(jnp.bfloat16...  93 us
    reduce_scatter x1, waiting for transfers between devices, body(): lax.psum_scatter(narrow_down_term.astype(jnp.bfloat16), 'dp', scatter_dim...  82 us
    reduce_scatter x1, waiting for transfers between devices, body(): lax.psum_scatter(input_term.astype(jnp.bfloat16), 'dp', scatter_dimension...  72.2 us
    all_gather x1, waiting for transfers between devices, body(): lax.all_gather(narrow_down, 'dp', axis=1, tiled=True)  60.4 us
    all_gather x1, waiting for transfers between devices, body(): lax.all_gather(narrow_up, 'dp', axis=0, tiled=True)  53.1 us
    all_gather x1, waiting for transfers between devices, body(): gathered = lax.all_gather(local_grad, 'dp', axis=0, tiled=True)  44.9 us
    all_gather x1, waiting for transfers between devices, body(): cot_full = lax.all_gather(cotangent, 'tensor', axis=1, tiled=True)  41.9 us
  transfers between devices with their start and end apart: 10, of which 10 were waited for; matrix products, arithmetic and copies ran while one was open for 6% of the time, Pallas kernels for 0%

commit v1 on v0

v1 whole, which is shorter than its diff:
```python
import jax
import jax.numpy as jnp
from jax import lax
from jax.sharding import Mesh, PartitionSpec as P

BF16 = jnp.bfloat16
F32 = jnp.float32
CHIPS = ("x", "yh")
TOK = ("yl", "z")


def silu_slope(values):
    sig = jax.nn.sigmoid(values)
    return sig * (1.0 + values * (1.0 - sig))


def dot(left, right, dims):
    return lax.dot_general(left, right, (dims, ((), ())), preferred_element_type=F32)


def swap_cores(value):
    return lax.ppermute(value, "c", [(0, 1), (1, 0)])


def swap_pair(value):
    return lax.ppermute(value, "yl", [(0, 1), (1, 0)])


def shift_z(value, by):
    return lax.ppermute(value, "z", [(i, (i + by) % 4) for i in range(4)])


def exchange(value, axes):
    return lax.all_to_all(value, axes, 0, 0, tiled=True)


def gather_all(value, axes, count):
    return exchange(jnp.broadcast_to(value[None], (count,) + value.shape), axes)


def pick(value, index, axis):
    return lax.dynamic_index_in_dim(value, index, axis, keepdims=False)


def z_columns(rows, z, core):
    cols = rows.reshape(rows.shape[0], 2, 4, -1)
    half = rows.shape[0] // 2
    own = pick(cols, z, 2).reshape(rows.shape[0], -1)
    mine = lax.dynamic_slice_in_dim(cols, core * half, half, 0)
    got = []
    for by in (1, 3, 2):
        got.append(shift_z(pick(mine, (z + by) % 4, 2).reshape(half, -1), by))
    got = jnp.stack(got)
    other = swap_cores(got)
    first = jnp.where(core == 0, got, other)
    second = jnp.where(core == 0, other, got)
    both = jnp.concatenate([first, second], axis=1)
    return jnp.concatenate([own[None], both]).reshape(4 * rows.shape[0], -1)


def z_rows(block):
    return jnp.concatenate([block] + [shift_z(block, by) for by in (1, 3, 2)])


def body(
    wide_up,
    wide_down,
    narrow_up,
    narrow_down,
    wide_input,
    wide_preact,
    narrow_input,
    narrow_preact,
    cotangent,
):
    core = lax.axis_index("c")
    z = lax.axis_index("z")
    yl = lax.axis_index("yl")
    chip = lax.axis_index("x") * 2 + lax.axis_index("yh")
    tok = yl * 4 + z
    tokens, width = cotangent.shape
    n_t, n_d = 8, 8
    half = narrow_down.shape[1]

    cot_rows = gather_all(cotangent, TOK, n_t)
    down_cols = gather_all(narrow_down, CHIPS, n_d)
    cot_cols = cot_rows.reshape(n_d, tokens, 2, half)
    keep = pick(cot_cols, core, 2)
    come = swap_cores(pick(cot_cols, 1 - core, 2))
    pre_f = narrow_preact.astype(F32)
    hid_keep = jnp.einsum("dtk,dfk->tf", keep, down_cols, preferred_element_type=F32)
    hid_send = jnp.einsum("dtk,dfk->tf", come, down_cols, preferred_element_type=F32)
    hidden_grad = hid_keep + swap_cores(hid_send)
    narrow_pre_grad = (hidden_grad * silu_slope(pre_f)).astype(BF16)

    pre_all = gather_all(narrow_pre_grad, CHIPS, n_d).reshape(n_d * tokens, -1)
    act_all = gather_all(jax.nn.silu(pre_f).astype(BF16), CHIPS, n_d).reshape(n_d * tokens, -1)
    cot_own = exchange(cot_rows, CHIPS)
    in_own = exchange(
        narrow_input.reshape(tokens, n_d, -1).transpose(1, 0, 2), CHIPS
    ).reshape(n_d * tokens, -1)

    up_other = swap_cores(narrow_up)
    up_first = jnp.where(core == 0, narrow_up, up_other)
    up_second = jnp.where(core == 0, up_other, narrow_up)
    up_rows = jnp.concatenate([up_first, up_second])
    share = dot(pre_all, up_rows, ((1,), (1,))).astype(BF16)
    share = exchange(share.reshape(n_t, tokens, -1), TOK)
    own = pick(cot_own, tok, 0).astype(F32) + jnp.sum(share.astype(F32), axis=0)
    own = own.astype(BF16)
    rows = gather_all(own, CHIPS, n_d).transpose(1, 0, 2).reshape(tokens, -1)
    rows_other = swap_cores(rows)
    boundary = jnp.concatenate(
        [jnp.where(core == 0, rows, rows_other), jnp.where(core == 0, rows_other, rows)]
    )

    wide_pre = wide_preact.astype(F32)
    wide_hidden_grad = dot(boundary, wide_down, ((1,), (1,)))
    wide_pre_grad = (wide_hidden_grad * silu_slope(wide_pre)).astype(BF16)
    term = dot(wide_pre_grad, wide_up, ((1,), (1,)))
    term = term.reshape(2 * tokens, n_d, 2, half)
    term_keep = pick(term, core, 2)
    term_come = swap_cores(pick(term, 1 - core, 2).astype(BF16))
    term_chip = (term_keep + term_come.astype(F32)).astype(BF16).transpose(1, 0, 2)
    term_all = exchange(term_chip, CHIPS)
    own_cols = lax.dynamic_slice_in_dim(boundary, (chip * 2 + core) * half, half, 1)
    wide_input_grad = (own_cols.astype(F32) + jnp.sum(term_all.astype(F32), axis=0)).astype(BF16)

    wide_act = jax.nn.silu(wide_pre).astype(BF16)
    act_rows = z_rows(wide_act)
    bound_cols = z_columns(boundary, z, core)
    input_cols = z_columns(wide_input, z, core)
    grad_rows = z_rows(wide_pre_grad)
    side = bound_cols.shape[1] // 2

    def take(cols, which):
        return lax.dynamic_slice_in_dim(cols, which * side, side, 1)

    down_send = dot(act_rows, take(bound_cols, 1 - yl), ((0,), (0,))).astype(BF16)
    down_come = swap_pair(down_send)
    down_keep = dot(act_rows, take(bound_cols, yl), ((0,), (0,)))
    wide_down_grad = (down_keep + down_come.astype(F32)).astype(BF16)
    up_send = dot(take(input_cols, 1 - yl), grad_rows, ((0,), (0,))).astype(BF16)
    up_come = swap_pair(up_send)
    up_keep = dot(take(input_cols, yl), grad_rows, ((0,), (0,)))
    wide_up_grad = (up_keep + up_come.astype(F32)).astype(BF16)

    cot_tok = cot_own.reshape(n_d * tokens, -1)

    def core_sum(part, axis):
        size = part.shape[axis] // 2
        send = lax.dynamic_slice_in_dim(part, (1 - core) * size, size, axis).astype(BF16)
        mine = lax.dynamic_slice_in_dim(part, core * size, size, axis)
        return (mine + swap_cores(send).astype(F32)).astype(BF16)

    narrow_down_grad = core_sum(dot(act_all, cot_tok, ((0,), (0,))), 1)
    narrow_up_grad = core_sum(dot(in_own, pre_all, ((0,), (0,))), 0)
    return (wide_input_grad, wide_up_grad, wide_down_grad, narrow_up_grad, narrow_down_grad)


def solution(mesh):
    fine = Mesh(mesh.devices.reshape(4, 2, 2, 2, 4), ("x", "yh", "c", "yl", "z"))
    dp = ("x", "yh", "c")
    tensor = ("yl", "z")
    in_specs = (
        P(None, dp),
        P(dp, None),
        P(dp, tensor),
        P(tensor, dp),
        P(tensor, None),
        P(tensor, dp),
        P(dp, None),
        P(dp, tensor),
        P(dp, tensor),
    )
    out_specs = (
        P(tensor, dp),
        P(tensor, dp),
        P(dp, tensor),
        P(dp, tensor),
        P(tensor, dp),
    )
    return jax.shard_map(body, mesh=fine, in_specs=in_specs, out_specs=out_specs, check_vma=False)
```

time: 700 us -> 325 us (0.46)
  waiting for transfers between devices: 603 us -> 112 us
  starting transfers between devices: 0.58 us -> 53.6 us
  local copies, waits for them, and re-layouts: 7.7 us -> 55.9 us
  other arithmetic: 3.25 us -> 20.9 us
  between operations: 14.3 us -> 1.23 us
  blocking collectives: 31.9 us -> 42.1 us
    reduce_scatter x6 -> x0, waiting for transfers between devices: 401 us -> none  [the longest x1 94.6 us: body(): lax.psum_scatter(wide_down_term.astype(jnp.bfloat16), 'tensor', scatter_d...]
    all_gather x4 -> x0, waiting for transfers between devices: 200 us -> none  [the longest x1 60.4 us: body(): lax.all_gather(narrow_down, 'dp', axis=1, tiled=True)]
    all_to_all x0 -> x7, waiting for transfers between devices: none -> 66.8 us  [exchange(): return lax.all_to_all(value, axes, 0, 0, tiled=True)]
    ppermute x0 -> x23, waiting for transfers between devices: none -> 45.3 us  [the longest x2 27.1 us: swap_pair(): return lax.ppermute(value, 'yl', [(0, 1), (1, 0)])]
    all_to_all x0 -> x7, starting transfers between devices: none -> 31.3 us  [exchange(): return lax.all_to_all(value, axes, 0, 0, tiled=True)]
    ppermute x0 -> x23, starting transfers between devices: none -> 22.4 us  [the longest x12 16.2 us: shift_z(): return lax.ppermute(value, 'z', [(i, (i + by) % 4) for i in range(4)])]
    dynamic_slice x0 -> x7, local copies, waits for them, and re-layouts: none -> 17.9 us  [pick(): return lax.dynamic_index_in_dim(value, index, axis, keepdims=False)]
    concatenate x0 -> x3, local copies, waits for them, and re-layouts: none -> 10.8 us  [the longest x2 6.48 us: z_columns(): return jnp.concatenate([own[None], both]).reshape(4 * rows.shape[0], -1)]
  transfers between devices with their start and end apart: 10 -> 30, of which waited for: 10 -> 15; matrix products, arithmetic and copies ran while one was open for 6% -> 32% of each run, Pallas kernels for 0% -> 0%
where the time goes in v1:
time: 325 us; the launch traced here: 323 us
  waiting for transfers between devices  112 us (34%)
  local copies, waits for them, and re-layouts  55.9 us (17%)
  starting transfers between devices  53.6 us (16%)
  blocking collectives  42.1 us (13%)
  matrix products  37.4 us (12%)
  other arithmetic  20.9 us (6%)
    all_to_all x7, waiting for transfers between devices, exchange(): return lax.all_to_all(value, axes, 0, 0, tiled=True)  66.8 us
    all_to_all x2, blocking collectives, exchange(): return lax.all_to_all(value, axes, 0, 0, tiled=True)  42.1 us
    dot_general x9, matrix products, dot(): lax.dot_general(left, right, (dims, ((), ())), preferred_element_type=F32)  34.8 us
    all_to_all x7, starting transfers between devices, exchange(): return lax.all_to_all(value, axes, 0, 0, tiled=True)  31.3 us
    ppermute x2, waiting for transfers between devices, swap_pair(): return lax.ppermute(value, 'yl', [(0, 1), (1, 0)])  27.1 us
    dynamic_slice x7, local copies, waits for them, and re-layouts, pick(): return lax.dynamic_index_in_dim(value, index, axis, keepdims=False)  17.9 us
    ppermute x12, starting transfers between devices, shift_z(): return lax.ppermute(value, 'z', [(i, (i + by) % 4) for i in range(4)])  16.2 us
    ppermute x12, waiting for transfers between devices, shift_z(): return lax.ppermute(value, 'z', [(i, (i + by) % 4) for i in range(4)])  14 us
  transfers between devices with their start and end apart: 30, of which 15 were waited for; matrix products, arithmetic and copies ran while one was open for 32% of the time, Pallas kernels for 0%

profile of v1, /device:TPU:0, one launch (start us, length us, event | category | flops | bytes accessed | tf_op | source)
XLA Modules:
  0.0 323.2 jit_solution(12249003573476268955)
XLA Ops:
  1.7 22.1 %all_to_all.45 = bf16[8,128,512]{2,1,0:T(8,128)(2,1)} all-to-all(bf16[8,128,512]{2,1,0:T(8,128)(2,1)S(1)} %broadcast_in_dim.12), channel_id=1, replica_groups=mesh['x'=4,'yh'=2,'c'=2,'yl'=2,'z'=4] {'yl','z'}, dimensions={0} | all-to-all | bytes 2097152 | tf_op jit(solution)/shard_map/all_to_all | solution.py:34
  25.2 6.6 %all-to-all-start.2 = ((bf16[8,512,256]{2,1,0:T(8,128)(2,1)}), bf16[8,512,256]{2,1,0:T(8,128)(2,1)S(1)}, u32[]{:S(2)}, u32[]{:S(2)}) async-start(bf16[8,512,256]{2,1,0:T(8,128)(2,1)} %broadcast_in_dim.13), calls=%async_computation.2 | async-start | bytes 4194304 | tf_op jit(solution)/shard_map/all_to_all | solution.py:34
  33.2 3.4 %constant_dynamic-slice_fusion.10 = (bf16[8,128,1,256]{3,2,1,0:T(2,128)(2,1)S(1)}, bf16[8,128,1,256]{3,2,1,0:T(2,128)(2,1)}) fusion(bf16[8,128,2,256]{3,2,1,0:T(2,128)(2,1)S(1)} %reshape.75, s32[]{:T(128)S(6)} %select_n.131, s32[]{:T(128)S(6)} %select_n.130), kind=kLoop, calls=%fused_computation.89 | loop fusion | bytes 2097160 | tf_op jit(solution)/shard_map/jit(dynamic_index_in_dim)/dynamic_slice | solution.py:42
  38.9 21.3 %all-to-all-done.2 = bf16[8,512,256]{2,1,0:T(8,128)(2,1)S(1)} async-done(((bf16[8,512,256]{2,1,0:T(8,128)(2,1)}), bf16[8,512,256]{2,1,0:T(8,128)(2,1)S(1)}, u32[]{:S(2)}, u32[]{:S(2)}) %all-to-all-start.2) | async-done | bytes 2097184 | tf_op jit(solution)/shard_map/all_to_all | solution.py:34
  64.1 20.0 %all_to_all.46 = bf16[8,128,512]{1,2,0:T(8,128)(2,1)S(1)} all-to-all(bf16[8,128,512]{1,2,0:T(8,128)(2,1)S(1)} %broadcast_in_dim.14), channel_id=1, replica_groups=mesh['x'=4,'yh'=2,'c'=2,'yl'=2,'z'=4] {'x','yh'}, dimensions={0} | all-to-all | bytes 2097152 | tf_op jit(solution)/shard_map/all_to_all | solution.py:34
  84.1 3.6 %all-to-all-start.1 = ((bf16[8,128,512]{2,1,0:T(8,128)(2,1)}), bf16[8,128,512]{2,1,0:T(8,128)(2,1)S(1)}, u32[]{:S(2)}, u32[]{:S(2)}) async-start(bf16[8,128,512]{2,1,0:T(8,128)(2,1)} %all_to_all.45), calls=%async_computation.1 | async-start | bytes 2097152 | tf_op jit(solution)/shard_map/all_to_all | solution.py:34
  93.2 9.8 %all-to-all-done.1 = bf16[8,128,512]{2,1,0:T(8,128)(2,1)S(1)} async-done(((bf16[8,128,512]{2,1,0:T(8,128)(2,1)}), bf16[8,128,512]{2,1,0:T(8,128)(2,1)S(1)}, u32[]{:S(2)}, u32[]{:S(2)}) %all-to-all-start.1) | async-done | bytes 1048608 | tf_op jit(solution)/shard_map/all_to_all | solution.py:34
  103.0 3.6 %all-to-all-start.4 = ((bf16[8,128,512]{2,1,0:T(8,128)(2,1)}), bf16[8,128,512]{2,1,0:T(8,128)(2,1)S(1)}, u32[]{:S(2)}, u32[]{:S(2)}) async-start(bf16[8,128,512]{2,1,0:T(8,128)(2,1)} %bitcast.5), calls=%async_computation.4 | async-start | bytes 2097152 | tf_op jit(solution)/shard_map/all_to_all | solution.py:34
  109.5 11.6 %all-to-all-done.4 = bf16[8,128,512]{2,1,0:T(8,128)(2,1)S(1)} async-done(((bf16[8,128,512]{2,1,0:T(8,128)(2,1)}), bf16[8,128,512]{2,1,0:T(8,128)(2,1)S(1)}, u32[]{:S(2)}, u32[]{:S(2)}) %all-to-all-start.4) | async-done | bytes 1048608 | tf_op jit(solution)/shard_map/all_to_all | solution.py:34
  121.1 4.3 %all-to-all-start.7 = ((bf16[8,128,512]{2,1,0:T(8,128)(2,1)}), bf16[8,128,512]{2,1,0:T(8,128)(2,1)}, u32[]{:S(2)}, u32[]{:S(2)}) async-start(bf16[8,128,512]{2,1,0:T(8,128)(2,1)} %bitcast.30), calls=%async_computation.7 | async-start | bytes 2097152 | tf_op jit(solution)/shard_map/all_to_all | solution.py:34
  125.4 3.3 %copy.65 = bf16[256,4096]{0,1:T(8,128)(2,1)S(1)} copy(bf16[256,4096]{1,0:T(8,128)(2,1)} %param.13) | data formatting | bytes 4194304 | tf_op args[4]
  136.0 5.0 %all-to-all-done.7 = bf16[8,128,512]{2,1,0:T(8,128)(2,1)} async-done(((bf16[8,128,512]{2,1,0:T(8,128)(2,1)}), bf16[8,128,512]{2,1,0:T(8,128)(2,1)}, u32[]{:S(2)}, u32[]{:S(2)}) %all-to-all-start.7) | async-done | bytes 1048608 | tf_op jit(solution)/shard_map/all_to_all | solution.py:34
  142.1 4.2 %all-to-all-start.5 = ((bf16[8,128,512]{2,1,0:T(8,128)(2,1)}), bf16[8,128,512]{2,1,0:T(8,128)(2,1)S(1)}, u32[]{:S(2)}, u32[]{:S(2)}) async-start(bf16[8,128,512]{2,1,0:T(8,128)(2,1)} %broadcast_in_dim.16), calls=%async_computation.5 | async-start | bytes 2097152 | tf_op jit(solution)/shard_map/all_to_all | solution.py:34
  151.3 10.4 %all-to-all-done.5 = bf16[8,128,512]{2,1,0:T(8,128)(2,1)S(1)} async-done(((bf16[8,128,512]{2,1,0:T(8,128)(2,1)}), bf16[8,128,512]{2,1,0:T(8,128)(2,1)S(1)}, u32[]{:S(2)}, u32[]{:S(2)}) %all-to-all-start.5) | async-done | bytes 1048608 | tf_op jit(solution)/shard_map/all_to_all | solution.py:34
  163.8 4.2 %all-to-all-start.8 = ((bf16[8,128,512]{1,2,0:T(8,128)(2,1)}), bf16[8,128,512]{1,2,0:T(8,128)(2,1)}, u32[]{:S(2)}, u32[]{:S(2)}) async-start(bf16[8,128,512]{1,2,0:T(8,128)(2,1)} %broadcast_in_dim.17), calls=%async_computation.8 | async-start | bytes 2097152 | tf_op jit(solution)/shard_map/all_to_all | solution.py:34
  176.9 6.6 %all-to-all-done.8 = bf16[8,128,512]{1,2,0:T(8,128)(2,1)} async-done(((bf16[8,128,512]{1,2,0:T(8,128)(2,1)}), bf16[8,128,512]{1,2,0:T(8,128)(2,1)}, u32[]{:S(2)}, u32[]{:S(2)}) %all-to-all-start.8) | async-done | bytes 1048608 | tf_op jit(solution)/shard_map/all_to_all | solution.py:34
  189.4 5.9 %fusion.1 = bf16[256,1024]{1,0:T(8,128)(2,1)S(1)} fusion(bf16[1024,4096]{1,0:T(8,128)(2,1)} %param.10, bf16[256,1024]{1,0:T(8,128)(2,1)S(1)} %copy-done.13, bf16[128,4096]{1,0:T(8,128)(2,1)S(1)} %get-tuple-element.37, bf16[128,4096]{1,0:T(8,128)(2,1)S(1)} %get-tuple-element.36), kind=kOutput, calls=%fused_computation.23 | convolution fusion | flops 2154299392 | bytes 11534336 | tf_op jit(solution)/shard_map/dot_general | solution.py:18
  195.3 4.3 %copy.67 = bf16[256,4096]{0,1:T(8,128)(2,1)} copy(bf16[256,4096]{1,0:T(8,128)(2,1)} %pad_maximum_fusion) | data formatting | bytes 4194304 | tf_op jit(solution)/shard_map/concatenate | solution.py:113
  206.7 7.8 %fusion.39 = f32[256,4096]{1,0:T(8,128)} fusion(bf16[256,1024]{1,0:T(8,128)(2,1)S(1)} %fusion.1, bf16[4096,1024]{1,0:T(8,128)(2,1)} %param.9), kind=kOutput, calls=%fused_computation.96 | convolution fusion | flops 2147483648 | bytes 13107200 | tf_op jit(solution)/shard_map/dot_general | solution.py:18
  214.5 6.6 %reshape.79 = f32[256,8,2,256]{3,2,1,0:T(2,128)} reshape(f32[256,4096]{1,0:T(8,128)} %fusion.39) | data formatting | bytes 8388608 | tf_op jit(solution)/shard_map/reshape | solution.py:121
  221.1 4.3 %constant_dynamic-slice_fusion.8 = bf16[256,8,1,256]{3,2,1,0:T(2,128)(2,1)S(1)} fusion(f32[256,8,2,256]{3,2,1,0:T(2,128)} %reshape.79, s32[]{:T(128)S(6)} %select_n.131), kind=kLoop, calls=%fused_computation.87 | loop fusion | bytes 2097156 | tf_op jit(solution)/shard_map/jit(dynamic_index_in_dim)/dynamic_slice | solution.py:42
  233.6 4.5 %constant_dynamic-slice_fusion.9 = f32[256,8,1,256]{3,2,1,0:T(1,128)S(1)} fusion(f32[256,8,2,256]{3,2,1,0:T(2,128)} %reshape.79, s32[]{:T(128)S(6)} %select_n.130), kind=kLoop, calls=%fused_computation.88 | loop fusion | bytes 4194308 | tf_op jit(solution)/shard_map/jit(dynamic_index_in_dim)/dynamic_slice | solution.py:42
  240.0 5.1 %collective-permute-done.11 = bf16[256,1024]{1,0:T(8,128)(2,1)S(1)} collective-permute-done((bf16[256,1024]{1,0:T(8,128)(2,1)}, bf16[256,1024]{1,0:T(8,128)(2,1)S(1)}, u32[]{:S(2)}, u32[]{:S(2)}) %collective-permute-start.11) | collective-permute-done | bytes 524320 | tf_op jit(solution)/shard_map/ppermute | solution.py:30
  246.1 8.1 %collective-permute-done.10 = bf16[256,1024]{1,0:T(8,128)(2,1)S(1)} collective-permute-done((bf16[256,1024]{1,0:T(8,128)(2,1)}, bf16[256,1024]{1,0:T(8,128)(2,1)S(1)}, u32[]{:S(2)}, u32[]{:S(2)}) %collective-permute-start.10) | collective-permute-done | bytes 524320 | tf_op jit(solution)/shard_map/ppermute | solution.py:30
  259.1 2.9 collective-permute-start.12
  264.7 4.8 %all-to-all-start.6 = ((bf16[8,256,256]{2,1,0:T(8,128)(2,1)}), bf16[8,256,256]{2,1,0:T(8,128)(2,1)S(1)}, u32[]{:S(2)}, u32[]{:S(2)}) async-start(bf16[8,256,256]{2,1,0:T(8,128)(2,1)} %copy.63), calls=%async_computation.6 | async-start | bytes 2097152 | tf_op jit(solution)/shard_map/all_to_all | solution.py:34
  272.7 4.0 %copy.68 = bf16[4,256,1024]{2,1,0:T(8,128)(2,1)} copy(bf16[4,256,1024]{1,2,0:T(8,128)(2,1)} %maximum_maximum_fusion.1) | data formatting | bytes 4194304 | tf_op jit(solution)/shard_map/concatenate | solution.py:58
  277.5 4.3 %convolution_convert_fusion = bf16[1024,512]{1,0:T(8,128)(2,1)} fusion(bf16[1024,1024]{1,0:T(8,128)(2,1)} %bitcast.85, s32[]{:T(128)S(6)} %select_n.154, bf16[256,1024]{1,0:T(8,128)(2,1)} %collective-permute-done.15, bf16[256,1024]{1,0:T(8,128)(2,1)} %collective-permute-done.14, bf16[256,1024]{1,0:T(8,128)(2,1)} %collective-permute-done.13, ...), kind=kOutput, calls=%fused_computation.17 | convolution fusion | flops 1082654720 | bytes 4194308 | tf_op jit(solution)/shard_map/dot_general | solution.py:18
  285.5 9.3 %collective-permute-done.12 = bf16[512,1024]{1,0:T(8,128)(2,1)} collective-permute-done((bf16[512,1024]{1,0:T(8,128)(2,1)}, bf16[512,1024]{1,0:T(8,128)(2,1)}, u32[]{:S(2)}, u32[]{:S(2)}) %collective-permute-start.12) | collective-permute-done | bytes 1048608 | tf_op jit(solution)/shard_map/ppermute | solution.py:26
  294.8 3.5 %add_convert_fusion.1 = bf16[512,1024]{1,0:T(8,128)(2,1)} fusion(bf16[512,1024]{1,0:T(8,128)(2,1)} %collective-permute-done.12, bf16[1024,1024]{1,0:T(8,128)(2,1)S(1)} %bitcast.84, s32[]{:T(128)S(6)} %select_n.153, bf16[256,1024]{1,0:T(8,128)(2,1)S(1)} %copy-done.22, bf16[256,1024]{1,0:T(8,128)(2,1)S(1)} %copy-done.24, ...), kind=kOutput, calls=%fused_computation.11 | convolution fusion | flops 1083703296 | bytes 5242884 | tf_op jit(solution)/shard_map/dot_general | solution.py:18
  301.3 17.8 %collective-permute-done.20 = bf16[1024,512]{1,0:T(8,128)(2,1)} collective-permute-done((bf16[1024,512]{1,0:T(8,128)(2,1)}, bf16[1024,512]{1,0:T(8,128)(2,1)}, u32[]{:S(2)}, u32[]{:S(2)}) %collective-permute-start.20) | collective-permute-done | bytes 1048608 | tf_op jit(solution)/shard_map/ppermute | solution.py:26
  319.0 4.1 %add_convert_fusion = bf16[1024,512]{1,0:T(8,128)(2,1)} fusion(bf16[1024,512]{1,0:T(8,128)(2,1)} %collective-permute-done.20, bf16[1024,1024]{1,0:T(8,128)(2,1)S(1)} %bitcast.86, s32[]{:T(128)S(6)} %select_n.153, bf16[256,1024]{1,0:T(8,128)(2,1)} %collective-permute-done.15, bf16[256,1024]{1,0:T(8,128)(2,1)} %collective-permute-done.14, ...), kind=kOutput, calls=%fused_computation.10 | convolution fusion | flops 1083703296 | bytes 5242884 | tf_op jit(solution)/shard_map/dot_general | solution.py:18
  (143 shorter events, 84.8 us)
Async XLA Ops:
  25.2 34.9 %all-to-all-start.2 = ((bf16[8,512,256]{2,1,0:T(8,128)(2,1)}), bf16[8,512,256]{2,1,0:T(8,128)(2,1)S(1)}, u32[]{:S(2)}, u32[]{:S(2)}) async-start(bf16[8,512,256]{2,1,0:T(8,128)(2,1)} %broadcast_in_dim.13), calls=%async_computation.2 | async-start | bytes 4194304 | tf_op jit(solution)/shard_map/all_to_all | solution.py:34
  36.6 25.5 %copy-start.2 = (bf16[8,128,1,256]{3,2,1,0:T(2,128)(2,1)S(1)}, bf16[8,128,1,256]{3,2,1,0:T(2,128)(2,1)}, u32[]{:S(2)}) copy-start(bf16[8,128,1,256]{3,2,1,0:T(2,128)(2,1)} %get-tuple-element.43) | copy-start | bytes 1572868
  36.7 2.1 collective-permute-start
  62.0 1.6 collective-permute-start.1
  64.1 23.6 %copy-start.16 = (bf16[256,512]{1,0:T(8,128)(2,1)S(1)}, bf16[256,512]{1,0:T(8,128)(2,1)}, u32[]{:S(2)}) copy-start(bf16[256,512]{1,0:T(8,128)(2,1)} %param.11) | copy-start | bytes 786436
  84.1 18.9 %all-to-all-start.1 = ((bf16[8,128,512]{2,1,0:T(8,128)(2,1)}), bf16[8,128,512]{2,1,0:T(8,128)(2,1)S(1)}, u32[]{:S(2)}, u32[]{:S(2)}) async-start(bf16[8,128,512]{2,1,0:T(8,128)(2,1)} %all_to_all.45), calls=%async_computation.1 | async-start | bytes 2097152 | tf_op jit(solution)/shard_map/all_to_all | solution.py:34
  87.7 1.6 collective-permute-start.2
  103.0 18.1 %all-to-all-start.4 = ((bf16[8,128,512]{2,1,0:T(8,128)(2,1)}), bf16[8,128,512]{2,1,0:T(8,128)(2,1)S(1)}, u32[]{:S(2)}, u32[]{:S(2)}) async-start(bf16[8,128,512]{2,1,0:T(8,128)(2,1)} %bitcast.5), calls=%async_computation.4 | async-start | bytes 2097152 | tf_op jit(solution)/shard_map/all_to_all | solution.py:34
  121.1 19.9 %all-to-all-start.7 = ((bf16[8,128,512]{2,1,0:T(8,128)(2,1)}), bf16[8,128,512]{2,1,0:T(8,128)(2,1)}, u32[]{:S(2)}, u32[]{:S(2)}) async-start(bf16[8,128,512]{2,1,0:T(8,128)(2,1)} %bitcast.30), calls=%async_computation.7 | async-start | bytes 2097152 | tf_op jit(solution)/shard_map/all_to_all | solution.py:34
  129.8 16.4 %collective-permute-start.7 = (bf16[128,1024]{0,1:T(8,128)(2,1)}, bf16[128,1024]{0,1:T(8,128)(2,1)S(1)}, u32[]{:S(2)}, u32[]{:S(2)}) collective-permute-start(bf16[128,1024]{0,1:T(8,128)(2,1)} %bitcast.17), channel_id=1, source_target_pairs={{0,2},{1,3},{2,0},{3,1},{4,6},{5,7},{6,4},{7,5},{8,10},{9,11},{10,... | collective-permute-start | bytes 786440 | tf_op jit(solution)/shard_map/ppermute | solution.py:30
  131.7 14.6 %collective-permute-start.5 = (bf16[128,1024]{0,1:T(8,128)(2,1)}, bf16[128,1024]{0,1:T(8,128)(2,1)}, u32[]{:S(2)}, u32[]{:S(2)}) collective-permute-start(bf16[128,1024]{0,1:T(8,128)(2,1)} %bitcast.13), channel_id=1, source_target_pairs={{0,1},{1,2},{2,3},{3,0},{4,5},{5,6},{6,7},{7,4},{8,9},{9,10},{10,1... | collective-permute-start | bytes 786440 | tf_op jit(solution)/shard_map/ppermute | solution.py:30
  132.2 14.1 %collective-permute-start.6 = (bf16[128,1024]{0,1:T(8,128)(2,1)}, bf16[128,1024]{0,1:T(8,128)(2,1)}, u32[]{:S(2)}, u32[]{:S(2)}) collective-permute-start(bf16[128,1024]{0,1:T(8,128)(2,1)} %bitcast.15), channel_id=1, source_target_pairs={{0,3},{1,0},{2,1},{3,2},{4,7},{5,4},{6,5},{7,6},{8,11},{9,8},{10,9... | collective-permute-start | bytes 786440 | tf_op jit(solution)/shard_map/ppermute | solution.py:30
  142.1 19.6 %all-to-all-start.5 = ((bf16[8,128,512]{2,1,0:T(8,128)(2,1)}), bf16[8,128,512]{2,1,0:T(8,128)(2,1)S(1)}, u32[]{:S(2)}, u32[]{:S(2)}) async-start(bf16[8,128,512]{2,1,0:T(8,128)(2,1)} %broadcast_in_dim.16), calls=%async_computation.5 | async-start | bytes 2097152 | tf_op jit(solution)/shard_map/all_to_all | solution.py:34
  148.3 21.2 %collective-permute-start.8 = (bf16[3,128,1024]{1,2,0:T(8,128)(2,1)}, bf16[3,128,1024]{1,2,0:T(8,128)(2,1)}, u32[]{:S(2)}, u32[]{:S(2)}) collective-permute-start(bf16[3,128,1024]{1,2,0:T(8,128)(2,1)} %pad_maximum_fusion.3), channel_id=1, source_target_pairs={{0,8},{8,0},{1,9},{9,1},{2,10},{10,2},{3,11},{11,3},{4,12},{12,4},... | collective-permute-start | bytes 2359304 | tf_op jit(solution)/shard_map/ppermute | solution.py:22
  163.8 19.8 %all-to-all-start.8 = ((bf16[8,128,512]{1,2,0:T(8,128)(2,1)}), bf16[8,128,512]{1,2,0:T(8,128)(2,1)}, u32[]{:S(2)}, u32[]{:S(2)}) async-start(bf16[8,128,512]{1,2,0:T(8,128)(2,1)} %broadcast_in_dim.17), calls=%async_computation.8 | async-start | bytes 2097152 | tf_op jit(solution)/shard_map/all_to_all | solution.py:34
  169.4 17.1 %collective-permute-start.3 = (bf16[128,4096]{1,0:T(8,128)(2,1)S(1)}, bf16[128,4096]{1,0:T(8,128)(2,1)}, u32[]{:S(2)}, u32[]{:S(2)}) collective-permute-start(bf16[128,4096]{1,0:T(8,128)(2,1)S(1)} %bitcast.79), channel_id=1, source_target_pairs={{0,8},{8,0},{1,9},{9,1},{2,10},{10,2},{3,11},{11,3},{4,12},{12,4},... | collective-permute-start | bytes 3145736 | tf_op jit(solution)/shard_map/ppermute | solution.py:22
  176.0 49.7 %collective-permute-start.21 = (bf16[256,512]{0,1:T(8,128)(2,1)S(1)}, bf16[256,512]{0,1:T(8,128)(2,1)}, u32[]{:S(2)}, u32[]{:S(2)}) collective-permute-start(bf16[256,512]{0,1:T(8,128)(2,1)S(1)} %fusion.26), channel_id=1, source_target_pairs={{0,8},{8,0},{1,9},{9,1},{2,10},{10,2},{3,11},{11,3},{4,12},{12,4},... | collective-permute-start | bytes 786440 | tf_op jit(solution)/shard_map/ppermute | solution.py:22
  202.2 27.4 %collective-permute-start.18 = (bf16[128,1024]{0,1:T(8,128)(2,1)}, bf16[128,1024]{0,1:T(8,128)(2,1)}, u32[]{:S(2)}, u32[]{:S(2)}) collective-permute-start(bf16[128,1024]{0,1:T(8,128)(2,1)} %bitcast.26), channel_id=1, source_target_pairs={{0,2},{1,3},{2,0},{3,1},{4,6},{5,7},{6,4},{7,5},{8,10},{9,11},{10,... | collective-permute-start | bytes 786440 | tf_op jit(solution)/shard_map/ppermute | solution.py:30
  203.5 27.2 %collective-permute-start.16 = (bf16[128,1024]{0,1:T(8,128)(2,1)}, bf16[128,1024]{0,1:T(8,128)(2,1)}, u32[]{:S(2)}, u32[]{:S(2)}) collective-permute-start(bf16[128,1024]{0,1:T(8,128)(2,1)} %bitcast.22), channel_id=1, source_target_pairs={{0,1},{1,2},{2,3},{3,0},{4,5},{5,6},{6,7},{7,4},{8,9},{9,10},{10,1... | collective-permute-start | bytes 786440 | tf_op jit(solution)/shard_map/ppermute | solution.py:30
  204.2 27.4 %collective-permute-start.17 = (bf16[128,1024]{0,1:T(8,128)(2,1)}, bf16[128,1024]{0,1:T(8,128)(2,1)}, u32[]{:S(2)}, u32[]{:S(2)}) collective-permute-start(bf16[128,1024]{0,1:T(8,128)(2,1)} %bitcast.24), channel_id=1, source_target_pairs={{0,3},{1,0},{2,1},{3,2},{4,7},{5,4},{6,5},{7,6},{8,11},{9,8},{10,9... | collective-permute-start | bytes 786440 | tf_op jit(solution)/shard_map/ppermute | solution.py:30
  225.6 33.6 %collective-permute-start.4 = (bf16[256,8,256]{2,1,0:T(8,128)(2,1)S(1)}, bf16[256,8,256]{2,1,0:T(8,128)(2,1)}, u32[]{:S(2)}, u32[]{:S(2)}) collective-permute-start(bf16[256,8,256]{2,1,0:T(8,128)(2,1)S(1)} %bitcast.89), channel_id=1, source_target_pairs={{0,8},{8,0},{1,9},{9,1},{2,10},{10,2},{3,11},{11,3},{4,12},{12,4},... | collective-permute-start | bytes 3145736 | tf_op jit(solution)/shard_map/ppermute | solution.py:22
  228.5 16.6 %collective-permute-start.11 = (bf16[256,1024]{1,0:T(8,128)(2,1)}, bf16[256,1024]{1,0:T(8,128)(2,1)S(1)}, u32[]{:S(2)}, u32[]{:S(2)}) collective-permute-start(bf16[256,1024]{1,0:T(8,128)(2,1)} %copy-done.18), channel_id=1, source_target_pairs={{0,2},{1,3},{2,0},{3,1},{4,6},{5,7},{6,4},{7,5},{8,10},{9,11},{10,... | collective-permute-start | bytes 1572872 | tf_op jit(solution)/shard_map/ppermute | solution.py:30
  229.5 24.7 %collective-permute-start.10 = (bf16[256,1024]{1,0:T(8,128)(2,1)}, bf16[256,1024]{1,0:T(8,128)(2,1)S(1)}, u32[]{:S(2)}, u32[]{:S(2)}) collective-permute-start(bf16[256,1024]{1,0:T(8,128)(2,1)} %copy-done.18), channel_id=1, source_target_pairs={{0,3},{1,0},{2,1},{3,2},{4,7},{5,4},{6,5},{7,6},{8,11},{9,8},{10,9... | collective-permute-start | bytes 1572872 | tf_op jit(solution)/shard_map/ppermute | solution.py:30
  230.7 26.2 %collective-permute-start.9 = (bf16[256,1024]{1,0:T(8,128)(2,1)}, bf16[256,1024]{1,0:T(8,128)(2,1)S(1)}, u32[]{:S(2)}, u32[]{:S(2)}) collective-permute-start(bf16[256,1024]{1,0:T(8,128)(2,1)} %copy-done.18), channel_id=1, source_target_pairs={{0,1},{1,2},{2,3},{3,0},{4,5},{5,6},{6,7},{7,4},{8,9},{9,10},{10,1... | collective-permute-start | bytes 1572872 | tf_op jit(solution)/shard_map/ppermute | solution.py:30
  233.6 35.9 %collective-permute-start.19 = (bf16[3,128,1024]{1,2,0:T(8,128)(2,1)}, bf16[3,128,1024]{1,2,0:T(8,128)(2,1)}, u32[]{:S(2)}, u32[]{:S(2)}) collective-permute-start(bf16[3,128,1024]{1,2,0:T(8,128)(2,1)} %pad_maximum_fusion.4), channel_id=1, source_target_pairs={{0,8},{8,0},{1,9},{9,1},{2,10},{10,2},{3,11},{11,3},{4,12},{12,4},... | collective-permute-start | bytes 2359304 | tf_op jit(solution)/shard_map/ppermute | solution.py:22
  245.1 31.6 %collective-permute-start.15 = (bf16[256,1024]{1,0:T(8,128)(2,1)}, bf16[256,1024]{1,0:T(8,128)(2,1)}, u32[]{:S(2)}, u32[]{:S(2)}) collective-permute-start(bf16[256,1024]{1,0:T(8,128)(2,1)} %fusion.7), channel_id=1, source_target_pairs={{0,2},{1,3},{2,0},{3,1},{4,6},{5,7},{6,4},{7,5},{8,10},{9,11},{10,... | collective-permute-start | bytes 1572872 | tf_op jit(solution)/shard_map/ppermute | solution.py:30
  254.2 22.5 %collective-permute-start.14 = (bf16[256,1024]{1,0:T(8,128)(2,1)}, bf16[256,1024]{1,0:T(8,128)(2,1)}, u32[]{:S(2)}, u32[]{:S(2)}) collective-permute-start(bf16[256,1024]{1,0:T(8,128)(2,1)} %fusion.7), channel_id=1, source_target_pairs={{0,3},{1,0},{2,1},{3,2},{4,7},{5,4},{6,5},{7,6},{8,11},{9,8},{10,9... | collective-permute-start | bytes 1572872 | tf_op jit(solution)/shard_map/ppermute | solution.py:30
  256.8 20.7 %collective-permute-start.13 = (bf16[256,1024]{1,0:T(8,128)(2,1)}, bf16[256,1024]{1,0:T(8,128)(2,1)}, u32[]{:S(2)}, u32[]{:S(2)}) collective-permute-start(bf16[256,1024]{1,0:T(8,128)(2,1)} %fusion.7), channel_id=1, source_target_pairs={{0,1},{1,2},{2,3},{3,0},{4,5},{5,6},{6,7},{7,4},{8,9},{9,10},{10,1... | collective-permute-start | bytes 1572872 | tf_op jit(solution)/shard_map/ppermute | solution.py:30
  259.1 35.7 %collective-permute-start.12 = (bf16[512,1024]{1,0:T(8,128)(2,1)}, bf16[512,1024]{1,0:T(8,128)(2,1)}, u32[]{:S(2)}, u32[]{:S(2)}) collective-permute-start(bf16[512,1024]{1,0:T(8,128)(2,1)} %convolution_convert_fusion.1), channel_id=1, source_target_pairs={{0,4},{4,0},{1,5},{5,1},{2,6},{6,2},{3,7},{7,3},{8,12},{12,8},{9,1... | collective-permute-start | bytes 3145736 | tf_op jit(solution)/shard_map/ppermute | solution.py:26
  264.7 35.7 %all-to-all-start.6 = ((bf16[8,256,256]{2,1,0:T(8,128)(2,1)}), bf16[8,256,256]{2,1,0:T(8,128)(2,1)S(1)}, u32[]{:S(2)}, u32[]{:S(2)}) async-start(bf16[8,256,256]{2,1,0:T(8,128)(2,1)} %copy.63), calls=%async_computation.6 | async-start | bytes 2097152 | tf_op jit(solution)/shard_map/all_to_all | solution.py:34
  269.5 14.2 %collective-permute-start.22 = (bf16[512,256]{1,0:T(8,128)(2,1)S(1)}, bf16[512,256]{1,0:T(8,128)(2,1)}, u32[]{:S(2)}, u32[]{:S(2)}) collective-permute-start(bf16[512,256]{1,0:T(8,128)(2,1)S(1)} %copy-done.15), channel_id=1, source_target_pairs={{0,8},{8,0},{1,9},{9,1},{2,10},{10,2},{3,11},{11,3},{4,12},{12,4},... | collective-permute-start | bytes 786440 | tf_op jit(solution)/shard_map/ppermute | solution.py:22
  281.8 37.3 %collective-permute-start.20 = (bf16[1024,512]{1,0:T(8,128)(2,1)}, bf16[1024,512]{1,0:T(8,128)(2,1)}, u32[]{:S(2)}, u32[]{:S(2)}) collective-permute-start(bf16[1024,512]{1,0:T(8,128)(2,1)} %convolution_convert_fusion), channel_id=1, source_target_pairs={{0,4},{4,0},{1,5},{5,1},{2,6},{6,2},{3,7},{7,3},{8,12},{12,8},{9,1... | collective-permute-start | bytes 3145736 | tf_op jit(solution)/shard_map/ppermute | solution.py:26
  (25 other events, 255.8 us)

commit v2 on v1

v2 whole, which is shorter than its diff:
```python
import jax
import jax.numpy as jnp
from jax import lax
from jax.experimental import pallas as pl
from jax.experimental.pallas import tpu as pltpu
from jax.sharding import Mesh, PartitionSpec as P

BF16 = jnp.bfloat16
F32 = jnp.float32
CHIPS = ("x", "yh")
TOK = ("yl", "z")


def silu_slope(values):
    sig = jax.nn.sigmoid(values)
    return sig * (1.0 + values * (1.0 - sig))


def dot(left, right, dims):
    return lax.dot_general(left, right, (dims, ((), ())), preferred_element_type=F32)


def flip(value, axis, by=1):
    size = lax.axis_size(axis)
    return lax.ppermute(value, axis, [(i, i ^ by) for i in range(size)])


def exchange(value, axes):
    return lax.all_to_all(value, axes, 0, 0, tiled=True)


def gather_all(value, axes, count):
    return exchange(jnp.broadcast_to(value[None], (count,) + value.shape), axes)


def pick(value, index, axis):
    return lax.dynamic_index_in_dim(value, index, axis, keepdims=False)


def cut(value, start, size, axis):
    return lax.dynamic_slice_in_dim(value, start, size, axis)


def after(value, *others):
    return lax.optimization_barrier((value,) + others)[0]


def z_columns(rows, yl, z, core, side):
    group = jnp.where(core == 0, yl, 1 - yl)
    got = [flip(cut(rows, (group * 4 + (z ^ by)) * side, side, 1), "z", by) for by in (1, 2, 3)]
    got = jnp.concatenate(got)
    come = flip(got, "c")
    own = jnp.concatenate([cut(rows, (yl * 4 + z) * side, side, 1), jnp.where(core == 0, got, come)])
    pair = jnp.concatenate([cut(rows, ((1 - yl) * 4 + z) * side, side, 1), jnp.where(core == 0, come, got)])
    return own, pair


def z_rows(block):
    return jnp.concatenate([block] + [flip(block, "z", by) for by in (1, 2, 3)])


def chip_blocks(blocks, x, yh):
    four = blocks.reshape((4, 2) + blocks.shape[1:])
    pair = jnp.stack([pick(four, yh, 1), flip(pick(four, 1 - yh, 1), "yh")])
    out = [pick(pair, x, 1)] + [flip(pick(pair, x ^ by, 1), "x", by) for by in (1, 2, 3)]
    return jnp.concatenate(out)


def term_kernel(parity_ref, grad_ref, up_ref, *rest):
    out_ref = rest[-1]
    part = lax.dot_general(
        grad_ref[...], up_ref[...], (((1,), (1,)), ((), ())), preferred_element_type=F32
    )
    for add in rest[:-1]:
        part = part + add[0].astype(F32)
    out_ref[0] = part.astype(BF16)


def term_blocks(grad, up, parity, half, add=()):
    rows, depth = grad.shape
    count = up.shape[0] // (2 * half)
    block = pl.BlockSpec((1, rows, half), lambda i, par: (i, 0, 0))
    return pl.pallas_call(
        term_kernel,
        grid_spec=pltpu.PrefetchScalarGridSpec(
            num_scalar_prefetch=1,
            grid=(count,),
            in_specs=[
                pl.BlockSpec((rows, depth), lambda i, par: (0, 0)),
                pl.BlockSpec((half, depth), lambda i, par: (2 * i + par[0], 0)),
            ]
            + [block] * len(add),
            out_specs=block,
        ),
        out_shape=jax.ShapeDtypeStruct((count, rows, half), BF16),
        cost_estimate=pl.CostEstimate(
            flops=2 * count * rows * half * depth,
            bytes_accessed=2 * count * half * depth,
            transcendentals=0,
        ),
        compiler_params=pltpu.CompilerParams(vmem_limit_bytes=16 * 1024 * 1024),
        name="term",
    )(parity.reshape(1).astype(jnp.int32), grad, up, *add)


def body(
    wide_up,
    wide_down,
    narrow_up,
    narrow_down,
    wide_input,
    wide_preact,
    narrow_input,
    narrow_preact,
    cotangent,
):
    core = lax.axis_index("c")
    z = lax.axis_index("z")
    yl = lax.axis_index("yl")
    x = lax.axis_index("x")
    yh = lax.axis_index("yh")
    chip = x * 2 + yh
    tok = yl * 4 + z
    tokens, side = cotangent.shape
    n_t, n_d = 8, 8
    half = narrow_down.shape[1]

    wide_pre = wide_preact.astype(F32)
    wide_act = jax.nn.silu(wide_pre).astype(BF16)
    act_all = lax.all_gather(wide_act, TOK, axis=0, tiled=True)

    down_copies = jnp.broadcast_to(narrow_down[None], (n_d,) + narrow_down.shape)
    down_cols = exchange(down_copies, CHIPS)
    cot = after(cotangent, down_copies)
    near = jnp.stack([cot, flip(cot, "yl")])
    near = jnp.stack([near] + [flip(near, "z", by) for by in (1, 2, 3)])
    near = near.reshape(n_t, tokens, side)
    cot_rows = jnp.stack([pick(near, (z ^ (i % 4)) * 2 + (yl ^ (i // 4)), 0) for i in range(n_t)])
    cot_here = lax.ppermute(
        cot,
        ("x", "yh", "yl", "z"),
        [(a * 8 + b, b * 8 + a) for a in range(8) for b in range(8)],
    )
    keep = cut(cot_rows, core * half, half, 2)
    come = flip(cut(cot_rows, (1 - core) * half, half, 2), "c")
    pre_f = narrow_preact.astype(F32)
    hid_keep = jnp.einsum("dtk,dfk->tf", keep, down_cols, preferred_element_type=F32)
    hid_send = jnp.einsum("dtk,dfk->tf", come, down_cols, preferred_element_type=F32)
    hidden_grad = hid_keep + flip(hid_send, "c")
    narrow_pre_grad = (hidden_grad * silu_slope(pre_f)).astype(BF16)

    narrow_act = jax.nn.silu(pre_f).astype(BF16)
    down_term = jnp.einsum("tf,dtk->fdk", narrow_act, cot_rows, preferred_element_type=F32)
    narrow_down_grad = lax.psum_scatter(
        down_term.astype(BF16).reshape(side, n_d * side), ("x", "yh", "c"), scatter_dimension=1, tiled=True
    )

    pre_all = gather_all(narrow_pre_grad, CHIPS, n_d).reshape(n_d * tokens, -1)
    up_other = flip(narrow_up, "c")
    up_rows = jnp.concatenate(
        [jnp.where(core == 0, narrow_up, up_other), jnp.where(core == 0, up_other, narrow_up)]
    )
    share = dot(pre_all, up_rows, ((1,), (1,))).astype(BF16)
    share = exchange(share.reshape(n_t, tokens, -1), TOK)
    own = (cot_here.astype(F32) + jnp.sum(share.astype(F32), axis=0)).astype(BF16)
    blocks = gather_all(own, CHIPS, n_d)
    rows = blocks.transpose(1, 0, 2).reshape(tokens, -1)
    rows_other = flip(rows, "c")
    boundary = jnp.concatenate(
        [jnp.where(core == 0, rows, rows_other), jnp.where(core == 0, rows_other, rows)]
    )

    wide_hidden_grad = dot(boundary, wide_down, ((1,), (1,)))
    wide_pre_grad = (wide_hidden_grad * silu_slope(wide_pre)).astype(BF16)
    input_own, input_pair = z_columns(after(wide_input, near), yl, z, core, side)
    grad_rows = z_rows(wide_pre_grad)
    up_come = flip(dot(input_pair, grad_rows, ((0,), (0,))).astype(BF16), "yl")
    wide_up_grad = (dot(input_own, grad_rows, ((0,), (0,))) + up_come.astype(F32)).astype(BF16)

    term_come = flip(term_blocks(wide_pre_grad, wide_up, 1 - core, half), "c")
    term_all = exchange(term_blocks(wide_pre_grad, wide_up, core, half, (term_come,)), CHIPS)
    own_cols = cut(boundary, (chip * 2 + core) * half, half, 1)
    wide_input_grad = (own_cols.astype(F32) + jnp.sum(term_all.astype(F32), axis=0)).astype(BF16)

    bound = exchange(after(blocks, wide_pre_grad), TOK).reshape(n_t * tokens, side)
    bound_other = flip(bound, "c")
    act_all = act_all.reshape(n_t, 2, tokens, -1)

    def act_of(parity):
        return pick(act_all, parity, 1).reshape(n_t * tokens, -1)

    wide_down_grad = (
        dot(act_of(core), bound, ((0,), (0,))) + dot(act_of(1 - core), bound_other, ((0,), (0,)))
    ).astype(BF16)

    in_blocks = after(narrow_input, pre_all).reshape(tokens, n_d, -1).transpose(1, 0, 2)
    in_near = chip_blocks(in_blocks, x, yh).reshape((4, 2, tokens, -1))
    in_own = jnp.stack(
        [pick(pick(in_near, x ^ (i // 2), 0), yh ^ (i % 2), 0) for i in range(n_d)]
    ).reshape(n_d * tokens, -1)
    up_part = dot(in_own, pre_all, ((0,), (0,)))
    up_send = cut(up_part, (1 - core) * half, half, 0).astype(BF16)
    narrow_up_grad = (cut(up_part, core * half, half, 0) + flip(up_send, "c").astype(F32)).astype(BF16)
    return (wide_input_grad, wide_up_grad, wide_down_grad, narrow_up_grad, narrow_down_grad)


def solution(mesh):
    fine = Mesh(mesh.devices.reshape(4, 2, 2, 2, 4), ("x", "yh", "c", "yl", "z"))
    dp = ("x", "yh", "c")
    tensor = ("yl", "z")
    in_specs = (
        P(None, dp),
        P(dp, None),
        P(dp, tensor),
        P(tensor, dp),
        P(tensor, None),
        P(tensor, dp),
        P(dp, None),
        P(dp, tensor),
        P(dp, tensor),
    )
    out_specs = (
        P(tensor, dp),
        P(tensor, dp),
        P(dp, tensor),
        P(dp, tensor),
        P(tensor, dp),
    )
    return jax.shard_map(body, mesh=fine, in_specs=in_specs, out_specs=out_specs, check_vma=False)
```

time: 325 us -> 269 us (0.83)
  blocking collectives: 42.1 us -> 0 us
  between operations: 1.23 us -> 16 us
  local copies, waits for them, and re-layouts: 55.9 us -> 43 us
  waiting for transfers between devices: 112 us -> 101 us
  other arithmetic: 20.9 us -> 11.8 us
  Pallas kernels: 0 us -> 7.09 us
  matrix products: 37.4 us -> 30.6 us
  starting transfers between devices: 53.6 us -> 57.4 us
    all_to_all x2 -> x0, blocking collectives: 42.1 us -> none  [exchange(): return lax.all_to_all(value, axes, 0, 0, tiled=True)]
    all_to_all x7 -> x6, waiting for transfers between devices: 66.8 us -> 31.3 us  [exchange(): return lax.all_to_all(value, axes, 0, 0, tiled=True)]
    ppermute x23 -> x24, waiting for transfers between devices: 45.3 us -> 69.5 us  [the longest x23 69.5 us: flip(): return lax.ppermute(value, axis, [(i, i ^ by) for i in range(size)])]
    dynamic_slice x7 -> x2, local copies, waits for them, and re-layouts: 17.9 us -> 2.89 us  [pick(): return lax.dynamic_index_in_dim(value, index, axis, keepdims=False)]
    unnamed x59 -> x74, local copies, waits for them, and re-layouts: 7.42 us -> 18.8 us
    dot_general x9 -> x7, matrix products: 34.8 us -> 23.5 us  [dot(): lax.dot_general(left, right, (dims, ((), ())), preferred_element_type=F32)]
    concatenate x3 -> x1, local copies, waits for them, and re-layouts: 10.8 us -> 1.66 us  [z_columns(): got = jnp.concatenate(got)]
    ppermute x23 -> x24, starting transfers between devices: 22.4 us -> 30.9 us  [the longest x23 29.6 us: flip(): return lax.ppermute(value, axis, [(i, i ^ by) for i in range(size)])]
  transfers between devices with their start and end apart: 30 -> 32, of which waited for: 15 -> 17; matrix products, arithmetic and copies ran while one was open for 32% -> 28% of each run, Pallas kernels for 0% -> 3%
where the time goes in v2:
time: 269 us; the launch traced here: 267 us
  waiting for transfers between devices  101 us (38%)
  starting transfers between devices  57.4 us (21%)
  local copies, waits for them, and re-layouts  43 us (16%)
  matrix products  30.6 us (11%)
  between operations  16 us (6%)
  other arithmetic  11.8 us (4%)
  Pallas kernels  7.09 us (3%)
    ppermute x23, waiting for transfers between devices, flip(): return lax.ppermute(value, axis, [(i, i ^ by) for i in range(size)])  69.5 us
    all_to_all x6, waiting for transfers between devices, exchange(): return lax.all_to_all(value, axes, 0, 0, tiled=True)  31.3 us
    ppermute x23, starting transfers between devices, flip(): return lax.ppermute(value, axis, [(i, i ^ by) for i in range(size)])  29.6 us
    all_to_all x6, starting transfers between devices, exchange(): return lax.all_to_all(value, axes, 0, 0, tiled=True)  26.4 us
    dot_general x7, matrix products, dot(): lax.dot_general(left, right, (dims, ((), ())), preferred_element_type=F32)  23.5 us
    unnamed x74, local copies, waits for them, and re-layouts  18.8 us
    pallas_call x2, Pallas kernels, term_blocks(): pl.pallas_call(term_kernel, grid_spec=pltpu.PrefetchScalarGridSpec(num_sc...  7.09 us
    reshape x1, local copies, waits for them, and re-layouts, body(): down_term.astype(BF16).reshape(side, n_d * side)  6.47 us
  transfers between devices with their start and end apart: 32, of which 17 were waited for; matrix products, arithmetic and copies ran while one was open for 28% of the time, Pallas kernels for 3%

profile of v2, /device:TPU:0, one launch (start us, length us, event | category | flops | bytes accessed | tf_op | source)
XLA Modules:
  0.0 266.8 jit_solution(11878202107751881207)
XLA Ops:
  14.4 3.5 %collective-permute-done.1 = bf16[128,512]{1,0:T(8,128)(2,1)S(1)} collective-permute-done((bf16[128,512]{1,0:T(8,128)(2,1)S(1)}, bf16[128,512]{1,0:T(8,128)(2,1)S(1)}, u32[]{:S(2)}, u32[]{:S(2)}) %collective-permute-start.1) | collective-permute-done | bytes 131104 | tf_op jit(solution)/shard_map/ppermute | solution.py:25
  17.9 4.1 %collective-permute-start.3 = (bf16[2,128,512]{2,1,0:T(8,128)(2,1)S(1)}, bf16[2,128,512]{2,1,0:T(8,128)(2,1)S(1)}, u32[]{:S(2)}, u32[]{:S(2)}) collective-permute-start(bf16[2,128,512]{2,1,0:T(8,128)(2,1)S(1)} %get-tuple-element.51), channel_id=1, source_target_pairs={{0,2},{1,3},{2,0},{3,1},{4,6},{5,7},{6,4},{7,5},{8,10},{9,11},{10,... | collective-permute-start | bytes 786440 | tf_op jit(solution)/shard_map/ppermute | solution.py:25
  23.0 6.9 %all-to-all-start = ((bf16[8,512,256]{2,1,0:T(8,128)(2,1)}), bf16[8,512,256]{2,1,0:T(8,128)(2,1)S(1)}, u32[]{:S(2)}, u32[]{:S(2)}) async-start(bf16[8,512,256]{2,1,0:T(8,128)(2,1)} %broadcast_in_dim.6), calls=%async_computation | async-start | bytes 4194304 | tf_op jit(solution)/shard_map/all_to_all | solution.py:29
  30.0 4.2 %collective-permute-done.3 = bf16[2,128,512]{2,1,0:T(8,128)(2,1)S(1)} collective-permute-done((bf16[2,128,512]{2,1,0:T(8,128)(2,1)S(1)}, bf16[2,128,512]{2,1,0:T(8,128)(2,1)S(1)}, u32[]{:S(2)}, u32[]{:S(2)}) %collective-permute-start.3) | collective-permute-done | bytes 262176 | tf_op jit(solution)/shard_map/ppermute | solution.py:25
  34.1 11.3 %collective-permute-done.2 = bf16[2,128,512]{2,1,0:T(8,128)(2,1)S(1)} collective-permute-done((bf16[2,128,512]{2,1,0:T(8,128)(2,1)S(1)}, bf16[2,128,512]{2,1,0:T(8,128)(2,1)S(1)}, u32[]{:S(2)}, u32[]{:S(2)}) %collective-permute-start.2) | collective-permute-done | bytes 262176 | tf_op jit(solution)/shard_map/ppermute | solution.py:25
  47.9 14.4 %all-to-all-done = bf16[8,512,256]{2,1,0:T(8,128)(2,1)S(1)} async-done(((bf16[8,512,256]{2,1,0:T(8,128)(2,1)}), bf16[8,512,256]{2,1,0:T(8,128)(2,1)S(1)}, u32[]{:S(2)}, u32[]{:S(2)}) %all-to-all-start) | async-done | bytes 2097184 | tf_op jit(solution)/shard_map/all_to_all | solution.py:29
  68.8 3.7 %all-to-all-start.1 = ((bf16[8,128,512]{2,1,0:T(8,128)(2,1)}), bf16[8,128,512]{2,1,0:T(8,128)(2,1)S(1)}, u32[]{:S(2)}, u32[]{:S(2)}) async-start(bf16[8,128,512]{2,1,0:T(8,128)(2,1)} %broadcast_in_dim.7), calls=%async_computation.1 | async-start | bytes 2097152 | tf_op jit(solution)/shard_map/all_to_all | solution.py:29
  77.1 7.3 %collective-permute-start.12 = (bf16[256,512]{1,0:T(8,128)(2,1)S(1)}, bf16[256,512]{1,0:T(8,128)(2,1)}, u32[]{:S(2)}, u32[]{:S(2)}) collective-permute-start(bf16[256,512]{1,0:T(8,128)(2,1)S(1)} %get-tuple-element.27), channel_id=1, source_target_pairs={{0,3},{1,2},{2,1},{3,0},{4,7},{5,6},{6,5},{7,4},{8,11},{9,10},{10,... | collective-permute-start | bytes 786440 | tf_op jit(solution)/shard_map/ppermute | solution.py:25
  85.2 9.7 %all-to-all-done.1 = bf16[8,128,512]{2,1,0:T(8,128)(2,1)S(1)} async-done(((bf16[8,128,512]{2,1,0:T(8,128)(2,1)}), bf16[8,128,512]{2,1,0:T(8,128)(2,1)S(1)}, u32[]{:S(2)}, u32[]{:S(2)}) %all-to-all-start.1) | async-done | bytes 1048608 | tf_op jit(solution)/shard_map/all_to_all | solution.py:29
  95.0 3.1 %convolution_convert_fusion.2 = bf16[1024,512]{1,0:T(8,128)(2,1)} fusion(bf16[1024,512]{1,0:T(8,128)(2,1)S(1)} %bitcast.92, bf16[256,512]{1,0:T(8,128)(2,1)} %get-tuple-element.49, bf16[256,512]{1,0:T(8,128)(2,1)} %get-tuple-element.48), kind=kOutput, calls=%fused_computation.14 | convolution fusion | flops 538443776 | bytes 2621440 | tf_op jit(solution)/shard_map/dot_general | solution.py:20
  98.1 3.7 %all-to-all-start.2 = ((bf16[8,128,512]{2,1,0:T(8,128)(2,1)}), bf16[8,128,512]{2,1,0:T(8,128)(2,1)S(1)}, u32[]{:S(2)}, u32[]{:S(2)}) async-start(bf16[8,128,512]{2,1,0:T(8,128)(2,1)} %bitcast.10), calls=%async_computation.2 | async-start | bytes 2097152 | tf_op jit(solution)/shard_map/all_to_all | solution.py:29
  101.8 6.9 %collective-permute-done.10 = bf16[256,512]{1,0:T(8,128)(2,1)S(1)} collective-permute-done((bf16[256,512]{1,0:T(8,128)(2,1)}, bf16[256,512]{1,0:T(8,128)(2,1)S(1)}, u32[]{:S(2)}, u32[]{:S(2)}) %collective-permute-start.10) | collective-permute-done | bytes 262176 | tf_op jit(solution)/shard_map/ppermute | solution.py:25
  113.3 5.8 %collective-permute-done.12 = bf16[256,512]{1,0:T(8,128)(2,1)} collective-permute-done((bf16[256,512]{1,0:T(8,128)(2,1)S(1)}, bf16[256,512]{1,0:T(8,128)(2,1)}, u32[]{:S(2)}, u32[]{:S(2)}) %collective-permute-start.12) | collective-permute-done | bytes 262176 | tf_op jit(solution)/shard_map/ppermute | solution.py:25
  120.7 3.4 %convolution_convert_fusion = bf16[512,8,512]{0,2,1:T(8,128)(2,1)} fusion(bf16[8,128,512]{2,1,0:T(8,128)(2,1)S(1)} %copy-done.7, bf16[128,512]{1,0:T(8,128)(2,1)S(1)} %copy-done.24), kind=kOutput, calls=%fused_computation | convolution fusion | flops 539361280 | bytes 5373952 | tf_op jit(solution)/shard_map/tf,dtk->fdk/dot_general | solution.py:153
  124.1 6.5 %copy.64 = bf16[512,4096]{1,0:T(8,128)(2,1)} copy(bf16[512,4096]{0,1:T(8,128)(2,1)} %bitcast.77) | data formatting | bytes 8388608 | tf_op jit(solution)/shard_map/reshape | solution.py:155
  134.7 3.4 %collective-permute-start.22 = (bf16[2,128,512]{2,1,0:T(8,128)(2,1)S(1)}, bf16[2,128,512]{2,1,0:T(8,128)(2,1)S(1)}, u32[]{:S(2)}, u32[]{:S(2)}) collective-permute-start(bf16[2,128,512]{2,1,0:T(8,128)(2,1)S(1)} %get-tuple-element.45), channel_id=1, source_target_pairs={{0,96},{32,64},{64,32},{96,0},{1,97},{33,65},{65,33},{97,1},{2,98}... | collective-permute-start | bytes 786440 | tf_op jit(solution)/shard_map/ppermute | solution.py:25
  140.4 4.2 %all-to-all-start.3 = ((bf16[8,128,512]{1,2,0:T(8,128)(2,1)}), bf16[8,128,512]{1,2,0:T(8,128)(2,1)}, u32[]{:S(2)}, u32[]{:S(2)}) async-start(bf16[8,128,512]{1,2,0:T(8,128)(2,1)} %broadcast_in_dim.8), calls=%async_computation.3 | async-start | bytes 2097152 | tf_op jit(solution)/shard_map/all_to_all | solution.py:29
  147.3 3.6 %collective-permute-done.22 = bf16[2,128,512]{2,1,0:T(8,128)(2,1)S(1)} collective-permute-done((bf16[2,128,512]{2,1,0:T(8,128)(2,1)S(1)}, bf16[2,128,512]{2,1,0:T(8,128)(2,1)S(1)}, u32[]{:S(2)}, u32[]{:S(2)}) %collective-permute-start.22) | collective-permute-done | bytes 262176 | tf_op jit(solution)/shard_map/ppermute | solution.py:25
  155.2 7.2 %all-to-all-done.3 = bf16[8,128,512]{1,2,0:T(8,128)(2,1)} async-done(((bf16[8,128,512]{1,2,0:T(8,128)(2,1)}), bf16[8,128,512]{1,2,0:T(8,128)(2,1)}, u32[]{:S(2)}, u32[]{:S(2)}) %all-to-all-start.3) | async-done | bytes 1048608 | tf_op jit(solution)/shard_map/all_to_all | solution.py:29
  170.7 6.0 %fusion.2.grad_ref = bf16[256,1024]{1,0:T(8,128)(2,1)S(1)} fusion(bf16[1024,4096]{1,0:T(8,128)(2,1)} %param.10, bf16[128,4096]{1,0:T(8,128)(2,1)S(1)} %get-tuple-element.31, bf16[128,4096]{1,0:T(8,128)(2,1)S(1)} %get-tuple-element.30, bf16[256,1024]{1,0:T(8,128)(2,1)S(1)} %copy-done.16), kind=kOutput, calls=%fused_computation.25 | convolution fusion | flops 2154299392 | bytes 11534336 | tf_op jit(solution)/shard_map/dot_general | solution.py:20
  176.7 3.9 %collective-permute-start.16 = (bf16[256,1024]{1,0:T(8,128)(2,1)S(1)}, bf16[256,1024]{1,0:T(8,128)(2,1)}, u32[]{:S(2)}, u32[]{:S(2)}) collective-permute-start(bf16[256,1024]{1,0:T(8,128)(2,1)S(1)} %fusion.2.grad_ref), channel_id=1, source_target_pairs={{0,3},{1,2},{2,1},{3,0},{4,7},{5,6},{6,5},{7,4},{8,11},{9,10},{10,... | collective-permute-start | bytes 1572872 | tf_op jit(solution)/shard_map/ppermute | solution.py:25
  180.6 3.5 %collective-permute-start.15 = (bf16[256,1024]{1,0:T(8,128)(2,1)S(1)}, bf16[256,1024]{1,0:T(8,128)(2,1)}, u32[]{:S(2)}, u32[]{:S(2)}) collective-permute-start(bf16[256,1024]{1,0:T(8,128)(2,1)S(1)} %fusion.2.grad_ref), channel_id=1, source_target_pairs={{0,2},{1,3},{2,0},{3,1},{4,6},{5,7},{6,4},{7,5},{8,10},{9,11},{10,... | collective-permute-start | bytes 1572872 | tf_op jit(solution)/shard_map/ppermute | solution.py:25
  184.8 4.3 %all-to-all-start.5 = ((bf16[8,128,512]{1,2,0:T(8,128)(2,1)}), bf16[8,128,512]{1,2,0:T(8,128)(2,1)}, u32[]{:S(2)}, u32[]{:S(2)}) async-start(bf16[8,128,512]{1,2,0:T(8,128)(2,1)} %all-to-all-done.3), calls=%async_computation.5 | async-start | bytes 2097152 | tf_op jit(solution)/shard_map/all_to_all | solution.py:29
  189.1 3.5 %copy-done = bf16[4096,1024]{1,0:T(8,128)(2,1)S(1)} copy-done((bf16[4096,1024]{1,0:T(8,128)(2,1)S(1)}, bf16[4096,1024]{1,0:T(8,128)(2,1)}, u32[]{:S(2)}) %copy-start) | copy-done | bytes 8388632
  198.7 11.7 %collective-permute-done.16 = bf16[256,1024]{1,0:T(8,128)(2,1)} collective-permute-done((bf16[256,1024]{1,0:T(8,128)(2,1)S(1)}, bf16[256,1024]{1,0:T(8,128)(2,1)}, u32[]{:S(2)}, u32[]{:S(2)}) %collective-permute-start.16) | collective-permute-done | bytes 524320 | tf_op jit(solution)/shard_map/ppermute | solution.py:25
  213.3 3.6 %convolution_convert_fusion.1 = bf16[512,1024]{1,0:T(8,128)(2,1)} fusion(bf16[768,512]{1,0:T(8,128)(2,1)S(1)} %get-tuple-element.33, bf16[256,512]{1,0:T(8,128)(2,1)S(1)} %copy-done.19, bf16[256,1024]{1,0:T(8,128)(2,1)} %collective-permute-done.16, bf16[256,1024]{1,0:T(8,128)(2,1)} %collective-permute-done.15, ...), kind=kOutput, calls=%fused_computation.13 | convolution fusion | flops 1084751872 | bytes 4194304 | tf_op jit(solution)/shard_map/dot_general | solution.py:20
  222.4 3.4 %copy-done.1 = bf16[4096,1024]{1,0:T(8,128)(2,1)S(1)} copy-done((bf16[4096,1024]{1,0:T(8,128)(2,1)S(1)}, bf16[4096,1024]{1,0:T(8,128)(2,1)}, u32[]{:S(2)}) %copy-start.1) | copy-done | bytes 8388632
  225.8 4.3 %term.3 = bf16[8,256,256]{2,1,0:T(8,128)(2,1)} custom-call(s32[1]{0:T(128)} %bitcast.14.parity_ref, bf16[256,1024]{1,0:T(8,128)(2,1)S(1)} %fusion.2.grad_ref, bf16[4096,1024]{1,0:T(8,128)(2,1)S(1)} %copy-done.1, bf16[8,256,256]{2,1,0:T(8,128)(2,1)S(1)} %collective-permute-done.9.rest_0_), custom_call_target="tpu_custom_call" | custom-call | flops 1073741824 | bytes 4194304 | tf_op jit(solution)/shard_map/term/pallas_call | solution.py:83
  230.1 3.6 %all-to-all-start.4 = ((bf16[8,256,256]{2,1,0:T(8,128)(2,1)}), bf16[8,256,256]{2,1,0:T(8,128)(2,1)S(1)}, u32[]{:S(2)}, u32[]{:S(2)}) async-start(bf16[8,256,256]{2,1,0:T(8,128)(2,1)} %term.3), calls=%async_computation.4 | async-start | bytes 2097152 | tf_op jit(solution)/shard_map/all_to_all | solution.py:29
  237.8 13.0 %collective-permute-done.17 = bf16[512,1024]{1,0:T(8,128)(2,1)} collective-permute-done((bf16[512,1024]{1,0:T(8,128)(2,1)}, bf16[512,1024]{1,0:T(8,128)(2,1)}, u32[]{:S(2)}, u32[]{:S(2)}) %collective-permute-start.17) | collective-permute-done | bytes 1048608 | tf_op jit(solution)/shard_map/ppermute | solution.py:25
  250.8 4.0 %add_convert_fusion.1 = bf16[512,1024]{1,0:T(8,128)(2,1)} fusion(bf16[512,1024]{1,0:T(8,128)(2,1)} %collective-permute-done.17, bf16[768,512]{1,0:T(8,128)(2,1)S(1)} %copy-done.14, bf16[256,512]{1,0:T(8,128)(2,1)S(1)} %copy-done.18, bf16[256,1024]{1,0:T(8,128)(2,1)} %collective-permute-done.16, bf16[256,1024]{1,0:T(8,128)(2,1)} %collective-permute-done.15, ...), kind=kOutput, calls=%fused_computation.7 | convolution fusion | flops 1085800448 | bytes 5242880 | tf_op jit(solution)/shard_map/dot_general | solution.py:20
  254.8 3.6 %add_convert_fusion = bf16[1024,512]{1,0:T(8,128)(2,1)} fusion(f32[1024,512]{1,0:T(8,128)S(1)} %fusion.48, bf16[1024,1024]{1,0:T(8,128)(2,1)S(1)} %bitcast.90, bf16[1024,512]{1,0:T(8,128)(2,1)} %collective-permute-done.18), kind=kOutput, calls=%fused_computation.6 | convolution fusion | flops 1074790400 | bytes 6291456 | tf_op jit(solution)/shard_map/dot_general | solution.py:20
  (151 shorter events, 69.6 us)
Async XLA Ops:
  8.0 225.7 %all-gather.2.cloned.1.call-start = ((), (), s32[]{:S(2)}) async-start(), calls=%async_computation.7 | async-start | bytes 4718592 | tf_op jit(solution)/shard_map/all_gather | solution.py:130
  12.7 5.2 %collective-permute-start.1 = (bf16[128,512]{1,0:T(8,128)(2,1)S(1)}, bf16[128,512]{1,0:T(8,128)(2,1)S(1)}, u32[]{:S(2)}, u32[]{:S(2)}) collective-permute-start(bf16[128,512]{1,0:T(8,128)(2,1)S(1)} %copy-done.23), channel_id=1, source_target_pairs={{0,4},{4,0},{1,5},{5,1},{2,6},{6,2},{3,7},{7,3},{8,12},{12,8},{9,1... | collective-permute-start | bytes 393224 | tf_op jit(solution)/shard_map/ppermute | solution.py:25
  17.9 16.2 %collective-permute-start.3 = (bf16[2,128,512]{2,1,0:T(8,128)(2,1)S(1)}, bf16[2,128,512]{2,1,0:T(8,128)(2,1)S(1)}, u32[]{:S(2)}, u32[]{:S(2)}) collective-permute-start(bf16[2,128,512]{2,1,0:T(8,128)(2,1)S(1)} %get-tuple-element.51), channel_id=1, source_target_pairs={{0,2},{1,3},{2,0},{3,1},{4,6},{5,7},{6,4},{7,5},{8,10},{9,11},{10,... | collective-permute-start | bytes 786440 | tf_op jit(solution)/shard_map/ppermute | solution.py:25
  22.0 23.4 %collective-permute-start.2 = (bf16[2,128,512]{2,1,0:T(8,128)(2,1)S(1)}, bf16[2,128,512]{2,1,0:T(8,128)(2,1)S(1)}, u32[]{:S(2)}, u32[]{:S(2)}) collective-permute-start(bf16[2,128,512]{2,1,0:T(8,128)(2,1)S(1)} %get-tuple-element.51), channel_id=1, source_target_pairs={{0,1},{1,0},{2,3},{3,2},{4,5},{5,4},{6,7},{7,6},{8,9},{9,8},{10,11... | collective-permute-start | bytes 786440 | tf_op jit(solution)/shard_map/ppermute | solution.py:25
  23.0 22.4 %collective-permute-start.4 = (bf16[2,128,512]{2,1,0:T(8,128)(2,1)S(1)}, bf16[2,128,512]{2,1,0:T(8,128)(2,1)S(1)}, u32[]{:S(2)}, u32[]{:S(2)}) collective-permute-start(bf16[2,128,512]{2,1,0:T(8,128)(2,1)S(1)} %get-tuple-element.51), channel_id=1, source_target_pairs={{0,3},{1,2},{2,1},{3,0},{4,7},{5,6},{6,5},{7,4},{8,11},{9,10},{10,... | collective-permute-start | bytes 786440 | tf_op jit(solution)/shard_map/ppermute | solution.py:25
  23.0 39.3 %all-to-all-start = ((bf16[8,512,256]{2,1,0:T(8,128)(2,1)}), bf16[8,512,256]{2,1,0:T(8,128)(2,1)S(1)}, u32[]{:S(2)}, u32[]{:S(2)}) async-start(bf16[8,512,256]{2,1,0:T(8,128)(2,1)} %broadcast_in_dim.6), calls=%async_computation | async-start | bytes 4194304 | tf_op jit(solution)/shard_map/all_to_all | solution.py:29
  45.8 2.1 collective-permute-start.5
  64.2 1.7 collective-permute-start.6
  68.8 26.1 %all-to-all-start.1 = ((bf16[8,128,512]{2,1,0:T(8,128)(2,1)}), bf16[8,128,512]{2,1,0:T(8,128)(2,1)S(1)}, u32[]{:S(2)}, u32[]{:S(2)}) async-start(bf16[8,128,512]{2,1,0:T(8,128)(2,1)} %broadcast_in_dim.7), calls=%async_computation.1 | async-start | bytes 2097152 | tf_op jit(solution)/shard_map/all_to_all | solution.py:29
  72.5 1.7 collective-permute-start.7
  72.7 65.5 %collective-permute-start = (bf16[128,512]{1,0:T(8,128)(2,1)S(1)}, bf16[128,512]{1,0:T(8,128)(2,1)}, u32[]{:S(2)}, u32[]{:S(2)}) collective-permute-start(bf16[128,512]{1,0:T(8,128)(2,1)S(1)} %copy-done.23), channel_id=1, source_target_pairs={{0,0},{1,16},{2,32},{3,48},{4,64},{5,80},{6,96},{7,112},{16,1},{17... | collective-permute-start | bytes 393224 | tf_op jit(solution)/shard_map/ppermute | solution.py:139
  77.1 42.0 %collective-permute-start.12 = (bf16[256,512]{1,0:T(8,128)(2,1)S(1)}, bf16[256,512]{1,0:T(8,128)(2,1)}, u32[]{:S(2)}, u32[]{:S(2)}) collective-permute-start(bf16[256,512]{1,0:T(8,128)(2,1)S(1)} %get-tuple-element.27), channel_id=1, source_target_pairs={{0,3},{1,2},{2,1},{3,0},{4,7},{5,6},{6,5},{7,4},{8,11},{9,10},{10,... | collective-permute-start | bytes 786440 | tf_op jit(solution)/shard_map/ppermute | solution.py:25
  84.4 27.3 %collective-permute-start.11 = (bf16[256,512]{1,0:T(8,128)(2,1)}, bf16[256,512]{1,0:T(8,128)(2,1)}, u32[]{:S(2)}, u32[]{:S(2)}) collective-permute-start(bf16[256,512]{1,0:T(8,128)(2,1)} %get-tuple-element.28), channel_id=1, source_target_pairs={{0,2},{1,3},{2,0},{3,1},{4,6},{5,7},{6,4},{7,5},{8,10},{9,11},{10,... | collective-permute-start | bytes 786440 | tf_op jit(solution)/shard_map/ppermute | solution.py:25
  84.4 24.4 %collective-permute-start.10 = (bf16[256,512]{1,0:T(8,128)(2,1)}, bf16[256,512]{1,0:T(8,128)(2,1)S(1)}, u32[]{:S(2)}, u32[]{:S(2)}) collective-permute-start(bf16[256,512]{1,0:T(8,128)(2,1)} %get-tuple-element.29), channel_id=1, source_target_pairs={{0,1},{1,0},{2,3},{3,2},{4,5},{5,4},{6,7},{7,6},{8,9},{9,8},{10,11... | collective-permute-start | bytes 786440 | tf_op jit(solution)/shard_map/ppermute | solution.py:25
  98.1 40.0 %all-to-all-start.2 = ((bf16[8,128,512]{2,1,0:T(8,128)(2,1)}), bf16[8,128,512]{2,1,0:T(8,128)(2,1)S(1)}, u32[]{:S(2)}, u32[]{:S(2)}) async-start(bf16[8,128,512]{2,1,0:T(8,128)(2,1)} %bitcast.10), calls=%async_computation.2 | async-start | bytes 2097152 | tf_op jit(solution)/shard_map/all_to_all | solution.py:29
  101.8 157.6 %reduce-scatter.2.cloned.1.call-start = ((), (), s32[]{:S(2)}) async-start(), calls=%async_computation.8 | async-start | bytes 4456448 | tf_op jit(solution)/shard_map/reduce_scatter | solution.py:154
  111.6 21.6 %collective-permute-start.19 = (bf16[4,128,512]{2,1,0:T(8,128)(2,1)S(1)}, bf16[4,128,512]{2,1,0:T(8,128)(2,1)S(1)}, u32[]{:S(2)}, u32[]{:S(2)}) collective-permute-start(bf16[4,128,512]{2,1,0:T(8,128)(2,1)S(1)} %get-tuple-element.46), channel_id=1, source_target_pairs={{0,16},{16,0},{1,17},{17,1},{2,18},{18,2},{3,19},{19,3},{4,20},{20... | collective-permute-start | bytes 1572872 | tf_op jit(solution)/shard_map/ppermute | solution.py:25
  120.7 24.0 %collective-permute-start.13 = (bf16[768,512]{1,0:T(8,128)(2,1)}, bf16[768,512]{1,0:T(8,128)(2,1)}, u32[]{:S(2)}, u32[]{:S(2)}) collective-permute-start(bf16[768,512]{1,0:T(8,128)(2,1)} %constant_dynamic-update-slice_fusion), channel_id=1, source_target_pairs={{0,8},{8,0},{1,9},{9,1},{2,10},{10,2},{3,11},{11,3},{4,12},{12,4},... | collective-permute-start | bytes 2359304 | tf_op jit(solution)/shard_map/ppermute | solution.py:25
  133.3 13.9 %collective-permute-start.20 = (bf16[2,128,512]{2,1,0:T(8,128)(2,1)S(1)}, bf16[2,128,512]{2,1,0:T(8,128)(2,1)S(1)}, u32[]{:S(2)}, u32[]{:S(2)}) collective-permute-start(bf16[2,128,512]{2,1,0:T(8,128)(2,1)S(1)} %get-tuple-element.43), channel_id=1, source_target_pairs={{0,32},{32,0},{64,96},{96,64},{1,33},{33,1},{65,97},{97,65},{2,34}... | collective-permute-start | bytes 786440 | tf_op jit(solution)/shard_map/ppermute | solution.py:25
  133.4 13.9 %collective-permute-start.21 = (bf16[2,128,512]{2,1,0:T(8,128)(2,1)S(1)}, bf16[2,128,512]{2,1,0:T(8,128)(2,1)S(1)}, u32[]{:S(2)}, u32[]{:S(2)}) collective-permute-start(bf16[2,128,512]{2,1,0:T(8,128)(2,1)S(1)} %get-tuple-element.44), channel_id=1, source_target_pairs={{0,64},{32,96},{64,0},{96,32},{1,65},{33,97},{65,1},{97,33},{2,66}... | collective-permute-start | bytes 786440 | tf_op jit(solution)/shard_map/ppermute | solution.py:25
  134.7 16.2 %collective-permute-start.22 = (bf16[2,128,512]{2,1,0:T(8,128)(2,1)S(1)}, bf16[2,128,512]{2,1,0:T(8,128)(2,1)S(1)}, u32[]{:S(2)}, u32[]{:S(2)}) collective-permute-start(bf16[2,128,512]{2,1,0:T(8,128)(2,1)S(1)} %get-tuple-element.45), channel_id=1, source_target_pairs={{0,96},{32,64},{64,32},{96,0},{1,97},{33,65},{65,33},{97,1},{2,98}... | collective-permute-start | bytes 786440 | tf_op jit(solution)/shard_map/ppermute | solution.py:25
  140.4 22.0 %all-to-all-start.3 = ((bf16[8,128,512]{1,2,0:T(8,128)(2,1)}), bf16[8,128,512]{1,2,0:T(8,128)(2,1)}, u32[]{:S(2)}, u32[]{:S(2)}) async-start(bf16[8,128,512]{1,2,0:T(8,128)(2,1)} %broadcast_in_dim.8), calls=%async_computation.3 | async-start | bytes 2097152 | tf_op jit(solution)/shard_map/all_to_all | solution.py:29
  163.9 5.8 %collective-permute-start.8 = (bf16[128,4096]{1,0:T(8,128)(2,1)S(1)}, bf16[128,4096]{1,0:T(8,128)(2,1)S(1)}, u32[]{:S(2)}, u32[]{:S(2)}) collective-permute-start(bf16[128,4096]{1,0:T(8,128)(2,1)S(1)} %copy.50), channel_id=1, source_target_pairs={{0,8},{8,0},{1,9},{9,1},{2,10},{10,2},{3,11},{11,3},{4,12},{12,4},... | collective-permute-start | bytes 3145736 | tf_op jit(solution)/shard_map/ppermute | solution.py:25
  176.7 33.7 %collective-permute-start.16 = (bf16[256,1024]{1,0:T(8,128)(2,1)S(1)}, bf16[256,1024]{1,0:T(8,128)(2,1)}, u32[]{:S(2)}, u32[]{:S(2)}) collective-permute-start(bf16[256,1024]{1,0:T(8,128)(2,1)S(1)} %fusion.2.grad_ref), channel_id=1, source_target_pairs={{0,3},{1,2},{2,1},{3,0},{4,7},{5,6},{6,5},{7,4},{8,11},{9,10},{10,... | collective-permute-start | bytes 1572872 | tf_op jit(solution)/shard_map/ppermute | solution.py:25
  180.6 29.7 %collective-permute-start.15 = (bf16[256,1024]{1,0:T(8,128)(2,1)S(1)}, bf16[256,1024]{1,0:T(8,128)(2,1)}, u32[]{:S(2)}, u32[]{:S(2)}) collective-permute-start(bf16[256,1024]{1,0:T(8,128)(2,1)S(1)} %fusion.2.grad_ref), channel_id=1, source_target_pairs={{0,2},{1,3},{2,0},{3,1},{4,6},{5,7},{6,4},{7,5},{8,10},{9,11},{10,... | collective-permute-start | bytes 1572872 | tf_op jit(solution)/shard_map/ppermute | solution.py:25
  184.2 29.2 %collective-permute-start.14 = (bf16[256,1024]{1,0:T(8,128)(2,1)S(1)}, bf16[256,1024]{1,0:T(8,128)(2,1)}, u32[]{:S(2)}, u32[]{:S(2)}) collective-permute-start(bf16[256,1024]{1,0:T(8,128)(2,1)S(1)} %fusion.2.grad_ref), channel_id=1, source_target_pairs={{0,1},{1,0},{2,3},{3,2},{4,5},{5,4},{6,7},{7,6},{8,9},{9,8},{10,11... | collective-permute-start | bytes 1572872 | tf_op jit(solution)/shard_map/ppermute | solution.py:25
  184.8 35.3 %all-to-all-start.5 = ((bf16[8,128,512]{1,2,0:T(8,128)(2,1)}), bf16[8,128,512]{1,2,0:T(8,128)(2,1)}, u32[]{:S(2)}, u32[]{:S(2)}) async-start(bf16[8,128,512]{1,2,0:T(8,128)(2,1)} %all-to-all-done.3), calls=%async_computation.5 | async-start | bytes 2097152 | tf_op jit(solution)/shard_map/all_to_all | solution.py:29
  195.4 27.0 %collective-permute-start.9 = (bf16[8,256,256]{2,1,0:T(8,128)(2,1)S(1)}, bf16[8,256,256]{2,1,0:T(8,128)(2,1)S(1)}, u32[]{:S(2)}, u32[]{:S(2)}) collective-permute-start(bf16[8,256,256]{2,1,0:T(8,128)(2,1)S(1)} %term.2), channel_id=1, source_target_pairs={{0,8},{8,0},{1,9},{9,1},{2,10},{10,2},{3,11},{11,3},{4,12},{12,4},... | collective-permute-start | bytes 3145736 | tf_op jit(solution)/shard_map/ppermute | solution.py:25
  198.2 20.0 %collective-permute-start.23 = (bf16[256,512]{1,0:T(8,128)(2,1)}, bf16[256,512]{1,0:T(8,128)(2,1)}, u32[]{:S(2)}, u32[]{:S(2)}) collective-permute-start(bf16[256,512]{1,0:T(8,128)(2,1)} %dynamic-slice_convert_fusion), channel_id=1, source_target_pairs={{0,8},{8,0},{1,9},{9,1},{2,10},{10,2},{3,11},{11,3},{4,12},{12,4},... | collective-permute-start | bytes 786440 | tf_op jit(solution)/shard_map/ppermute | solution.py:25
  217.0 33.9 %collective-permute-start.17 = (bf16[512,1024]{1,0:T(8,128)(2,1)}, bf16[512,1024]{1,0:T(8,128)(2,1)}, u32[]{:S(2)}, u32[]{:S(2)}) collective-permute-start(bf16[512,1024]{1,0:T(8,128)(2,1)} %convolution_convert_fusion.1), channel_id=1, source_target_pairs={{0,4},{4,0},{1,5},{5,1},{2,6},{6,2},{3,7},{7,3},{8,12},{12,8},{9,1... | collective-permute-start | bytes 3145736 | tf_op jit(solution)/shard_map/ppermute | solution.py:25
  222.4 32.4 %collective-permute-start.18 = (bf16[1024,512]{1,0:T(8,128)(2,1)}, bf16[1024,512]{1,0:T(8,128)(2,1)}, u32[]{:S(2)}, u32[]{:S(2)}) collective-permute-start(bf16[1024,512]{1,0:T(8,128)(2,1)} %bitcast.93), channel_id=1, source_target_pairs={{0,8},{8,0},{1,9},{9,1},{2,10},{10,2},{3,11},{11,3},{4,12},{12,4},... | collective-permute-start | bytes 3145736 | tf_op jit(solution)/shard_map/ppermute | solution.py:25
  230.1 28.4 %all-to-all-start.4 = ((bf16[8,256,256]{2,1,0:T(8,128)(2,1)}), bf16[8,256,256]{2,1,0:T(8,128)(2,1)S(1)}, u32[]{:S(2)}, u32[]{:S(2)}) async-start(bf16[8,256,256]{2,1,0:T(8,128)(2,1)} %term.3), calls=%async_computation.4 | async-start | bytes 2097152 | tf_op jit(solution)/shard_map/all_to_all | solution.py:29
  (25 other events, 191.3 us)
Sparse Core Ops, SparseCore 0:
  10.5 100.4 all-gather.1
Sparse Core Ops, SparseCore 1:
  130.7 83.1 reduce-scatter.1

commit v3 on v2

v3 whole, which is shorter than its diff:
```python
import jax
import jax.numpy as jnp
from jax import lax
from jax.experimental import pallas as pl
from jax.experimental.pallas import tpu as pltpu
from jax.sharding import Mesh, PartitionSpec as P

BF16 = jnp.bfloat16
F32 = jnp.float32
CHIPS = ("x", "yh")
TOK = ("yl", "z")


def silu_slope(values):
    sig = jax.nn.sigmoid(values)
    return sig * (1.0 + values * (1.0 - sig))


def dot(left, right, dims):
    return lax.dot_general(left, right, (dims, ((), ())), preferred_element_type=F32)


def gate(*values):
    return lax.optimization_barrier(values)


def flip(value, axis, by=1):
    size = lax.axis_size(axis)
    return lax.ppermute(value, axis, [(i, i ^ by) for i in range(size)])


def exchange(value, axes):
    return lax.all_to_all(value, axes, 0, 0, tiled=True)


def gather_all(value, axes, count):
    return exchange(jnp.broadcast_to(value[None], (count,) + value.shape), axes)


def pick(value, index, axis):
    return lax.dynamic_index_in_dim(value, index, axis, keepdims=False)


def cut(value, start, size, axis):
    return lax.dynamic_slice_in_dim(value, start, size, axis)


def gate(*values):
    return lax.optimization_barrier(values)


def flip(value, axis, by=1):
    size = lax.axis_size(axis)
    return lax.ppermute(value, axis, [(i, i ^ by) for i in range(size)])


def exchange(value, axes):
    return lax.all_to_all(value, axes, 0, 0, tiled=True)


def gather_all(value, axes, count):
    return exchange(jnp.broadcast_to(value[None], (count,) + value.shape), axes)


def pick(value, index, axis):
    return lax.dynamic_index_in_dim(value, index, axis, keepdims=False)


def cut(value, start, size, axis):
    return lax.dynamic_slice_in_dim(value, start, size, axis)


def after(value, *others):
    return lax.optimization_barrier((value,) + others)[0]


def z_rows(block):
    return jnp.concatenate([block] + [flip(block, "z", by) for by in (1, 2, 3)])


def term_kernel(core_ref, grad_ref, up_ref, keep_ref, send_ref):
    half = keep_ref.shape[2]
    part = lax.dot_general(
        grad_ref[...], up_ref[...], (((1,), (1,)), ((), ())), preferred_element_type=F32
    )
    first, second = part[:, :half], part[:, half:]
    even = core_ref[0] == 0
    keep_ref[0] = jnp.where(even, first, second)
    send_ref[0] = jnp.where(even, second, first).astype(BF16)


def term_blocks(grad, up, core, half):
    rows, depth = grad.shape
    count = up.shape[0] // (2 * half)
    block = pl.BlockSpec((1, rows, half), lambda i, core: (i, 0, 0))
    shape = (count, rows, half)
    return pl.pallas_call(
        term_kernel,
        grid_spec=pltpu.PrefetchScalarGridSpec(
            num_scalar_prefetch=1,
            grid=(count,),
            in_specs=[
                pl.BlockSpec((rows, depth), lambda i, core: (0, 0)),
                pl.BlockSpec((2 * half, depth), lambda i, core: (i, 0)),
            ],
            out_specs=[block, block],
        ),
        out_shape=[jax.ShapeDtypeStruct(shape, F32), jax.ShapeDtypeStruct(shape, BF16)],
        cost_estimate=pl.CostEstimate(
            flops=4 * count * rows * half * depth,
            bytes_accessed=4 * count * half * depth,
            transcendentals=0,
        ),
        compiler_params=pltpu.CompilerParams(vmem_limit_bytes=20 * 1024 * 1024),
        name="term",
    )(core.reshape(1).astype(jnp.int32), grad, up)


def body(
    wide_up,
    wide_down,
    narrow_up,
    narrow_down,
    wide_input,
    wide_preact,
    narrow_input,
    narrow_preact,
    cotangent,
):
    core = lax.axis_index("c")
    z = lax.axis_index("z")
    yl = lax.axis_index("yl")
    x = lax.axis_index("x")
    yh = lax.axis_index("yh")
    chip = x * 2 + yh
    tokens, side = cotangent.shape
    n_t, n_d = 8, 8
    half = narrow_down.shape[1]

    wide_pre = wide_preact.astype(F32)
    wide_act = jax.nn.silu(wide_pre).astype(BF16)
    act_all = lax.all_gather(wide_act, TOK, axis=0, tiled=True)

    down_come = flip(narrow_down, "yh")
    down_come, up_mine, cot = gate(down_come, narrow_up, cotangent)
    down_pair = jnp.stack([narrow_down, down_come])
    down_cols = jnp.concatenate([down_pair] + [flip(down_pair, "x", by) for by in (1, 2, 3)])
    up_other, cot = gate(flip(up_mine, "c"), cot)
    cot_rows = gather_all(cot, TOK, n_t)
    cot_near = jnp.stack(
        [pick(cot_rows, (x ^ k) * 2 + (yh ^ r), 0) for k in range(4) for r in range(2)]
    )
    keep = cut(cot_near, core * half, half, 2)
    come = flip(cut(cot_near, (1 - core) * half, half, 2), "c")
    down_cols, come, keep = gate(down_cols, come, keep)

    pre_f = narrow_preact.astype(F32)
    hid_send = jnp.einsum("dtk,dfk->tf", come, down_cols, preferred_element_type=F32)
    hid_keep = jnp.einsum("dtk,dfk->tf", keep, down_cols, preferred_element_type=F32)
    hidden_grad = hid_keep + flip(hid_send, "c")
    narrow_pre_grad = (hidden_grad * silu_slope(pre_f)).astype(BF16)

    pre_copies = jnp.broadcast_to(narrow_pre_grad[None], (n_d, tokens, side))
    pre_copies, turned, source = gate(pre_copies, cotangent, wide_input)
    pre_all = exchange(pre_copies, CHIPS).reshape(n_d * tokens, -1)
    group = jnp.where(core == 0, yl, 1 - yl)
    got = [flip(cut(source, (group * 4 + (z ^ by)) * side, side, 1), "z", by) for by in (1, 2, 3)]
    turned = lax.ppermute(
        turned, ("x", "yh", "yl", "z"), [(a * 8 + b, b * 8 + a) for a in range(8) for b in range(8)]
    )
    up_rows = jnp.concatenate(
        [jnp.where(core == 0, narrow_up, up_other), jnp.where(core == 0, up_other, narrow_up)]
    )
    narrow_act = jax.nn.silu(pre_f).astype(BF16)
    down_term = dot(narrow_act, cot_rows.transpose(1, 0, 2).reshape(tokens, -1), ((0,), (0,)))
    pre_all, up_rows, got, turned, down_term = gate(
        pre_all, up_rows, tuple(got), turned, down_term.astype(BF16)
    )
    narrow_down_grad = lax.psum_scatter(
        down_term, ("x", "yh", "c"), scatter_dimension=1, tiled=True
    )

    share = dot(pre_all, up_rows, ((1,), (1,))).astype(BF16)
    share, got = gate(share, jnp.concatenate(got))
    other = flip(got, "c")
    share = exchange(share.reshape(n_t, tokens, -1), TOK)
    share, other, act_all = gate(share, other, act_all)
    own = (turned.astype(F32) + jnp.sum(share.astype(F32), axis=0)).astype(BF16)
    blocks = gather_all(own, CHIPS, n_d)
    mine = cut(wide_input, (yl * 4 + z) * side, side, 1)
    pair = cut(wide_input, ((1 - yl) * 4 + z) * side, side, 1)
    input_own = jnp.concatenate([mine, jnp.where(core == 0, got, other)])
    input_pair = jnp.concatenate([pair, jnp.where(core == 0, other, got)])
    in_blocks = narrow_input.reshape(tokens, n_d, -1).transpose(1, 0, 2)
    blocks, input_pair, input_own, in_blocks = gate(blocks, input_pair, input_own, in_blocks)
    rows = blocks.transpose(1, 0, 2).reshape(tokens, -1)
    rows, blocks = gate(rows, blocks)
    rows_other = flip(rows, "c")
    boundary = jnp.concatenate(
        [jnp.where(core == 0, rows, rows_other), jnp.where(core == 0, rows_other, rows)]
    )
    bound = exchange(blocks, TOK)

    wide_hidden_grad = dot(boundary, wide_down, ((1,), (1,)))
    wide_pre_grad = (wide_hidden_grad * silu_slope(wide_pre)).astype(BF16)
    grad_rows = z_rows(wide_pre_grad)
    term_keep, term_send = term_blocks(wide_pre_grad, wide_up, core, half)
    term_send, in_blocks = gate(term_send, in_blocks)
    term_chip = (term_keep + flip(term_send, "c").astype(F32)).astype(BF16)
    in_own = exchange(in_blocks, CHIPS).reshape(n_d * tokens, side)
    term_chip, bound_other, in_own = gate(term_chip, flip(bound, "c"), in_own)
    term_all = exchange(term_chip, CHIPS)

    up_send = dot(input_pair, grad_rows, ((0,), (0,))).astype(BF16)
    up_come = flip(up_send, "yl")

    bound = jnp.stack(
        [jnp.where(core == 0, bound, bound_other), jnp.where(core == 0, bound_other, bound)], axis=1
    ).reshape(-1, side)
    wide_down_grad = dot(act_all, bound, ((0,), (0,))).astype(BF16)

    up_part = dot(in_own, pre_all, ((0,), (0,)))
    narrow_send = cut(up_part, (1 - core) * half, half, 0).astype(BF16)
    narrow_keep = cut(up_part, core * half, half, 0)
    narrow_up_grad = (narrow_keep + flip(narrow_send, "c").astype(F32)).astype(BF16)

    up_come, wide_down_grad, narrow_up_grad = gate(up_come, wide_down_grad, narrow_up_grad)
    wide_up_grad = (dot(input_own, grad_rows, ((0,), (0,))) + up_come.astype(F32)).astype(BF16)
    own_cols = cut(boundary, (chip * 2 + core) * half, half, 1)
    wide_input_grad = (own_cols.astype(F32) + jnp.sum(term_all.astype(F32), axis=0)).astype(BF16)
    return (wide_input_grad, wide_up_grad, wide_down_grad, narrow_up_grad, narrow_down_grad)


def solution(mesh):
    fine = Mesh(mesh.devices.reshape(4, 2, 2, 2, 4), ("x", "yh", "c", "yl", "z"))
    dp = ("x", "yh", "c")
    tensor = ("yl", "z")
    in_specs = (
        P(None, dp),
        P(dp, None),
        P(dp, tensor),
        P(tensor, dp),
        P(tensor, None),
        P(tensor, dp),
        P(dp, None),
        P(dp, tensor),
        P(dp, tensor),
    )
    out_specs = (
        P(tensor, dp),
        P(tensor, dp),
        P(dp, tensor),
        P(dp, tensor),
        P(tensor, dp),
    )
    return jax.shard_map(body, mesh=fine, in_specs=in_specs, out_specs=out_specs, check_vma=False)
```

time: 269 us -> 249 us (0.926)
  local copies, waits for them, and re-layouts: 43 us -> 20.8 us
  starting transfers between devices: 57.4 us -> 63 us
  other arithmetic: 11.8 us -> 16.7 us
  waiting for transfers between devices: 101 us -> 97.9 us
    ppermute x23 -> x19, waiting for transfers between devices: 69.5 us -> 55.4 us  [flip(): return lax.ppermute(value, axis, [(i, i ^ by) for i in range(size)])]
    unnamed x74 -> x50, local copies, waits for them, and re-layouts: 18.8 us -> 6.48 us
    all_to_all x6 -> x7, starting transfers between devices: 26.4 us -> 38.7 us  [exchange(): return lax.all_to_all(value, axes, 0, 0, tiled=True)]
    all_to_all x6 -> x7, waiting for transfers between devices: 31.3 us -> 42.5 us  [exchange(): return lax.all_to_all(value, axes, 0, 0, tiled=True)]
    reshape x2 -> x0, local copies, waits for them, and re-layouts: 7.96 us -> none  [the longest x1 6.47 us: body(): down_term.astype(BF16).reshape(side, n_d * side)]
    ppermute x23 -> x19, starting transfers between devices: 29.6 us -> 22.1 us  [flip(): return lax.ppermute(value, axis, [(i, i ^ by) for i in range(size)])]
    dot_general x7, matrix products: 23.5 us -> 27.1 us  [dot(): lax.dot_general(left, right, (dims, ((), ())), preferred_element_type=F32)]
    another operation x2 -> x3, other arithmetic: 0.17 us -> 3.7 us  [the longest x2 1.9 us: body(): jnp.stack([jnp.where(core == 0, bound, bound_other), jnp.where(core == 0,...]
  transfers between devices with their start and end apart: 32 -> 29, of which waited for: 17 -> 12; matrix products, arithmetic and copies ran while one was open for 28% -> 23% of each run, Pallas kernels for 3% -> 2%
where the time goes in v3:
time: 249 us; the launch traced here: 248 us
  waiting for transfers between devices  97.9 us (39%)
  starting transfers between devices  63 us (25%)
  matrix products  28.8 us (12%)
  local copies, waits for them, and re-layouts  20.8 us (8%)
  other arithmetic  16.7 us (7%)
  between operations  15.9 us (6%)
  Pallas kernels  5.06 us (2%)
    ppermute x19, waiting for transfers between devices, flip(): return lax.ppermute(value, axis, [(i, i ^ by) for i in range(size)])  55.4 us
    all_to_all x7, waiting for transfers between devices, exchange(): return lax.all_to_all(value, axes, 0, 0, tiled=True)  42.5 us
    all_to_all x7, starting transfers between devices, exchange(): return lax.all_to_all(value, axes, 0, 0, tiled=True)  38.7 us
    dot_general x7, matrix products, dot(): lax.dot_general(left, right, (dims, ((), ())), preferred_element_type=F32)  27.1 us
    ppermute x19, starting transfers between devices, flip(): return lax.ppermute(value, axis, [(i, i ^ by) for i in range(size)])  22.1 us
    unnamed x50, local copies, waits for them, and re-layouts  6.48 us
    pallas_call x1, Pallas kernels, term_blocks(): pl.pallas_call(term_kernel, grid_spec=pltpu.PrefetchScalarGridSpec(num_sc...  5.06 us
  transfers between devices with their start and end apart: 29, of which 12 were waited for; matrix products, arithmetic and copies ran while one was open for 23% of the time, Pallas kernels for 2%

profile of v3, /device:TPU:0, one launch (start us, length us, event | category | flops | bytes accessed | tf_op | source)
XLA Modules:
  0.0 248.2 jit_solution(1491849623754700307)
XLA Ops:
  8.0 2.2 fusion.9
  10.2 3.4 %collective-permute-start = (bf16[512,256]{1,0:T(8,128)(2,1)}, bf16[512,256]{1,0:T(8,128)(2,1)}, u32[]{:S(2)}, u32[]{:S(2)}) collective-permute-start(bf16[512,256]{1,0:T(8,128)(2,1)} %param.12), channel_id=1, source_target_pairs={{0,16},{16,0},{1,17},{17,1},{2,18},{18,2},{3,19},{19,3},{4,20},{20... | collective-permute-start | bytes 786440 | tf_op jit(solution)/shard_map/ppermute | solution.py:54
  13.6 6.6 %collective-permute-done = bf16[512,256]{1,0:T(8,128)(2,1)} collective-permute-done((bf16[512,256]{1,0:T(8,128)(2,1)}, bf16[512,256]{1,0:T(8,128)(2,1)}, u32[]{:S(2)}, u32[]{:S(2)}) %collective-permute-start) | collective-permute-done | bytes 262176 | tf_op jit(solution)/shard_map/ppermute | solution.py:54
  20.2 1.9 collective-permute-done.4
  24.2 6.4 %all-to-all-start = ((bf16[8,128,512]{1,2,0:T(8,128)(2,1)}), bf16[8,128,512]{1,2,0:T(8,128)(2,1)S(1)}, u32[]{:S(2)}, u32[]{:S(2)}) async-start(bf16[8,128,512]{1,2,0:T(8,128)(2,1)} %broadcast_in_dim.6), calls=%async_computation | async-start | bytes 2097152 | tf_op jit(solution)/shard_map/all_to_all | solution.py:58
  32.4 2.8 %collective-permute-start.3 = (bf16[2,512,256]{2,1,0:T(8,128)(2,1)}, bf16[2,512,256]{2,1,0:T(8,128)(2,1)}, u32[]{:S(2)}, u32[]{:S(2)}) collective-permute-start(bf16[2,512,256]{2,1,0:T(8,128)(2,1)} %pad_maximum_fusion.11), channel_id=1, source_target_pairs={{0,96},{32,64},{64,32},{96,0},{1,97},{33,65},{65,33},{97,1},{2,98}... | collective-permute-start | bytes 1572872 | tf_op jit(solution)/shard_map/ppermute | solution.py:54
  36.5 21.9 %all-to-all-done = bf16[8,128,512]{1,2,0:T(8,128)(2,1)S(1)} async-done(((bf16[8,128,512]{1,2,0:T(8,128)(2,1)}), bf16[8,128,512]{1,2,0:T(8,128)(2,1)S(1)}, u32[]{:S(2)}, u32[]{:S(2)}) %all-to-all-start) | async-done | bytes 1048608 | tf_op jit(solution)/shard_map/all_to_all | solution.py:58
  67.7 6.6 %all-to-all-start.1 = ((bf16[8,128,512]{2,1,0:T(8,128)(2,1)}), bf16[8,128,512]{2,1,0:T(8,128)(2,1)S(1)}, u32[]{:S(2)}, u32[]{:S(2)}) async-start(bf16[8,128,512]{2,1,0:T(8,128)(2,1)} %broadcast_in_dim.7), calls=%async_computation.1 | async-start | bytes 2097152 | tf_op jit(solution)/shard_map/all_to_all | solution.py:58
  75.3 2.2 collective-permute-start.10
  78.7 6.9 %collective-permute-start.9 = (bf16[256,512]{1,0:T(8,128)(2,1)S(1)}, bf16[256,512]{1,0:T(8,128)(2,1)}, u32[]{:S(2)}, u32[]{:S(2)}) collective-permute-start(bf16[256,512]{1,0:T(8,128)(2,1)S(1)} %get-tuple-element.94), channel_id=1, source_target_pairs={{0,3},{1,2},{2,1},{3,0},{4,7},{5,6},{6,5},{7,4},{8,11},{9,10},{10,... | collective-permute-start | bytes 786440 | tf_op jit(solution)/shard_map/ppermute | solution.py:54
  86.6 3.3 %convolution_convert_fusion = bf16[512,4096]{1,0:T(8,128)(2,1)} fusion(bf16[128,4096]{0,1:T(8,128)(2,1)S(1)} %bitcast.48, bf16[128,512]{1,0:T(8,128)(2,1)S(1)} %copy-done.13), kind=kOutput, calls=%fused_computation | convolution fusion | flops 539361280 | bytes 5373952 | tf_op jit(solution)/shard_map/dot_general | solution.py:20
  89.9 9.4 %collective-permute-done.9 = bf16[256,512]{1,0:T(8,128)(2,1)} collective-permute-done((bf16[256,512]{1,0:T(8,128)(2,1)S(1)}, bf16[256,512]{1,0:T(8,128)(2,1)}, u32[]{:S(2)}, u32[]{:S(2)}) %collective-permute-start.9) | collective-permute-done | bytes 262176 | tf_op jit(solution)/shard_map/ppermute | solution.py:54
  99.3 1.9 collective-permute-done.7
  104.5 4.5 %all-to-all-start.2 = ((bf16[8,128,512]{2,1,0:T(8,128)(2,1)}), bf16[8,128,512]{2,1,0:T(8,128)(2,1)S(1)}, u32[]{:S(2)}, u32[]{:S(2)}) async-start(bf16[8,128,512]{2,1,0:T(8,128)(2,1)} %bitcast.7), calls=%async_computation.2 | async-start | bytes 2097152 | tf_op jit(solution)/shard_map/all_to_all | solution.py:58
  109.0 2.3 collective-permute-done.11
  111.3 11.5 %all-to-all-done.2 = bf16[8,128,512]{2,1,0:T(8,128)(2,1)S(1)} async-done(((bf16[8,128,512]{2,1,0:T(8,128)(2,1)}), bf16[8,128,512]{2,1,0:T(8,128)(2,1)S(1)}, u32[]{:S(2)}, u32[]{:S(2)}) %all-to-all-start.2) | async-done | bytes 1048608 | tf_op jit(solution)/shard_map/all_to_all | solution.py:58
  125.2 6.2 %all-to-all-start.3 = ((bf16[8,128,512]{1,2,0:T(8,128)(2,1)}), bf16[8,128,512]{1,2,0:T(8,128)(2,1)}, u32[]{:S(2)}, u32[]{:S(2)}) async-start(bf16[8,128,512]{1,2,0:T(8,128)(2,1)} %broadcast_in_dim.8), calls=%async_computation.3 | async-start | bytes 2097152 | tf_op jit(solution)/shard_map/all_to_all | solution.py:58
  135.4 9.1 %all-to-all-done.3 = bf16[8,128,512]{1,2,0:T(8,128)(2,1)} async-done(((bf16[8,128,512]{1,2,0:T(8,128)(2,1)}), bf16[8,128,512]{1,2,0:T(8,128)(2,1)}, u32[]{:S(2)}, u32[]{:S(2)}) %all-to-all-start.3) | async-done | bytes 1048608 | tf_op jit(solution)/shard_map/all_to_all | solution.py:58
  146.2 5.9 %all-to-all-start.4 = ((bf16[8,128,512]{1,2,0:T(8,128)(2,1)}), bf16[8,128,512]{1,2,0:T(8,128)(2,1)}, u32[]{:S(2)}, u32[]{:S(2)}) async-start(bf16[8,128,512]{1,2,0:T(8,128)(2,1)} %all-to-all-done.3), calls=%async_computation.4 | async-start | bytes 2097152 | tf_op jit(solution)/shard_map/all_to_all | solution.py:58
  153.1 7.4 %fusion.2.grad_ref = bf16[256,1024]{1,0:T(8,128)(2,1)S(1)} fusion(bf16[1024,4096]{1,0:T(8,128)(2,1)} %param.10, bf16[128,4096]{1,0:T(8,128)(2,1)S(1)} %get-tuple-element.91, bf16[128,4096]{1,0:T(8,128)(2,1)S(1)} %get-tuple-element.90, bf16[256,1024]{1,0:T(8,128)(2,1)S(1)} %copy-done.12), kind=kOutput, calls=%fused_computation.18 | convolution fusion | flops 2154299392 | bytes 11534336 | tf_op jit(solution)/shard_map/dot_general | solution.py:20
  160.5 5.1 %term.1 = (f32[8,256,256]{2,1,0:T(8,128)S(1)}, bf16[8,256,256]{2,1,0:T(8,128)(2,1)}) custom-call(s32[1]{0:T(128)} %bitcast.12.core_ref, bf16[256,1024]{1,0:T(8,128)(2,1)S(1)} %fusion.2.grad_ref, bf16[4096,1024]{1,0:T(8,128)(2,1)S(1)} %bitcast.47), custom_call_target="tpu_custom_call" | custom-call | flops 2147483648 | bytes 8388608 | tf_op jit(solution)/shard_map/term/pallas_call | solution.py:97
  165.8 3.1 %collective-permute-start.17 = (bf16[256,1024]{1,0:T(8,128)(2,1)S(1)}, bf16[256,1024]{1,0:T(8,128)(2,1)S(1)}, u32[]{:S(2)}, u32[]{:S(2)}) collective-permute-start(bf16[256,1024]{1,0:T(8,128)(2,1)S(1)} %fusion.2.grad_ref), channel_id=1, source_target_pairs={{0,3},{1,2},{2,1},{3,0},{4,7},{5,6},{6,5},{7,4},{8,11},{9,10},{10,... | collective-permute-start | bytes 1572872 | tf_op jit(solution)/shard_map/ppermute | solution.py:54
  169.9 4.4 %all-to-all-start.5 = ((bf16[8,128,512]{1,2,0:T(8,128)(2,1)}), bf16[8,128,512]{1,2,0:T(8,128)(2,1)}, u32[]{:S(2)}, u32[]{:S(2)}) async-start(bf16[8,128,512]{1,2,0:T(8,128)(2,1)} %bitcast.49), calls=%async_computation.5 | async-start | bytes 2097152 | tf_op jit(solution)/shard_map/all_to_all | solution.py:58
  174.3 18.4 %collective-permute-done.17 = bf16[256,1024]{1,0:T(8,128)(2,1)S(1)} collective-permute-done((bf16[256,1024]{1,0:T(8,128)(2,1)S(1)}, bf16[256,1024]{1,0:T(8,128)(2,1)S(1)}, u32[]{:S(2)}, u32[]{:S(2)}) %collective-permute-start.17) | collective-permute-done | bytes 524320 | tf_op jit(solution)/shard_map/ppermute | solution.py:54
  193.4 3.8 %convolution_convert_fusion.1 = bf16[512,1024]{1,0:T(8,128)(2,1)} fusion(bf16[1024,512]{1,0:T(8,128)(2,1)} %get-tuple-element.75, bf16[256,1024]{1,0:T(8,128)(2,1)S(1)} %collective-permute-done.17, bf16[256,1024]{1,0:T(8,128)(2,1)} %collective-permute-done.16, bf16[256,1024]{1,0:T(8,128)(2,1)} %collective-permute-done.15, ...), kind=kOutput, calls=%fused_computation.14 | convolution fusion | flops 1082654720 | bytes 4194304 | tf_op jit(solution)/shard_map/dot_general | solution.py:20
  198.9 2.3 copy.34
  201.2 2.5 add_convert_fusion.1
  203.6 4.8 %all-to-all-start.6 = ((bf16[8,256,256]{2,1,0:T(8,128)(2,1)}), bf16[8,256,256]{2,1,0:T(8,128)(2,1)}, u32[]{:S(2)}, u32[]{:S(2)}) async-start(bf16[8,256,256]{2,1,0:T(8,128)(2,1)} %add_convert_fusion.1), calls=%async_computation.6 | async-start | bytes 2097152 | tf_op jit(solution)/shard_map/all_to_all | solution.py:58
  212.1 2.6 %copy.35 = bf16[8,2,128,512]{3,2,1,0:T(8,128)(2,1)} copy(bf16[8,2,128,512]{2,3,0,1:T(8,128)(2,1)S(1)} %pad_maximum_fusion.3) | data formatting | bytes 4194304 | tf_op jit(solution)/shard_map/stack | solution.py:217
  214.7 6.3 %convolution_convert_fusion.3 = bf16[1024,512]{1,0:T(8,128)(2,1)} fusion(bf16[2048,1024]{1,0:T(8,128)(2,1)} %all-gather.2.cloned.1.call-done, bf16[2048,512]{1,0:T(8,128)(2,1)} %bitcast.50), kind=kOutput, calls=%fused_computation.16 | convolution fusion | flops 2148007936 | bytes 7340032 | tf_op jit(solution)/shard_map/dot_general | solution.py:20
  221.8 12.9 %collective-permute-done.18 = bf16[512,1024]{1,0:T(8,128)(2,1)} collective-permute-done((bf16[512,1024]{1,0:T(8,128)(2,1)}, bf16[512,1024]{1,0:T(8,128)(2,1)}, u32[]{:S(2)}, u32[]{:S(2)}) %collective-permute-start.18) | collective-permute-done | bytes 1048608 | tf_op jit(solution)/shard_map/ppermute | solution.py:54
  234.8 3.8 %add_convert_fusion = bf16[512,1024]{1,0:T(8,128)(2,1)} fusion(bf16[512,1024]{1,0:T(8,128)(2,1)} %collective-permute-done.18, bf16[1024,512]{1,0:T(8,128)(2,1)S(1)} %copy-done.9, bf16[256,1024]{1,0:T(8,128)(2,1)S(1)} %copy-done.16, bf16[256,1024]{1,0:T(8,128)(2,1)} %collective-permute-done.16, bf16[256,1024]{1,0:T(8,128)(2,1)} %collective-permute-done.15, ...), kind=kOutput, calls=%fused_computation.7 | convolution fusion | flops 1083703296 | bytes 5242880 | tf_op jit(solution)/shard_map/dot_general | solution.py:20
  (119 shorter events, 40.0 us)
Async XLA Ops:
  8.0 114.8 %all-gather.2.cloned.1.call-start = ((), (), s32[]{:S(2)}) async-start(), calls=%async_computation.8 | async-start | bytes 4718592 | tf_op jit(solution)/shard_map/all_gather | solution.py:142
  10.2 20.4 %copy-start.8 = (bf16[512,256]{1,0:T(8,128)(2,1)S(1)}, bf16[512,256]{1,0:T(8,128)(2,1)}, u32[]{:S(2)}) copy-start(bf16[512,256]{1,0:T(8,128)(2,1)} %param.12) | copy-start | bytes 786436
  10.2 10.0 %collective-permute-start = (bf16[512,256]{1,0:T(8,128)(2,1)}, bf16[512,256]{1,0:T(8,128)(2,1)}, u32[]{:S(2)}, u32[]{:S(2)}) collective-permute-start(bf16[512,256]{1,0:T(8,128)(2,1)} %param.12), channel_id=1, source_target_pairs={{0,16},{16,0},{1,17},{17,1},{2,18},{18,2},{3,19},{19,3},{4,20},{20... | collective-permute-start | bytes 786440 | tf_op jit(solution)/shard_map/ppermute | solution.py:54
  20.2 1.9 collective-permute-start.4
  24.2 34.2 %all-to-all-start = ((bf16[8,128,512]{1,2,0:T(8,128)(2,1)}), bf16[8,128,512]{1,2,0:T(8,128)(2,1)S(1)}, u32[]{:S(2)}, u32[]{:S(2)}) async-start(bf16[8,128,512]{1,2,0:T(8,128)(2,1)} %broadcast_in_dim.6), calls=%async_computation | async-start | bytes 2097152 | tf_op jit(solution)/shard_map/all_to_all | solution.py:58
  32.4 29.6 %collective-permute-start.3 = (bf16[2,512,256]{2,1,0:T(8,128)(2,1)}, bf16[2,512,256]{2,1,0:T(8,128)(2,1)}, u32[]{:S(2)}, u32[]{:S(2)}) collective-permute-start(bf16[2,512,256]{2,1,0:T(8,128)(2,1)} %pad_maximum_fusion.11), channel_id=1, source_target_pairs={{0,96},{32,64},{64,32},{96,0},{1,97},{33,65},{65,33},{97,1},{2,98}... | collective-permute-start | bytes 1572872 | tf_op jit(solution)/shard_map/ppermute | solution.py:54
  35.2 25.7 %collective-permute-start.2 = (bf16[2,512,256]{2,1,0:T(8,128)(2,1)}, bf16[2,512,256]{2,1,0:T(8,128)(2,1)}, u32[]{:S(2)}, u32[]{:S(2)}) collective-permute-start(bf16[2,512,256]{2,1,0:T(8,128)(2,1)} %pad_maximum_fusion.11), channel_id=1, source_target_pairs={{0,64},{32,96},{64,0},{96,32},{1,65},{33,97},{65,1},{97,33},{2,66}... | collective-permute-start | bytes 1572872 | tf_op jit(solution)/shard_map/ppermute | solution.py:54
  36.0 23.8 %collective-permute-start.1 = (bf16[2,512,256]{2,1,0:T(8,128)(2,1)}, bf16[2,512,256]{2,1,0:T(8,128)(2,1)}, u32[]{:S(2)}, u32[]{:S(2)}) collective-permute-start(bf16[2,512,256]{2,1,0:T(8,128)(2,1)} %pad_maximum_fusion.11), channel_id=1, source_target_pairs={{0,32},{32,0},{64,96},{96,64},{1,33},{33,1},{65,97},{97,65},{2,34}... | collective-permute-start | bytes 1572872 | tf_op jit(solution)/shard_map/ppermute | solution.py:54
  58.8 4.4 %collective-permute-start.5 = (bf16[8,128,256]{1,2,0:T(8,128)(2,1)S(1)}, bf16[8,128,256]{1,2,0:T(8,128)(2,1)S(1)}, u32[]{:S(2)}, u32[]{:S(2)}) collective-permute-start(bf16[8,128,256]{1,2,0:T(8,128)(2,1)S(1)} %get-tuple-element.100), channel_id=1, source_target_pairs={{0,8},{8,0},{1,9},{9,1},{2,10},{10,2},{3,11},{11,3},{4,12},{12,4},... | collective-permute-start | bytes 1572872 | tf_op jit(solution)/shard_map/ppermute | solution.py:54
  64.0 1.7 collective-permute-start.6
  67.7 33.6 %all-to-all-start.1 = ((bf16[8,128,512]{2,1,0:T(8,128)(2,1)}), bf16[8,128,512]{2,1,0:T(8,128)(2,1)S(1)}, u32[]{:S(2)}, u32[]{:S(2)}) async-start(bf16[8,128,512]{2,1,0:T(8,128)(2,1)} %broadcast_in_dim.7), calls=%async_computation.1 | async-start | bytes 2097152 | tf_op jit(solution)/shard_map/all_to_all | solution.py:58
  75.3 14.5 %collective-permute-start.10 = (bf16[128,512]{1,0:T(8,128)(2,1)}, bf16[128,512]{1,0:T(8,128)(2,1)}, u32[]{:S(2)}, u32[]{:S(2)}) collective-permute-start(bf16[128,512]{1,0:T(8,128)(2,1)} %param.17), channel_id=1, source_target_pairs={{0,0},{1,16},{2,32},{3,48},{4,64},{5,80},{6,96},{7,112},{16,1},{17... | collective-permute-start | bytes 393224 | tf_op jit(solution)/shard_map/ppermute | solution.py:168
  78.7 20.6 %collective-permute-start.9 = (bf16[256,512]{1,0:T(8,128)(2,1)S(1)}, bf16[256,512]{1,0:T(8,128)(2,1)}, u32[]{:S(2)}, u32[]{:S(2)}) collective-permute-start(bf16[256,512]{1,0:T(8,128)(2,1)S(1)} %get-tuple-element.94), channel_id=1, source_target_pairs={{0,3},{1,2},{2,1},{3,0},{4,7},{5,6},{6,5},{7,4},{8,11},{9,10},{10,... | collective-permute-start | bytes 786440 | tf_op jit(solution)/shard_map/ppermute | solution.py:54
  85.6 13.7 %collective-permute-start.8 = (bf16[256,512]{1,0:T(8,128)(2,1)S(1)}, bf16[256,512]{1,0:T(8,128)(2,1)}, u32[]{:S(2)}, u32[]{:S(2)}) collective-permute-start(bf16[256,512]{1,0:T(8,128)(2,1)S(1)} %get-tuple-element.95), channel_id=1, source_target_pairs={{0,2},{1,3},{2,0},{3,1},{4,6},{5,7},{6,4},{7,5},{8,10},{9,11},{10,... | collective-permute-start | bytes 786440 | tf_op jit(solution)/shard_map/ppermute | solution.py:54
  85.6 15.6 %collective-permute-start.7 = (bf16[256,512]{1,0:T(8,128)(2,1)S(1)}, bf16[256,512]{1,0:T(8,128)(2,1)}, u32[]{:S(2)}, u32[]{:S(2)}) collective-permute-start(bf16[256,512]{1,0:T(8,128)(2,1)S(1)} %get-tuple-element.96), channel_id=1, source_target_pairs={{0,1},{1,0},{2,3},{3,2},{4,5},{5,4},{6,7},{7,6},{8,9},{9,8},{10,11... | collective-permute-start | bytes 786440 | tf_op jit(solution)/shard_map/ppermute | solution.py:54
  104.5 18.3 %all-to-all-start.2 = ((bf16[8,128,512]{2,1,0:T(8,128)(2,1)}), bf16[8,128,512]{2,1,0:T(8,128)(2,1)S(1)}, u32[]{:S(2)}, u32[]{:S(2)}) async-start(bf16[8,128,512]{2,1,0:T(8,128)(2,1)} %bitcast.7), calls=%async_computation.2 | async-start | bytes 2097152 | tf_op jit(solution)/shard_map/all_to_all | solution.py:58
  109.0 2.3 collective-permute-start.11
  125.2 19.3 %all-to-all-start.3 = ((bf16[8,128,512]{1,2,0:T(8,128)(2,1)}), bf16[8,128,512]{1,2,0:T(8,128)(2,1)}, u32[]{:S(2)}, u32[]{:S(2)}) async-start(bf16[8,128,512]{1,2,0:T(8,128)(2,1)} %broadcast_in_dim.8), calls=%async_computation.3 | async-start | bytes 2097152 | tf_op jit(solution)/shard_map/all_to_all | solution.py:58
  131.4 109.4 %reduce-scatter.2.cloned.1.call-start = ((), (), s32[]{:S(2)}) async-start(), calls=%async_computation.9 | async-start | bytes 4456448 | tf_op jit(solution)/shard_map/reduce_scatter | solution.py:179
  146.0 6.0 %collective-permute-start.12 = (bf16[128,4096]{1,0:T(8,128)(2,1)S(1)}, bf16[128,4096]{1,0:T(8,128)(2,1)S(1)}, u32[]{:S(2)}, u32[]{:S(2)}) collective-permute-start(bf16[128,4096]{1,0:T(8,128)(2,1)S(1)} %copy.32), channel_id=1, source_target_pairs={{0,8},{8,0},{1,9},{9,1},{2,10},{10,2},{3,11},{11,3},{4,12},{12,4},... | collective-permute-start | bytes 3145736 | tf_op jit(solution)/shard_map/ppermute | solution.py:54
  146.2 23.7 %all-to-all-start.4 = ((bf16[8,128,512]{1,2,0:T(8,128)(2,1)}), bf16[8,128,512]{1,2,0:T(8,128)(2,1)}, u32[]{:S(2)}, u32[]{:S(2)}) async-start(bf16[8,128,512]{1,2,0:T(8,128)(2,1)} %all-to-all-done.3), calls=%async_computation.4 | async-start | bytes 2097152 | tf_op jit(solution)/shard_map/all_to_all | solution.py:58
  165.6 35.6 %collective-permute-start.13 = (bf16[8,256,256]{2,1,0:T(8,128)(2,1)}, bf16[8,256,256]{2,1,0:T(8,128)(2,1)}, u32[]{:S(2)}, u32[]{:S(2)}) collective-permute-start(bf16[8,256,256]{2,1,0:T(8,128)(2,1)} %get-tuple-element.70), channel_id=1, source_target_pairs={{0,8},{8,0},{1,9},{9,1},{2,10},{10,2},{3,11},{11,3},{4,12},{12,4},... | collective-permute-start | bytes 3145736 | tf_op jit(solution)/shard_map/ppermute | solution.py:54
  165.8 26.9 %collective-permute-start.17 = (bf16[256,1024]{1,0:T(8,128)(2,1)S(1)}, bf16[256,1024]{1,0:T(8,128)(2,1)S(1)}, u32[]{:S(2)}, u32[]{:S(2)}) collective-permute-start(bf16[256,1024]{1,0:T(8,128)(2,1)S(1)} %fusion.2.grad_ref), channel_id=1, source_target_pairs={{0,3},{1,2},{2,1},{3,0},{4,7},{5,6},{6,5},{7,4},{8,11},{9,10},{10,... | collective-permute-start | bytes 1572872 | tf_op jit(solution)/shard_map/ppermute | solution.py:54
  168.8 23.8 %collective-permute-start.16 = (bf16[256,1024]{1,0:T(8,128)(2,1)S(1)}, bf16[256,1024]{1,0:T(8,128)(2,1)}, u32[]{:S(2)}, u32[]{:S(2)}) collective-permute-start(bf16[256,1024]{1,0:T(8,128)(2,1)S(1)} %fusion.2.grad_ref), channel_id=1, source_target_pairs={{0,2},{1,3},{2,0},{3,1},{4,6},{5,7},{6,4},{7,5},{8,10},{9,11},{10,... | collective-permute-start | bytes 1572872 | tf_op jit(solution)/shard_map/ppermute | solution.py:54
  169.6 23.8 %collective-permute-start.15 = (bf16[256,1024]{1,0:T(8,128)(2,1)S(1)}, bf16[256,1024]{1,0:T(8,128)(2,1)}, u32[]{:S(2)}, u32[]{:S(2)}) collective-permute-start(bf16[256,1024]{1,0:T(8,128)(2,1)S(1)} %fusion.2.grad_ref), channel_id=1, source_target_pairs={{0,1},{1,0},{2,3},{3,2},{4,5},{5,4},{6,7},{7,6},{8,9},{9,8},{10,11... | collective-permute-start | bytes 1572872 | tf_op jit(solution)/shard_map/ppermute | solution.py:54
  169.9 29.0 %all-to-all-start.5 = ((bf16[8,128,512]{1,2,0:T(8,128)(2,1)}), bf16[8,128,512]{1,2,0:T(8,128)(2,1)}, u32[]{:S(2)}, u32[]{:S(2)}) async-start(bf16[8,128,512]{1,2,0:T(8,128)(2,1)} %bitcast.49), calls=%async_computation.5 | async-start | bytes 2097152 | tf_op jit(solution)/shard_map/all_to_all | solution.py:58
  174.3 29.4 %collective-permute-start.14 = (bf16[8,128,512]{1,2,0:T(8,128)(2,1)}, bf16[8,128,512]{1,2,0:T(8,128)(2,1)}, u32[]{:S(2)}, u32[]{:S(2)}) collective-permute-start(bf16[8,128,512]{1,2,0:T(8,128)(2,1)} %all-to-all-done.4), channel_id=1, source_target_pairs={{0,8},{8,0},{1,9},{9,1},{2,10},{10,2},{3,11},{11,3},{4,12},{12,4},... | collective-permute-start | bytes 3145736 | tf_op jit(solution)/shard_map/ppermute | solution.py:54
  197.2 37.5 %collective-permute-start.18 = (bf16[512,1024]{1,0:T(8,128)(2,1)}, bf16[512,1024]{1,0:T(8,128)(2,1)}, u32[]{:S(2)}, u32[]{:S(2)}) collective-permute-start(bf16[512,1024]{1,0:T(8,128)(2,1)} %convolution_convert_fusion.1), channel_id=1, source_target_pairs={{0,4},{4,0},{1,5},{5,1},{2,6},{6,2},{3,7},{7,3},{8,12},{12,8},{9,1... | collective-permute-start | bytes 3145736 | tf_op jit(solution)/shard_map/ppermute | solution.py:54
  203.6 35.0 %all-to-all-start.6 = ((bf16[8,256,256]{2,1,0:T(8,128)(2,1)}), bf16[8,256,256]{2,1,0:T(8,128)(2,1)}, u32[]{:S(2)}, u32[]{:S(2)}) async-start(bf16[8,256,256]{2,1,0:T(8,128)(2,1)} %add_convert_fusion.1), calls=%async_computation.6 | async-start | bytes 2097152 | tf_op jit(solution)/shard_map/all_to_all | solution.py:58
  210.1 10.9 %collective-permute-start.19 = (bf16[256,512]{1,0:T(8,128)(2,1)S(1)}, bf16[256,512]{1,0:T(8,128)(2,1)S(1)}, u32[]{:S(2)}, u32[]{:S(2)}) collective-permute-start(bf16[256,512]{1,0:T(8,128)(2,1)S(1)} %dynamic-slice_convert_fusion), channel_id=1, source_target_pairs={{0,8},{8,0},{1,9},{9,1},{2,10},{10,2},{3,11},{11,3},{4,12},{12,4},... | collective-permute-start | bytes 786440 | tf_op jit(solution)/shard_map/ppermute | solution.py:54
  214.7 20.1 %copy-start.9 = (bf16[1024,512]{1,0:T(8,128)(2,1)S(1)}, bf16[1024,512]{1,0:T(8,128)(2,1)}, u32[]{:S(2)}) copy-start(bf16[1024,512]{1,0:T(8,128)(2,1)} %get-tuple-element.74) | copy-start | bytes 3145732
  214.7 20.1 %copy-start.16 = (bf16[256,1024]{1,0:T(8,128)(2,1)S(1)}, bf16[256,1024]{1,0:T(8,128)(2,1)}, u32[]{:S(2)}) copy-start(bf16[256,1024]{1,0:T(8,128)(2,1)} %copy-done.15) | copy-start | bytes 1572868
  (16 other events, 114.4 us)
Sparse Core Ops, SparseCore 0:
  10.5 66.5 all-gather.1
Sparse Core Ops, SparseCore 1:
  146.2 91.1 reduce-scatter.1

commit v4 on v3

--- a/solution.py
+++ b/solution.py
@@ -161,38 +161,34 @@
     narrow_pre_grad = (hidden_grad * silu_slope(pre_f)).astype(BF16)
 
     pre_copies = jnp.broadcast_to(narrow_pre_grad[None], (n_d, tokens, side))
-    pre_copies, turned, source = gate(pre_copies, cotangent, wide_input)
+    pre_copies, turned = gate(pre_copies, cotangent)
     pre_all = exchange(pre_copies, CHIPS).reshape(n_d * tokens, -1)
+    turned = lax.ppermute(
+        turned, ("x", "yh", "yl", "z"), [(a * 8 + b, b * 8 + a) for a in range(8) for b in range(8)]
+    )
+    up_rows = jnp.concatenate(
+        [jnp.where(core == 0, narrow_up, up_other), jnp.where(core == 0, up_other, narrow_up)]
+    )
+    narrow_act = jax.nn.silu(pre_f).astype(BF16)
+    down_term = dot(narrow_act, cot_rows.transpose(1, 0, 2).reshape(tokens, -1), ((0,), (0,)))
+    pre_all, up_rows, turned, down_term, act_all = gate(
+        pre_all, up_rows, turned, down_term.astype(BF16), act_all
+    )
+    narrow_down_grad = lax.psum_scatter(
+        down_term, ("x", "yh", "c"), scatter_dimension=1, tiled=True
+    )
+
+    share = dot(pre_all, up_rows, ((1,), (1,))).astype(BF16)
+    share = exchange(share.reshape(n_t, tokens, -1), TOK)
+    own = (turned.astype(F32) + jnp.sum(share.astype(F32), axis=0)).astype(BF16)
+    own_copies = jnp.broadcast_to(own[None], (n_d, tokens, side))
+    own_copies, source = gate(own_copies, wide_input)
+    blocks = exchange(own_copies, CHIPS)
     group = jnp.where(core == 0, yl, 1 - yl)
     got = [flip(cut(source, (group * 4 + (z ^ by)) * side, side, 1), "z", by) for by in (1, 2, 3)]
-    turned = lax.ppermute(
-        turned, ("x", "yh", "yl", "z"), [(a * 8 + b, b * 8 + a) for a in range(8) for b in range(8)]
-    )
-    up_rows = jnp.concatenate(
-        [jnp.where(core == 0, narrow_up, up_other), jnp.where(core == 0, up_other, narrow_up)]
-    )
-    narrow_act = jax.nn.silu(pre_f).astype(BF16)
-    down_term = dot(narrow_act, cot_rows.transpose(1, 0, 2).reshape(tokens, -1), ((0,), (0,)))
-    pre_all, up_rows, got, turned, down_term = gate(
-        pre_all, up_rows, tuple(got), turned, down_term.astype(BF16)
-    )
-    narrow_down_grad = lax.psum_scatter(
-        down_term, ("x", "yh", "c"), scatter_dimension=1, tiled=True
-    )
-
-    share = dot(pre_all, up_rows, ((1,), (1,))).astype(BF16)
-    share, got = gate(share, jnp.concatenate(got))
-    other = flip(got, "c")
-    share = exchange(share.reshape(n_t, tokens, -1), TOK)
-    share, other, act_all = gate(share, other, act_all)
-    own = (turned.astype(F32) + jnp.sum(share.astype(F32), axis=0)).astype(BF16)
-    blocks = gather_all(own, CHIPS, n_d)
-    mine = cut(wide_input, (yl * 4 + z) * side, side, 1)
-    pair = cut(wide_input, ((1 - yl) * 4 + z) * side, side, 1)
-    input_own = jnp.concatenate([mine, jnp.where(core == 0, got, other)])
-    input_pair = jnp.concatenate([pair, jnp.where(core == 0, other, got)])
     in_blocks = narrow_input.reshape(tokens, n_d, -1).transpose(1, 0, 2)
-    blocks, input_pair, input_own, in_blocks = gate(blocks, input_pair, input_own, in_blocks)
+    blocks, got, in_blocks = gate(blocks, tuple(got), in_blocks)
+    got = jnp.concatenate(got)
     rows = blocks.transpose(1, 0, 2).reshape(tokens, -1)
     rows, blocks = gate(rows, blocks)
     rows_other = flip(rows, "c")
@@ -203,14 +199,20 @@
 
     wide_hidden_grad = dot(boundary, wide_down, ((1,), (1,)))
     wide_pre_grad = (wide_hidden_grad * silu_slope(wide_pre)).astype(BF16)
+    wide_pre_grad, got = gate(wide_pre_grad, got)
     grad_rows = z_rows(wide_pre_grad)
     term_keep, term_send = term_blocks(wide_pre_grad, wide_up, core, half)
     term_send, in_blocks = gate(term_send, in_blocks)
     term_chip = (term_keep + flip(term_send, "c").astype(F32)).astype(BF16)
     in_own = exchange(in_blocks, CHIPS).reshape(n_d * tokens, side)
-    term_chip, bound_other, in_own = gate(term_chip, flip(bound, "c"), in_own)
+    term_chip, bound_other, narrow_down_grad = gate(term_chip, flip(bound, "c"), narrow_down_grad)
     term_all = exchange(term_chip, CHIPS)
 
+    other = flip(got, "c")
+    mine = cut(wide_input, (yl * 4 + z) * side, side, 1)
+    pair = cut(wide_input, ((1 - yl) * 4 + z) * side, side, 1)
+    input_own = jnp.concatenate([mine, jnp.where(core == 0, got, other)])
+    input_pair = jnp.concatenate([pair, jnp.where(core == 0, other, got)])
     up_send = dot(input_pair, grad_rows, ((0,), (0,))).astype(BF16)
     up_come = flip(up_send, "yl")
 
@@ -219,6 +221,7 @@
     ).reshape(-1, side)
     wide_down_grad = dot(act_all, bound, ((0,), (0,))).astype(BF16)
 
+    wide_down_grad, in_own = gate(wide_down_grad, in_own)
     up_part = dot(in_own, pre_all, ((0,), (0,)))
     narrow_send = cut(up_part, (1 - core) * half, half, 0).astype(BF16)
     narrow_keep = cut(up_part, core * half, half, 0)
@@ -227,6 +230,7 @@
     up_come, wide_down_grad, narrow_up_grad = gate(up_come, wide_down_grad, narrow_up_grad)
     wide_up_grad = (dot(input_own, grad_rows, ((0,), (0,))) + up_come.astype(F32)).astype(BF16)
     own_cols = cut(boundary, (chip * 2 + core) * half, half, 1)
+    wide_up_grad, own_cols = gate(wide_up_grad, own_cols)
     wide_input_grad = (own_cols.astype(F32) + jnp.sum(term_all.astype(F32), axis=0)).astype(BF16)
     return (wide_input_grad, wide_up_grad, wide_down_grad, narrow_up_grad, narrow_down_grad)
 

time: 249 us -> 243 us (0.976)
  waiting for transfers between devices: 97.9 us -> 84.6 us
  local copies, waits for them, and re-layouts: 20.8 us -> 33 us
    ppermute x19, waiting for transfers between devices: 55.4 us -> 29 us  [flip(): return lax.ppermute(value, axis, [(i, i ^ by) for i in range(size)])]
    all_to_all x7, waiting for transfers between devices: 42.5 us -> 51.4 us  [exchange(): return lax.all_to_all(value, axes, 0, 0, tiled=True)]
    unnamed x50 -> x53, local copies, waits for them, and re-layouts: 6.48 us -> 15.2 us
    ppermute x19, starting transfers between devices: 22.1 us -> 18.5 us  [flip(): return lax.ppermute(value, axis, [(i, i ^ by) for i in range(size)])]
    reduce_scatter x1, waiting for transfers between devices: 0.01 us -> 3.56 us  [body(): lax.psum_scatter(down_term, ('x', 'yh', 'c'), scatter_dimension=1, tiled=...]
    all_to_all x7, starting transfers between devices: 38.7 us -> 42 us  [exchange(): return lax.all_to_all(value, axes, 0, 0, tiled=True)]
  transfers between devices with their start and end apart: 29 -> 29, of which waited for: 12 -> 13; matrix products, arithmetic and copies ran while one was open for 23% -> 27% of each run, Pallas kernels for 2% -> 2%
where the time goes in v4:
time: 243 us; the launch traced here: 241 us
  waiting for transfers between devices  84.6 us (35%)
  starting transfers between devices  61.3 us (25%)
  local copies, waits for them, and re-layouts  33 us (14%)
  matrix products  27.6 us (11%)
  other arithmetic  15.5 us (6%)
  between operations  14.5 us (6%)
  Pallas kernels  5.01 us (2%)
    all_to_all x7, waiting for transfers between devices, exchange(): return lax.all_to_all(value, axes, 0, 0, tiled=True)  51.4 us
    all_to_all x7, starting transfers between devices, exchange(): return lax.all_to_all(value, axes, 0, 0, tiled=True)  42 us
    ppermute x19, waiting for transfers between devices, flip(): return lax.ppermute(value, axis, [(i, i ^ by) for i in range(size)])  29 us
    dot_general x7, matrix products, dot(): lax.dot_general(left, right, (dims, ((), ())), preferred_element_type=F32)  25.9 us
    ppermute x19, starting transfers between devices, flip(): return lax.ppermute(value, axis, [(i, i ^ by) for i in range(size)])  18.5 us
    unnamed x53, local copies, waits for them, and re-layouts  15.2 us
    pallas_call x1, Pallas kernels, term_blocks(): pl.pallas_call(term_kernel, grid_spec=pltpu.PrefetchScalarGridSpec(num_sc...  5.01 us
  transfers between devices with their start and end apart: 29, of which 13 were waited for; matrix products, arithmetic and copies ran while one was open for 27% of the time, Pallas kernels for 2%

profile of v4, /device:TPU:0, one launch (start us, length us, event | category | flops | bytes accessed | tf_op | source)
XLA Modules:
  0.0 241.4 jit_solution(9031945622512651276)
XLA Ops:
  7.2 2.2 fusion.9
  9.4 3.4 %collective-permute-start = (bf16[512,256]{1,0:T(8,128)(2,1)}, bf16[512,256]{1,0:T(8,128)(2,1)}, u32[]{:S(2)}, u32[]{:S(2)}) collective-permute-start(bf16[512,256]{1,0:T(8,128)(2,1)} %param.12), channel_id=1, source_target_pairs={{0,16},{16,0},{1,17},{17,1},{2,18},{18,2},{3,19},{19,3},{4,20},{20... | collective-permute-start | bytes 786440 | tf_op jit(solution)/shard_map/ppermute | solution.py:54
  12.7 6.6 %collective-permute-done = bf16[512,256]{1,0:T(8,128)(2,1)} collective-permute-done((bf16[512,256]{1,0:T(8,128)(2,1)}, bf16[512,256]{1,0:T(8,128)(2,1)}, u32[]{:S(2)}, u32[]{:S(2)}) %collective-permute-start) | collective-permute-done | bytes 262176 | tf_op jit(solution)/shard_map/ppermute | solution.py:54
  23.4 6.4 %all-to-all-start = ((bf16[8,128,512]{1,2,0:T(8,128)(2,1)}), bf16[8,128,512]{1,2,0:T(8,128)(2,1)S(1)}, u32[]{:S(2)}, u32[]{:S(2)}) async-start(bf16[8,128,512]{1,2,0:T(8,128)(2,1)} %broadcast_in_dim.6), calls=%async_computation | async-start | bytes 2097152 | tf_op jit(solution)/shard_map/all_to_all | solution.py:58
  31.6 2.8 %collective-permute-start.3 = (bf16[2,512,256]{2,1,0:T(8,128)(2,1)}, bf16[2,512,256]{2,1,0:T(8,128)(2,1)}, u32[]{:S(2)}, u32[]{:S(2)}) collective-permute-start(bf16[2,512,256]{2,1,0:T(8,128)(2,1)} %pad_maximum_fusion.8), channel_id=1, source_target_pairs={{0,96},{32,64},{64,32},{96,0},{1,97},{33,65},{65,33},{97,1},{2,98}... | collective-permute-start | bytes 1572872 | tf_op jit(solution)/shard_map/ppermute | solution.py:54
  35.7 21.9 %all-to-all-done = bf16[8,128,512]{1,2,0:T(8,128)(2,1)S(1)} async-done(((bf16[8,128,512]{1,2,0:T(8,128)(2,1)}), bf16[8,128,512]{1,2,0:T(8,128)(2,1)S(1)}, u32[]{:S(2)}, u32[]{:S(2)}) %all-to-all-start) | async-done | bytes 1048608 | tf_op jit(solution)/shard_map/all_to_all | solution.py:58
  66.8 6.8 %all-to-all-start.1 = ((bf16[8,128,512]{2,1,0:T(8,128)(2,1)}), bf16[8,128,512]{2,1,0:T(8,128)(2,1)S(1)}, u32[]{:S(2)}, u32[]{:S(2)}) async-start(bf16[8,128,512]{2,1,0:T(8,128)(2,1)} %broadcast_in_dim.7), calls=%async_computation.1 | async-start | bytes 2097152 | tf_op jit(solution)/shard_map/all_to_all | solution.py:58
  75.3 3.3 %convolution_convert_fusion = bf16[512,4096]{1,0:T(8,128)(2,1)} fusion(bf16[128,4096]{0,1:T(8,128)(2,1)S(1)} %bitcast.46, bf16[128,512]{1,0:T(8,128)(2,1)S(1)} %copy-done.12), kind=kOutput, calls=%fused_computation | convolution fusion | flops 539361280 | bytes 5373952 | tf_op jit(solution)/shard_map/dot_general | solution.py:20
  78.6 13.0 %all-to-all-done.1 = bf16[8,128,512]{2,1,0:T(8,128)(2,1)S(1)} async-done(((bf16[8,128,512]{2,1,0:T(8,128)(2,1)}), bf16[8,128,512]{2,1,0:T(8,128)(2,1)S(1)}, u32[]{:S(2)}, u32[]{:S(2)}) %all-to-all-start.1) | async-done | bytes 1048608 | tf_op jit(solution)/shard_map/all_to_all | solution.py:58
  93.3 8.7 %all-to-all-start.2 = ((bf16[8,128,512]{2,1,0:T(8,128)(2,1)}), bf16[8,128,512]{2,1,0:T(8,128)(2,1)S(1)}, u32[]{:S(2)}, u32[]{:S(2)}) async-start(bf16[8,128,512]{2,1,0:T(8,128)(2,1)} %bitcast.7), calls=%async_computation.2 | async-start | bytes 2097152 | tf_op jit(solution)/shard_map/all_to_all | solution.py:58
  102.8 14.0 %all-to-all-done.2 = bf16[8,128,512]{2,1,0:T(8,128)(2,1)S(1)} async-done(((bf16[8,128,512]{2,1,0:T(8,128)(2,1)}), bf16[8,128,512]{2,1,0:T(8,128)(2,1)S(1)}, u32[]{:S(2)}, u32[]{:S(2)}) %all-to-all-start.2) | async-done | bytes 1048608 | tf_op jit(solution)/shard_map/all_to_all | solution.py:58
  118.2 4.7 %all-to-all-start.3 = ((bf16[8,128,512]{1,2,0:T(8,128)(2,1)}), bf16[8,128,512]{1,2,0:T(8,128)(2,1)}, u32[]{:S(2)}, u32[]{:S(2)}) async-start(bf16[8,128,512]{1,2,0:T(8,128)(2,1)} %broadcast_in_dim.8), calls=%async_computation.3 | async-start | bytes 2097152 | tf_op jit(solution)/shard_map/all_to_all | solution.py:58
  129.6 9.0 %collective-permute-done.10 = bf16[256,512]{1,0:T(8,128)(2,1)S(1)} collective-permute-done((bf16[256,512]{1,0:T(8,128)(2,1)S(1)}, bf16[256,512]{1,0:T(8,128)(2,1)S(1)}, u32[]{:S(2)}, u32[]{:S(2)}) %collective-permute-start.10) | collective-permute-done | bytes 262176 | tf_op jit(solution)/shard_map/ppermute | solution.py:54
  141.6 4.4 %all-to-all-start.4 = ((bf16[8,128,512]{1,2,0:T(8,128)(2,1)}), bf16[8,128,512]{1,2,0:T(8,128)(2,1)}, u32[]{:S(2)}, u32[]{:S(2)}) async-start(bf16[8,128,512]{1,2,0:T(8,128)(2,1)} %all-to-all-done.3), calls=%async_computation.4 | async-start | bytes 2097152 | tf_op jit(solution)/shard_map/all_to_all | solution.py:58
  148.1 6.0 %fusion.2.grad_ref = bf16[256,1024]{1,0:T(8,128)(2,1)S(1)} fusion(bf16[1024,4096]{1,0:T(8,128)(2,1)} %param.10, bf16[128,4096]{1,0:T(8,128)(2,1)S(1)} %get-tuple-element.95, bf16[128,4096]{1,0:T(8,128)(2,1)S(1)} %get-tuple-element.94, bf16[256,1024]{1,0:T(8,128)(2,1)S(1)} %copy-done.11), kind=kOutput, calls=%fused_computation.17 | convolution fusion | flops 2154299392 | bytes 11534336 | tf_op jit(solution)/shard_map/dot_general | solution.py:20
  155.8 2.7 %collective-permute-start.14 = (bf16[256,1024]{1,0:T(8,128)(2,1)S(1)}, bf16[256,1024]{1,0:T(8,128)(2,1)}, u32[]{:S(2)}, u32[]{:S(2)}) collective-permute-start(bf16[256,1024]{1,0:T(8,128)(2,1)S(1)} %fusion.2.grad_ref), channel_id=1, source_target_pairs={{0,2},{1,3},{2,0},{3,1},{4,6},{5,7},{6,4},{7,5},{8,10},{9,11},{10,... | collective-permute-start | bytes 1572872 | tf_op jit(solution)/shard_map/ppermute | solution.py:54
  160.7 3.4 %copy-done = bf16[4096,1024]{1,0:T(8,128)(2,1)S(1)} copy-done((bf16[4096,1024]{1,0:T(8,128)(2,1)S(1)}, bf16[4096,1024]{1,0:T(8,128)(2,1)}, u32[]{:S(2)}) %copy-start) | copy-done | bytes 8388632
  164.1 5.0 %term.1 = (f32[8,256,256]{2,1,0:T(8,128)S(1)}, bf16[8,256,256]{2,1,0:T(8,128)(2,1)}) custom-call(s32[1]{0:T(128)} %bitcast.12.core_ref, bf16[256,1024]{1,0:T(8,128)(2,1)S(1)} %fusion.2.grad_ref, bf16[4096,1024]{1,0:T(8,128)(2,1)S(1)} %copy-done), custom_call_target="tpu_custom_call" | custom-call | flops 2147483648 | bytes 8388608 | tf_op jit(solution)/shard_map/term/pallas_call | solution.py:97
  170.2 7.3 %all-to-all-start.5 = ((bf16[8,128,512]{1,2,0:T(8,128)(2,1)}), bf16[8,128,512]{1,2,0:T(8,128)(2,1)}, u32[]{:S(2)}, u32[]{:S(2)}) async-start(bf16[8,128,512]{1,2,0:T(8,128)(2,1)} %bitcast.47), calls=%async_computation.6 | async-start | bytes 2097152 | tf_op jit(solution)/shard_map/all_to_all | solution.py:58
  179.5 7.1 %collective-permute-done.14 = bf16[256,1024]{1,0:T(8,128)(2,1)} collective-permute-done((bf16[256,1024]{1,0:T(8,128)(2,1)S(1)}, bf16[256,1024]{1,0:T(8,128)(2,1)}, u32[]{:S(2)}, u32[]{:S(2)}) %collective-permute-start.14) | collective-permute-done | bytes 524320 | tf_op jit(solution)/shard_map/ppermute | solution.py:54
  188.5 1.9 constant_dynamic-update-slice_fusion.5
  190.4 2.3 broadcast_select_fusion.3
  192.7 2.2 convolution_convert_fusion.1
  196.0 2.3 copy.35
  198.2 2.4 %add_convert_fusion.1 = bf16[8,256,256]{2,1,0:T(8,128)(2,1)} fusion(f32[8,256,256]{2,1,0:T(8,128)S(1)} %get-tuple-element.69, bf16[8,256,256]{2,1,0:T(8,128)(2,1)} %collective-permute-done.17), kind=kLoop, calls=%fused_computation.8 | loop fusion | flops 1572864 | bytes 4194304 | tf_op jit(solution)/shard_map/convert_element_type | solution.py:206
  200.7 3.6 %reduce-scatter.2.cloned.1.call-done = bf16[512,256]{1,0:T(8,128)(2,1)} async-done(((bf16[512,4096]{1,0:T(8,128)(2,1)}), bf16[512,256]{1,0:T(8,128)(2,1)}) %reduce-scatter.2.cloned.1.call-update) | async-done | bytes 262160 | tf_op jit(solution)/shard_map/reduce_scatter | solution.py:177
  206.1 2.6 %copy.34 = bf16[8,2,128,512]{3,2,1,0:T(8,128)(2,1)} copy(bf16[8,2,128,512]{2,3,0,1:T(8,128)(2,1)S(1)} %pad_maximum_fusion.2) | data formatting | bytes 4194304 | tf_op jit(solution)/shard_map/stack | solution.py:219
  208.8 6.2 %convolution_convert_fusion.3 = bf16[1024,512]{1,0:T(8,128)(2,1)} fusion(bf16[2048,1024]{1,0:T(8,128)(2,1)} %all-gather.2.cloned.1.call-done, bf16[2048,512]{1,0:T(8,128)(2,1)} %bitcast.48), kind=kOutput, calls=%fused_computation.15 | convolution fusion | flops 2148007936 | bytes 7340032 | tf_op jit(solution)/shard_map/dot_general | solution.py:20
  215.0 3.7 %all-to-all-start.6 = ((bf16[8,256,256]{2,1,0:T(8,128)(2,1)}), bf16[8,256,256]{2,1,0:T(8,128)(2,1)S(1)}, u32[]{:S(2)}, u32[]{:S(2)}) async-start(bf16[8,256,256]{2,1,0:T(8,128)(2,1)} %add_convert_fusion.1), calls=%async_computation.7 | async-start | bytes 2097152 | tf_op jit(solution)/shard_map/all_to_all | solution.py:58
  218.7 2.4 %fusion.31 = f32[512,512]{1,0:T(8,128)S(1)} fusion(bf16[1024,512]{1,0:T(8,128)(2,1)} %bitcast.51, bf16[1024,512]{1,0:T(8,128)(2,1)} %bitcast.50), kind=kOutput, calls=%fused_computation.89 | convolution fusion | flops 536870912 | bytes 3145728 | tf_op jit(solution)/shard_map/dot_general | solution.py:20
  227.1 4.1 %add_convert_fusion = bf16[512,1024]{1,0:T(8,128)(2,1)} fusion(bf16[512,1024]{1,0:T(8,128)(2,1)} %collective-permute-done.16, bf16[1024,1024]{1,0:T(8,128)(2,1)} %constant_dynamic-update-slice_fusion.5, bf16[768,512]{1,0:T(8,128)(2,1)S(1)} %copy-done.8, bf16[256,512]{1,0:T(8,128)(2,1)S(1)} %copy-done.13), kind=kOutput, calls=%fused_computation.7 | convolution fusion | flops 1077411840 | bytes 5242880 | tf_op jit(solution)/shard_map/dot_general | solution.py:20
  231.2 2.6 %all-to-all-done.6 = bf16[8,256,256]{2,1,0:T(8,128)(2,1)S(1)} async-done(((bf16[8,256,256]{2,1,0:T(8,128)(2,1)}), bf16[8,256,256]{2,1,0:T(8,128)(2,1)S(1)}, u32[]{:S(2)}, u32[]{:S(2)}) %all-to-all-start.6) | async-done | bytes 1048608 | tf_op jit(solution)/shard_map/all_to_all | solution.py:58
  (122 shorter events, 52.1 us)
Async XLA Ops:
  7.2 84.5 %all-gather.2.cloned.1.call-start = ((), (), s32[]{:S(2)}) async-start(), calls=%async_computation.8 | async-start | bytes 4718592 | tf_op jit(solution)/shard_map/all_gather | solution.py:142
  9.4 20.4 %copy-start.7 = (bf16[512,256]{1,0:T(8,128)(2,1)S(1)}, bf16[512,256]{1,0:T(8,128)(2,1)}, u32[]{:S(2)}) copy-start(bf16[512,256]{1,0:T(8,128)(2,1)} %param.12) | copy-start | bytes 786436
  9.4 10.0 %collective-permute-start = (bf16[512,256]{1,0:T(8,128)(2,1)}, bf16[512,256]{1,0:T(8,128)(2,1)}, u32[]{:S(2)}, u32[]{:S(2)}) collective-permute-start(bf16[512,256]{1,0:T(8,128)(2,1)} %param.12), channel_id=1, source_target_pairs={{0,16},{16,0},{1,17},{17,1},{2,18},{18,2},{3,19},{19,3},{4,20},{20... | collective-permute-start | bytes 786440 | tf_op jit(solution)/shard_map/ppermute | solution.py:54
  19.4 1.9 collective-permute-start.4
  23.4 34.2 %all-to-all-start = ((bf16[8,128,512]{1,2,0:T(8,128)(2,1)}), bf16[8,128,512]{1,2,0:T(8,128)(2,1)S(1)}, u32[]{:S(2)}, u32[]{:S(2)}) async-start(bf16[8,128,512]{1,2,0:T(8,128)(2,1)} %broadcast_in_dim.6), calls=%async_computation | async-start | bytes 2097152 | tf_op jit(solution)/shard_map/all_to_all | solution.py:58
  31.6 29.6 %collective-permute-start.3 = (bf16[2,512,256]{2,1,0:T(8,128)(2,1)}, bf16[2,512,256]{2,1,0:T(8,128)(2,1)}, u32[]{:S(2)}, u32[]{:S(2)}) collective-permute-start(bf16[2,512,256]{2,1,0:T(8,128)(2,1)} %pad_maximum_fusion.8), channel_id=1, source_target_pairs={{0,96},{32,64},{64,32},{96,0},{1,97},{33,65},{65,33},{97,1},{2,98}... | collective-permute-start | bytes 1572872 | tf_op jit(solution)/shard_map/ppermute | solution.py:54
  34.3 25.7 %collective-permute-start.2 = (bf16[2,512,256]{2,1,0:T(8,128)(2,1)}, bf16[2,512,256]{2,1,0:T(8,128)(2,1)}, u32[]{:S(2)}, u32[]{:S(2)}) collective-permute-start(bf16[2,512,256]{2,1,0:T(8,128)(2,1)} %pad_maximum_fusion.8), channel_id=1, source_target_pairs={{0,64},{32,96},{64,0},{96,32},{1,65},{33,97},{65,1},{97,33},{2,66}... | collective-permute-start | bytes 1572872 | tf_op jit(solution)/shard_map/ppermute | solution.py:54
  35.1 23.8 %collective-permute-start.1 = (bf16[2,512,256]{2,1,0:T(8,128)(2,1)}, bf16[2,512,256]{2,1,0:T(8,128)(2,1)}, u32[]{:S(2)}, u32[]{:S(2)}) collective-permute-start(bf16[2,512,256]{2,1,0:T(8,128)(2,1)} %pad_maximum_fusion.8), channel_id=1, source_target_pairs={{0,32},{32,0},{64,96},{96,64},{1,33},{33,1},{65,97},{97,65},{2,34}... | collective-permute-start | bytes 1572872 | tf_op jit(solution)/shard_map/ppermute | solution.py:54
  57.9 4.4 %collective-permute-start.5 = (bf16[8,128,256]{1,2,0:T(8,128)(2,1)S(1)}, bf16[8,128,256]{1,2,0:T(8,128)(2,1)S(1)}, u32[]{:S(2)}, u32[]{:S(2)}) collective-permute-start(bf16[8,128,256]{1,2,0:T(8,128)(2,1)S(1)} %get-tuple-element.102), channel_id=1, source_target_pairs={{0,8},{8,0},{1,9},{9,1},{2,10},{10,2},{3,11},{11,3},{4,12},{12,4},... | collective-permute-start | bytes 1572872 | tf_op jit(solution)/shard_map/ppermute | solution.py:54
  63.1 1.7 collective-permute-start.6
  65.7 7.9 %copy-start.15 = (bf16[256,512]{1,0:T(8,128)(2,1)S(1)}, bf16[256,512]{1,0:T(8,128)(2,1)}, u32[]{:S(2)}) copy-start(bf16[256,512]{1,0:T(8,128)(2,1)} %param.11) | copy-start | bytes 786436
  66.8 24.8 %all-to-all-start.1 = ((bf16[8,128,512]{2,1,0:T(8,128)(2,1)}), bf16[8,128,512]{2,1,0:T(8,128)(2,1)S(1)}, u32[]{:S(2)}, u32[]{:S(2)}) async-start(bf16[8,128,512]{2,1,0:T(8,128)(2,1)} %broadcast_in_dim.7), calls=%async_computation.1 | async-start | bytes 2097152 | tf_op jit(solution)/shard_map/all_to_all | solution.py:58
  74.6 4.0 %collective-permute-start.7 = (bf16[128,512]{1,0:T(8,128)(2,1)S(1)}, bf16[128,512]{1,0:T(8,128)(2,1)S(1)}, u32[]{:S(2)}, u32[]{:S(2)}) collective-permute-start(bf16[128,512]{1,0:T(8,128)(2,1)S(1)} %copy-done.18), channel_id=1, source_target_pairs={{0,0},{1,16},{2,32},{3,48},{4,64},{5,80},{6,96},{7,112},{16,1},{17... | collective-permute-start | bytes 393224 | tf_op jit(solution)/shard_map/ppermute | solution.py:166
  93.3 23.4 %all-to-all-start.2 = ((bf16[8,128,512]{2,1,0:T(8,128)(2,1)}), bf16[8,128,512]{2,1,0:T(8,128)(2,1)S(1)}, u32[]{:S(2)}, u32[]{:S(2)}) async-start(bf16[8,128,512]{2,1,0:T(8,128)(2,1)} %bitcast.7), calls=%async_computation.2 | async-start | bytes 2097152 | tf_op jit(solution)/shard_map/all_to_all | solution.py:58
  102.1 102.2 %reduce-scatter.2.cloned.1.call-start = ((), (), s32[]{:S(2)}) async-start(), calls=%async_computation.9 | async-start | bytes 4456448 | tf_op jit(solution)/shard_map/reduce_scatter | solution.py:177
  118.2 10.1 %copy-start.5 = (bf16[128,4096]{1,0:T(8,128)(2,1)S(1)}, bf16[128,4096]{1,0:T(8,128)(2,1)}, u32[]{:S(2)}) copy-start(bf16[128,4096]{1,0:T(8,128)(2,1)} %param.15) | copy-start | bytes 3145732
  118.2 21.1 %all-to-all-start.3 = ((bf16[8,128,512]{1,2,0:T(8,128)(2,1)}), bf16[8,128,512]{1,2,0:T(8,128)(2,1)}, u32[]{:S(2)}, u32[]{:S(2)}) async-start(bf16[8,128,512]{1,2,0:T(8,128)(2,1)} %broadcast_in_dim.8), calls=%async_computation.3 | async-start | bytes 2097152 | tf_op jit(solution)/shard_map/all_to_all | solution.py:58
  124.1 14.5 %collective-permute-start.10 = (bf16[256,512]{1,0:T(8,128)(2,1)S(1)}, bf16[256,512]{1,0:T(8,128)(2,1)S(1)}, u32[]{:S(2)}, u32[]{:S(2)}) collective-permute-start(bf16[256,512]{1,0:T(8,128)(2,1)S(1)} %get-tuple-element.96), channel_id=1, source_target_pairs={{0,3},{1,2},{2,1},{3,0},{4,7},{5,6},{6,5},{7,4},{8,11},{9,10},{10,... | collective-permute-start | bytes 786440 | tf_op jit(solution)/shard_map/ppermute | solution.py:54
  125.7 13.0 %collective-permute-start.9 = (bf16[256,512]{1,0:T(8,128)(2,1)S(1)}, bf16[256,512]{1,0:T(8,128)(2,1)S(1)}, u32[]{:S(2)}, u32[]{:S(2)}) collective-permute-start(bf16[256,512]{1,0:T(8,128)(2,1)S(1)} %get-tuple-element.97), channel_id=1, source_target_pairs={{0,2},{1,3},{2,0},{3,1},{4,6},{5,7},{6,4},{7,5},{8,10},{9,11},{10,... | collective-permute-start | bytes 786440 | tf_op jit(solution)/shard_map/ppermute | solution.py:54
  127.1 12.1 %collective-permute-start.8 = (bf16[256,512]{1,0:T(8,128)(2,1)S(1)}, bf16[256,512]{1,0:T(8,128)(2,1)S(1)}, u32[]{:S(2)}, u32[]{:S(2)}) collective-permute-start(bf16[256,512]{1,0:T(8,128)(2,1)S(1)} %get-tuple-element.98), channel_id=1, source_target_pairs={{0,1},{1,0},{2,3},{3,2},{4,5},{5,4},{6,7},{7,6},{8,9},{9,8},{10,11... | collective-permute-start | bytes 786440 | tf_op jit(solution)/shard_map/ppermute | solution.py:54
  141.5 5.6 %collective-permute-start.11 = (bf16[128,4096]{1,0:T(8,128)(2,1)S(1)}, bf16[128,4096]{1,0:T(8,128)(2,1)S(1)}, u32[]{:S(2)}, u32[]{:S(2)}) collective-permute-start(bf16[128,4096]{1,0:T(8,128)(2,1)S(1)} %copy.32), channel_id=1, source_target_pairs={{0,8},{8,0},{1,9},{9,1},{2,10},{10,2},{3,11},{11,3},{4,12},{12,4},... | collective-permute-start | bytes 3145736 | tf_op jit(solution)/shard_map/ppermute | solution.py:54
  141.6 28.6 %all-to-all-start.4 = ((bf16[8,128,512]{1,2,0:T(8,128)(2,1)}), bf16[8,128,512]{1,2,0:T(8,128)(2,1)}, u32[]{:S(2)}, u32[]{:S(2)}) async-start(bf16[8,128,512]{1,2,0:T(8,128)(2,1)} %all-to-all-done.3), calls=%async_computation.4 | async-start | bytes 2097152 | tf_op jit(solution)/shard_map/all_to_all | solution.py:58
  154.0 23.4 %collective-permute-start.13 = (bf16[256,1024]{1,0:T(8,128)(2,1)S(1)}, bf16[256,1024]{1,0:T(8,128)(2,1)}, u32[]{:S(2)}, u32[]{:S(2)}) collective-permute-start(bf16[256,1024]{1,0:T(8,128)(2,1)S(1)} %fusion.2.grad_ref), channel_id=1, source_target_pairs={{0,1},{1,0},{2,3},{3,2},{4,5},{5,4},{6,7},{7,6},{8,9},{9,8},{10,11... | collective-permute-start | bytes 1572872 | tf_op jit(solution)/shard_map/ppermute | solution.py:54
  155.8 30.7 %collective-permute-start.14 = (bf16[256,1024]{1,0:T(8,128)(2,1)S(1)}, bf16[256,1024]{1,0:T(8,128)(2,1)}, u32[]{:S(2)}, u32[]{:S(2)}) collective-permute-start(bf16[256,1024]{1,0:T(8,128)(2,1)S(1)} %fusion.2.grad_ref), channel_id=1, source_target_pairs={{0,2},{1,3},{2,0},{3,1},{4,6},{5,7},{6,4},{7,5},{8,10},{9,11},{10,... | collective-permute-start | bytes 1572872 | tf_op jit(solution)/shard_map/ppermute | solution.py:54
  158.5 31.9 %collective-permute-start.12 = (bf16[768,512]{1,0:T(8,128)(2,1)S(1)}, bf16[768,512]{1,0:T(8,128)(2,1)}, u32[]{:S(2)}, u32[]{:S(2)}) collective-permute-start(bf16[768,512]{1,0:T(8,128)(2,1)S(1)} %pad_maximum_fusion.7), channel_id=1, source_target_pairs={{0,8},{8,0},{1,9},{9,1},{2,10},{10,2},{3,11},{11,3},{4,12},{12,4},... | collective-permute-start | bytes 2359304 | tf_op jit(solution)/shard_map/ppermute | solution.py:54
  160.4 28.1 %collective-permute-start.15 = (bf16[256,1024]{1,0:T(8,128)(2,1)S(1)}, bf16[256,1024]{1,0:T(8,128)(2,1)}, u32[]{:S(2)}, u32[]{:S(2)}) collective-permute-start(bf16[256,1024]{1,0:T(8,128)(2,1)S(1)} %fusion.2.grad_ref), channel_id=1, source_target_pairs={{0,3},{1,2},{2,1},{3,0},{4,7},{5,6},{6,5},{7,4},{8,11},{9,10},{10,... | collective-permute-start | bytes 1572872 | tf_op jit(solution)/shard_map/ppermute | solution.py:54
  169.1 29.2 %collective-permute-start.17 = (bf16[8,256,256]{2,1,0:T(8,128)(2,1)}, bf16[8,256,256]{2,1,0:T(8,128)(2,1)}, u32[]{:S(2)}, u32[]{:S(2)}) collective-permute-start(bf16[8,256,256]{2,1,0:T(8,128)(2,1)} %get-tuple-element.72), channel_id=1, source_target_pairs={{0,8},{8,0},{1,9},{9,1},{2,10},{10,2},{3,11},{11,3},{4,12},{12,4},... | collective-permute-start | bytes 3145736 | tf_op jit(solution)/shard_map/ppermute | solution.py:54
  170.2 25.8 %all-to-all-start.5 = ((bf16[8,128,512]{1,2,0:T(8,128)(2,1)}), bf16[8,128,512]{1,2,0:T(8,128)(2,1)}, u32[]{:S(2)}, u32[]{:S(2)}) async-start(bf16[8,128,512]{1,2,0:T(8,128)(2,1)} %bitcast.47), calls=%async_computation.6 | async-start | bytes 2097152 | tf_op jit(solution)/shard_map/all_to_all | solution.py:58
  177.5 23.2 %collective-permute-start.18 = (bf16[8,128,512]{1,2,0:T(8,128)(2,1)}, bf16[8,128,512]{1,2,0:T(8,128)(2,1)}, u32[]{:S(2)}, u32[]{:S(2)}) collective-permute-start(bf16[8,128,512]{1,2,0:T(8,128)(2,1)} %all-to-all-done.4), channel_id=1, source_target_pairs={{0,8},{8,0},{1,9},{9,1},{2,10},{10,2},{3,11},{11,3},{4,12},{12,4},... | collective-permute-start | bytes 3145736 | tf_op jit(solution)/shard_map/ppermute | solution.py:54
  195.0 32.1 %collective-permute-start.16 = (bf16[512,1024]{1,0:T(8,128)(2,1)}, bf16[512,1024]{1,0:T(8,128)(2,1)}, u32[]{:S(2)}, u32[]{:S(2)}) collective-permute-start(bf16[512,1024]{1,0:T(8,128)(2,1)} %convolution_convert_fusion.1), channel_id=1, source_target_pairs={{0,4},{4,0},{1,5},{5,1},{2,6},{6,2},{3,7},{7,3},{8,12},{12,8},{9,1... | collective-permute-start | bytes 3145736 | tf_op jit(solution)/shard_map/ppermute | solution.py:54
  215.0 18.8 %all-to-all-start.6 = ((bf16[8,256,256]{2,1,0:T(8,128)(2,1)}), bf16[8,256,256]{2,1,0:T(8,128)(2,1)S(1)}, u32[]{:S(2)}, u32[]{:S(2)}) async-start(bf16[8,256,256]{2,1,0:T(8,128)(2,1)} %add_convert_fusion.1), calls=%async_computation.7 | async-start | bytes 2097152 | tf_op jit(solution)/shard_map/all_to_all | solution.py:58
  222.8 1.9 collective-permute-start.19
  (16 other events, 59.1 us)
Sparse Core Ops, SparseCore 0:
  9.6 66.5 all-gather.1
  107.5 96.6 reduce-scatter.1

commit v5 on v4

--- a/solution.py
+++ b/solution.py
@@ -145,14 +145,14 @@
     down_come, up_mine, cot = gate(down_come, narrow_up, cotangent)
     down_pair = jnp.stack([narrow_down, down_come])
     down_cols = jnp.concatenate([down_pair] + [flip(down_pair, "x", by) for by in (1, 2, 3)])
-    up_other, cot = gate(flip(up_mine, "c"), cot)
+    up_other = flip(up_mine, "c")
     cot_rows = gather_all(cot, TOK, n_t)
     cot_near = jnp.stack(
         [pick(cot_rows, (x ^ k) * 2 + (yh ^ r), 0) for k in range(4) for r in range(2)]
     )
     keep = cut(cot_near, core * half, half, 2)
     come = flip(cut(cot_near, (1 - core) * half, half, 2), "c")
-    down_cols, come, keep = gate(down_cols, come, keep)
+    down_cols, come, keep, up_other = gate(down_cols, come, keep, up_other)
 
     pre_f = narrow_preact.astype(F32)
     hid_send = jnp.einsum("dtk,dfk->tf", come, down_cols, preferred_element_type=F32)

time: 243 us -> 240 us (0.988)
  transfers between devices with their start and end apart: 29 -> 29, of which waited for: 13 -> 12; matrix products, arithmetic and copies ran while one was open for 27% -> 27% of each run, Pallas kernels for 2% -> 2%
where the time goes in v5:
time: 240 us; the launch traced here: 239 us
  waiting for transfers between devices  84.6 us (35%)
  starting transfers between devices  59.8 us (25%)
  local copies, waits for them, and re-layouts  33 us (14%)
  matrix products  27.6 us (12%)
  other arithmetic  14.5 us (6%)
  between operations  14.5 us (6%)
  Pallas kernels  5 us (2%)
    all_to_all x7, waiting for transfers between devices, exchange(): return lax.all_to_all(value, axes, 0, 0, tiled=True)  52.8 us
    all_to_all x7, starting transfers between devices, exchange(): return lax.all_to_all(value, axes, 0, 0, tiled=True)  40.6 us
    ppermute x19, waiting for transfers between devices, flip(): return lax.ppermute(value, axis, [(i, i ^ by) for i in range(size)])  27.6 us
    dot_general x7, matrix products, dot(): lax.dot_general(left, right, (dims, ((), ())), preferred_element_type=F32)  25.9 us
    ppermute x19, starting transfers between devices, flip(): return lax.ppermute(value, axis, [(i, i ^ by) for i in range(size)])  18.5 us
    unnamed x53, local copies, waits for them, and re-layouts  15.2 us
    pallas_call x1, Pallas kernels, term_blocks(): pl.pallas_call(term_kernel, grid_spec=pltpu.PrefetchScalarGridSpec(num_sc...  5 us
  transfers between devices with their start and end apart: 29, of which 12 were waited for; matrix products, arithmetic and copies ran while one was open for 27% of the time, Pallas kernels for 2%

profile of v5, /device:TPU:0, one launch (start us, length us, event | category | flops | bytes accessed | tf_op | source)
XLA Modules:
  0.0 239.0 jit_solution(4563142625648114876)
XLA Ops:
  7.2 2.2 fusion.9
  9.4 3.4 %collective-permute-start = (bf16[512,256]{1,0:T(8,128)(2,1)}, bf16[512,256]{1,0:T(8,128)(2,1)}, u32[]{:S(2)}, u32[]{:S(2)}) collective-permute-start(bf16[512,256]{1,0:T(8,128)(2,1)} %param.12), channel_id=1, source_target_pairs={{0,16},{16,0},{1,17},{17,1},{2,18},{18,2},{3,19},{19,3},{4,20},{20... | collective-permute-start | bytes 786440 | tf_op jit(solution)/shard_map/ppermute | solution.py:54
  12.7 6.6 %collective-permute-done = bf16[512,256]{1,0:T(8,128)(2,1)} collective-permute-done((bf16[512,256]{1,0:T(8,128)(2,1)}, bf16[512,256]{1,0:T(8,128)(2,1)}, u32[]{:S(2)}, u32[]{:S(2)}) %collective-permute-start) | collective-permute-done | bytes 262176 | tf_op jit(solution)/shard_map/ppermute | solution.py:54
  21.5 6.4 %all-to-all-start = ((bf16[8,128,512]{1,2,0:T(8,128)(2,1)}), bf16[8,128,512]{1,2,0:T(8,128)(2,1)S(1)}, u32[]{:S(2)}, u32[]{:S(2)}) async-start(bf16[8,128,512]{1,2,0:T(8,128)(2,1)} %broadcast_in_dim.6), calls=%async_computation | async-start | bytes 2097152 | tf_op jit(solution)/shard_map/all_to_all | solution.py:58
  29.7 2.8 %collective-permute-start.3 = (bf16[2,512,256]{2,1,0:T(8,128)(2,1)}, bf16[2,512,256]{2,1,0:T(8,128)(2,1)}, u32[]{:S(2)}, u32[]{:S(2)}) collective-permute-start(bf16[2,512,256]{2,1,0:T(8,128)(2,1)} %pad_maximum_fusion.8), channel_id=1, source_target_pairs={{0,96},{32,64},{64,32},{96,0},{1,97},{33,65},{65,33},{97,1},{2,98}... | collective-permute-start | bytes 1572872 | tf_op jit(solution)/shard_map/ppermute | solution.py:54
  33.8 21.5 %all-to-all-done = bf16[8,128,512]{1,2,0:T(8,128)(2,1)S(1)} async-done(((bf16[8,128,512]{1,2,0:T(8,128)(2,1)}), bf16[8,128,512]{1,2,0:T(8,128)(2,1)S(1)}, u32[]{:S(2)}, u32[]{:S(2)}) %all-to-all-start) | async-done | bytes 1048608 | tf_op jit(solution)/shard_map/all_to_all | solution.py:58
  64.5 6.6 %all-to-all-start.1 = ((bf16[8,128,512]{2,1,0:T(8,128)(2,1)}), bf16[8,128,512]{2,1,0:T(8,128)(2,1)S(1)}, u32[]{:S(2)}, u32[]{:S(2)}) async-start(bf16[8,128,512]{2,1,0:T(8,128)(2,1)} %broadcast_in_dim.7), calls=%async_computation.1 | async-start | bytes 2097152 | tf_op jit(solution)/shard_map/all_to_all | solution.py:58
  71.2 3.3 %convolution_convert_fusion = bf16[512,4096]{1,0:T(8,128)(2,1)} fusion(bf16[128,4096]{0,1:T(8,128)(2,1)S(1)} %bitcast.46, bf16[128,512]{1,0:T(8,128)(2,1)S(1)} %copy-done.12), kind=kOutput, calls=%fused_computation | convolution fusion | flops 539361280 | bytes 5373952 | tf_op jit(solution)/shard_map/dot_general | solution.py:20
  75.3 15.5 %all-to-all-done.1 = bf16[8,128,512]{2,1,0:T(8,128)(2,1)S(1)} async-done(((bf16[8,128,512]{2,1,0:T(8,128)(2,1)}), bf16[8,128,512]{2,1,0:T(8,128)(2,1)S(1)}, u32[]{:S(2)}, u32[]{:S(2)}) %all-to-all-start.1) | async-done | bytes 1048608 | tf_op jit(solution)/shard_map/all_to_all | solution.py:58
  92.5 7.4 %all-to-all-start.2 = ((bf16[8,128,512]{2,1,0:T(8,128)(2,1)}), bf16[8,128,512]{2,1,0:T(8,128)(2,1)S(1)}, u32[]{:S(2)}, u32[]{:S(2)}) async-start(bf16[8,128,512]{2,1,0:T(8,128)(2,1)} %bitcast.7), calls=%async_computation.2 | async-start | bytes 2097152 | tf_op jit(solution)/shard_map/all_to_all | solution.py:58
  100.6 13.8 %all-to-all-done.2 = bf16[8,128,512]{2,1,0:T(8,128)(2,1)S(1)} async-done(((bf16[8,128,512]{2,1,0:T(8,128)(2,1)}), bf16[8,128,512]{2,1,0:T(8,128)(2,1)S(1)}, u32[]{:S(2)}, u32[]{:S(2)}) %all-to-all-start.2) | async-done | bytes 1048608 | tf_op jit(solution)/shard_map/all_to_all | solution.py:58
  115.8 4.7 %all-to-all-start.3 = ((bf16[8,128,512]{1,2,0:T(8,128)(2,1)}), bf16[8,128,512]{1,2,0:T(8,128)(2,1)}, u32[]{:S(2)}, u32[]{:S(2)}) async-start(bf16[8,128,512]{1,2,0:T(8,128)(2,1)} %broadcast_in_dim.8), calls=%async_computation.3 | async-start | bytes 2097152 | tf_op jit(solution)/shard_map/all_to_all | solution.py:58
  127.2 9.1 %collective-permute-done.10 = bf16[256,512]{1,0:T(8,128)(2,1)S(1)} collective-permute-done((bf16[256,512]{1,0:T(8,128)(2,1)S(1)}, bf16[256,512]{1,0:T(8,128)(2,1)S(1)}, u32[]{:S(2)}, u32[]{:S(2)}) %collective-permute-start.10) | collective-permute-done | bytes 262176 | tf_op jit(solution)/shard_map/ppermute | solution.py:54
  139.2 4.4 %all-to-all-start.4 = ((bf16[8,128,512]{1,2,0:T(8,128)(2,1)}), bf16[8,128,512]{1,2,0:T(8,128)(2,1)}, u32[]{:S(2)}, u32[]{:S(2)}) async-start(bf16[8,128,512]{1,2,0:T(8,128)(2,1)} %all-to-all-done.3), calls=%async_computation.4 | async-start | bytes 2097152 | tf_op jit(solution)/shard_map/all_to_all | solution.py:58
  145.7 6.0 %fusion.2.grad_ref = bf16[256,1024]{1,0:T(8,128)(2,1)S(1)} fusion(bf16[1024,4096]{1,0:T(8,128)(2,1)} %param.10, bf16[128,4096]{1,0:T(8,128)(2,1)S(1)} %get-tuple-element.93, bf16[128,4096]{1,0:T(8,128)(2,1)S(1)} %get-tuple-element.92, bf16[256,1024]{1,0:T(8,128)(2,1)S(1)} %copy-done.11), kind=kOutput, calls=%fused_computation.17 | convolution fusion | flops 2154299392 | bytes 11534336 | tf_op jit(solution)/shard_map/dot_general | solution.py:20
  153.5 2.7 %collective-permute-start.14 = (bf16[256,1024]{1,0:T(8,128)(2,1)S(1)}, bf16[256,1024]{1,0:T(8,128)(2,1)}, u32[]{:S(2)}, u32[]{:S(2)}) collective-permute-start(bf16[256,1024]{1,0:T(8,128)(2,1)S(1)} %fusion.2.grad_ref), channel_id=1, source_target_pairs={{0,2},{1,3},{2,0},{3,1},{4,6},{5,7},{6,4},{7,5},{8,10},{9,11},{10,... | collective-permute-start | bytes 1572872 | tf_op jit(solution)/shard_map/ppermute | solution.py:54
  158.3 3.4 %copy-done = bf16[4096,1024]{1,0:T(8,128)(2,1)S(1)} copy-done((bf16[4096,1024]{1,0:T(8,128)(2,1)S(1)}, bf16[4096,1024]{1,0:T(8,128)(2,1)}, u32[]{:S(2)}) %copy-start) | copy-done | bytes 8388632
  161.7 5.0 %term.1 = (f32[8,256,256]{2,1,0:T(8,128)S(1)}, bf16[8,256,256]{2,1,0:T(8,128)(2,1)}) custom-call(s32[1]{0:T(128)} %bitcast.12.core_ref, bf16[256,1024]{1,0:T(8,128)(2,1)S(1)} %fusion.2.grad_ref, bf16[4096,1024]{1,0:T(8,128)(2,1)S(1)} %copy-done), custom_call_target="tpu_custom_call" | custom-call | flops 2147483648 | bytes 8388608 | tf_op jit(solution)/shard_map/term/pallas_call | solution.py:97
  167.8 7.3 %all-to-all-start.5 = ((bf16[8,128,512]{1,2,0:T(8,128)(2,1)}), bf16[8,128,512]{1,2,0:T(8,128)(2,1)}, u32[]{:S(2)}, u32[]{:S(2)}) async-start(bf16[8,128,512]{1,2,0:T(8,128)(2,1)} %bitcast.47), calls=%async_computation.6 | async-start | bytes 2097152 | tf_op jit(solution)/shard_map/all_to_all | solution.py:58
  177.1 7.1 %collective-permute-done.14 = bf16[256,1024]{1,0:T(8,128)(2,1)} collective-permute-done((bf16[256,1024]{1,0:T(8,128)(2,1)S(1)}, bf16[256,1024]{1,0:T(8,128)(2,1)}, u32[]{:S(2)}, u32[]{:S(2)}) %collective-permute-start.14) | collective-permute-done | bytes 524320 | tf_op jit(solution)/shard_map/ppermute | solution.py:54
  186.1 1.9 constant_dynamic-update-slice_fusion.5
  188.0 2.3 broadcast_select_fusion.3
  190.3 2.2 convolution_convert_fusion.1
  193.6 2.3 copy.35
  195.8 2.4 %add_convert_fusion.1 = bf16[8,256,256]{2,1,0:T(8,128)(2,1)} fusion(f32[8,256,256]{2,1,0:T(8,128)S(1)} %get-tuple-element.67, bf16[8,256,256]{2,1,0:T(8,128)(2,1)} %collective-permute-done.17), kind=kLoop, calls=%fused_computation.8 | loop fusion | flops 1572864 | bytes 4194304 | tf_op jit(solution)/shard_map/convert_element_type | solution.py:206
  198.3 3.5 %reduce-scatter.2.cloned.1.call-done = bf16[512,256]{1,0:T(8,128)(2,1)} async-done(((bf16[512,4096]{1,0:T(8,128)(2,1)}), bf16[512,256]{1,0:T(8,128)(2,1)}) %reduce-scatter.2.cloned.1.call-update) | async-done | bytes 262160 | tf_op jit(solution)/shard_map/reduce_scatter | solution.py:177
  203.7 2.6 %copy.34 = bf16[8,2,128,512]{3,2,1,0:T(8,128)(2,1)} copy(bf16[8,2,128,512]{2,3,0,1:T(8,128)(2,1)S(1)} %pad_maximum_fusion.2) | data formatting | bytes 4194304 | tf_op jit(solution)/shard_map/stack | solution.py:219
  206.3 6.2 %convolution_convert_fusion.3 = bf16[1024,512]{1,0:T(8,128)(2,1)} fusion(bf16[2048,1024]{1,0:T(8,128)(2,1)} %all-gather.2.cloned.1.call-done, bf16[2048,512]{1,0:T(8,128)(2,1)} %bitcast.48), kind=kOutput, calls=%fused_computation.15 | convolution fusion | flops 2148007936 | bytes 7340032 | tf_op jit(solution)/shard_map/dot_general | solution.py:20
  212.5 3.7 %all-to-all-start.6 = ((bf16[8,256,256]{2,1,0:T(8,128)(2,1)}), bf16[8,256,256]{2,1,0:T(8,128)(2,1)S(1)}, u32[]{:S(2)}, u32[]{:S(2)}) async-start(bf16[8,256,256]{2,1,0:T(8,128)(2,1)} %add_convert_fusion.1), calls=%async_computation.7 | async-start | bytes 2097152 | tf_op jit(solution)/shard_map/all_to_all | solution.py:58
  216.3 2.4 %fusion.31 = f32[512,512]{1,0:T(8,128)S(1)} fusion(bf16[1024,512]{1,0:T(8,128)(2,1)} %bitcast.51, bf16[1024,512]{1,0:T(8,128)(2,1)} %bitcast.50), kind=kOutput, calls=%fused_computation.89 | convolution fusion | flops 536870912 | bytes 3145728 | tf_op jit(solution)/shard_map/dot_general | solution.py:20
  225.2 4.1 %add_convert_fusion = bf16[512,1024]{1,0:T(8,128)(2,1)} fusion(bf16[512,1024]{1,0:T(8,128)(2,1)} %collective-permute-done.16, bf16[1024,1024]{1,0:T(8,128)(2,1)} %constant_dynamic-update-slice_fusion.5, bf16[768,512]{1,0:T(8,128)(2,1)S(1)} %copy-done.8, bf16[256,512]{1,0:T(8,128)(2,1)S(1)} %copy-done.13), kind=kOutput, calls=%fused_computation.7 | convolution fusion | flops 1077411840 | bytes 5242880 | tf_op jit(solution)/shard_map/dot_general | solution.py:20
  229.3 2.0 all-to-all-done.6
  (122 shorter events, 49.8 us)
Async XLA Ops:
  7.2 83.6 %all-gather.2.cloned.1.call-start = ((), (), s32[]{:S(2)}) async-start(), calls=%async_computation.8 | async-start | bytes 4718592 | tf_op jit(solution)/shard_map/all_gather | solution.py:142
  9.4 18.5 %copy-start.7 = (bf16[512,256]{1,0:T(8,128)(2,1)S(1)}, bf16[512,256]{1,0:T(8,128)(2,1)}, u32[]{:S(2)}) copy-start(bf16[512,256]{1,0:T(8,128)(2,1)} %param.12) | copy-start | bytes 786436
  9.4 10.0 %collective-permute-start = (bf16[512,256]{1,0:T(8,128)(2,1)}, bf16[512,256]{1,0:T(8,128)(2,1)}, u32[]{:S(2)}, u32[]{:S(2)}) collective-permute-start(bf16[512,256]{1,0:T(8,128)(2,1)} %param.12), channel_id=1, source_target_pairs={{0,16},{16,0},{1,17},{17,1},{2,18},{18,2},{3,19},{19,3},{4,20},{20... | collective-permute-start | bytes 786440 | tf_op jit(solution)/shard_map/ppermute | solution.py:54
  21.5 33.8 %all-to-all-start = ((bf16[8,128,512]{1,2,0:T(8,128)(2,1)}), bf16[8,128,512]{1,2,0:T(8,128)(2,1)S(1)}, u32[]{:S(2)}, u32[]{:S(2)}) async-start(bf16[8,128,512]{1,2,0:T(8,128)(2,1)} %broadcast_in_dim.6), calls=%async_computation | async-start | bytes 2097152 | tf_op jit(solution)/shard_map/all_to_all | solution.py:58
  29.7 29.2 %collective-permute-start.3 = (bf16[2,512,256]{2,1,0:T(8,128)(2,1)}, bf16[2,512,256]{2,1,0:T(8,128)(2,1)}, u32[]{:S(2)}, u32[]{:S(2)}) collective-permute-start(bf16[2,512,256]{2,1,0:T(8,128)(2,1)} %pad_maximum_fusion.8), channel_id=1, source_target_pairs={{0,96},{32,64},{64,32},{96,0},{1,97},{33,65},{65,33},{97,1},{2,98}... | collective-permute-start | bytes 1572872 | tf_op jit(solution)/shard_map/ppermute | solution.py:54
  32.5 25.3 %collective-permute-start.2 = (bf16[2,512,256]{2,1,0:T(8,128)(2,1)}, bf16[2,512,256]{2,1,0:T(8,128)(2,1)}, u32[]{:S(2)}, u32[]{:S(2)}) collective-permute-start(bf16[2,512,256]{2,1,0:T(8,128)(2,1)} %pad_maximum_fusion.8), channel_id=1, source_target_pairs={{0,64},{32,96},{64,0},{96,32},{1,65},{33,97},{65,1},{97,33},{2,66}... | collective-permute-start | bytes 1572872 | tf_op jit(solution)/shard_map/ppermute | solution.py:54
  33.3 23.4 %collective-permute-start.1 = (bf16[2,512,256]{2,1,0:T(8,128)(2,1)}, bf16[2,512,256]{2,1,0:T(8,128)(2,1)}, u32[]{:S(2)}, u32[]{:S(2)}) collective-permute-start(bf16[2,512,256]{2,1,0:T(8,128)(2,1)} %pad_maximum_fusion.8), channel_id=1, source_target_pairs={{0,32},{32,0},{64,96},{96,64},{1,33},{33,1},{65,97},{97,65},{2,34}... | collective-permute-start | bytes 1572872 | tf_op jit(solution)/shard_map/ppermute | solution.py:54
  33.8 26.2 %collective-permute-start.5 = (bf16[256,512]{1,0:T(8,128)(2,1)}, bf16[256,512]{1,0:T(8,128)(2,1)S(1)}, u32[]{:S(2)}, u32[]{:S(2)}) collective-permute-start(bf16[256,512]{1,0:T(8,128)(2,1)} %param.11), channel_id=1, source_target_pairs={{0,8},{8,0},{1,9},{9,1},{2,10},{10,2},{3,11},{11,3},{4,12},{12,4},... | collective-permute-start | bytes 786440 | tf_op jit(solution)/shard_map/ppermute | solution.py:54
  55.6 4.4 %collective-permute-start.4 = (bf16[8,128,256]{1,2,0:T(8,128)(2,1)S(1)}, bf16[8,128,256]{1,2,0:T(8,128)(2,1)S(1)}, u32[]{:S(2)}, u32[]{:S(2)}) collective-permute-start(bf16[8,128,256]{1,2,0:T(8,128)(2,1)S(1)} %get-tuple-element.100), channel_id=1, source_target_pairs={{0,8},{8,0},{1,9},{9,1},{2,10},{10,2},{3,11},{11,3},{4,12},{12,4},... | collective-permute-start | bytes 1572872 | tf_op jit(solution)/shard_map/ppermute | solution.py:54
  60.9 1.7 collective-permute-start.6
  64.5 26.2 %all-to-all-start.1 = ((bf16[8,128,512]{2,1,0:T(8,128)(2,1)}), bf16[8,128,512]{2,1,0:T(8,128)(2,1)S(1)}, u32[]{:S(2)}, u32[]{:S(2)}) async-start(bf16[8,128,512]{2,1,0:T(8,128)(2,1)} %broadcast_in_dim.7), calls=%async_computation.1 | async-start | bytes 2097152 | tf_op jit(solution)/shard_map/all_to_all | solution.py:58
  74.5 0.8 collective-permute-start.7
  92.5 21.9 %all-to-all-start.2 = ((bf16[8,128,512]{2,1,0:T(8,128)(2,1)}), bf16[8,128,512]{2,1,0:T(8,128)(2,1)S(1)}, u32[]{:S(2)}, u32[]{:S(2)}) async-start(bf16[8,128,512]{2,1,0:T(8,128)(2,1)} %bitcast.7), calls=%async_computation.2 | async-start | bytes 2097152 | tf_op jit(solution)/shard_map/all_to_all | solution.py:58
  99.9 101.9 %reduce-scatter.2.cloned.1.call-start = ((), (), s32[]{:S(2)}) async-start(), calls=%async_computation.9 | async-start | bytes 4456448 | tf_op jit(solution)/shard_map/reduce_scatter | solution.py:177
  115.8 10.1 %copy-start.5 = (bf16[128,4096]{1,0:T(8,128)(2,1)S(1)}, bf16[128,4096]{1,0:T(8,128)(2,1)}, u32[]{:S(2)}) copy-start(bf16[128,4096]{1,0:T(8,128)(2,1)} %param.15) | copy-start | bytes 3145732
  115.8 21.1 %all-to-all-start.3 = ((bf16[8,128,512]{1,2,0:T(8,128)(2,1)}), bf16[8,128,512]{1,2,0:T(8,128)(2,1)}, u32[]{:S(2)}, u32[]{:S(2)}) async-start(bf16[8,128,512]{1,2,0:T(8,128)(2,1)} %broadcast_in_dim.8), calls=%async_computation.3 | async-start | bytes 2097152 | tf_op jit(solution)/shard_map/all_to_all | solution.py:58
  121.7 14.5 %collective-permute-start.10 = (bf16[256,512]{1,0:T(8,128)(2,1)S(1)}, bf16[256,512]{1,0:T(8,128)(2,1)S(1)}, u32[]{:S(2)}, u32[]{:S(2)}) collective-permute-start(bf16[256,512]{1,0:T(8,128)(2,1)S(1)} %get-tuple-element.94), channel_id=1, source_target_pairs={{0,3},{1,2},{2,1},{3,0},{4,7},{5,6},{6,5},{7,4},{8,11},{9,10},{10,... | collective-permute-start | bytes 786440 | tf_op jit(solution)/shard_map/ppermute | solution.py:54
  123.3 13.0 %collective-permute-start.9 = (bf16[256,512]{1,0:T(8,128)(2,1)S(1)}, bf16[256,512]{1,0:T(8,128)(2,1)S(1)}, u32[]{:S(2)}, u32[]{:S(2)}) collective-permute-start(bf16[256,512]{1,0:T(8,128)(2,1)S(1)} %get-tuple-element.95), channel_id=1, source_target_pairs={{0,2},{1,3},{2,0},{3,1},{4,6},{5,7},{6,4},{7,5},{8,10},{9,11},{10,... | collective-permute-start | bytes 786440 | tf_op jit(solution)/shard_map/ppermute | solution.py:54
  124.7 12.2 %collective-permute-start.8 = (bf16[256,512]{1,0:T(8,128)(2,1)S(1)}, bf16[256,512]{1,0:T(8,128)(2,1)S(1)}, u32[]{:S(2)}, u32[]{:S(2)}) collective-permute-start(bf16[256,512]{1,0:T(8,128)(2,1)S(1)} %get-tuple-element.96), channel_id=1, source_target_pairs={{0,1},{1,0},{2,3},{3,2},{4,5},{5,4},{6,7},{7,6},{8,9},{9,8},{10,11... | collective-permute-start | bytes 786440 | tf_op jit(solution)/shard_map/ppermute | solution.py:54
  139.1 5.6 %collective-permute-start.11 = (bf16[128,4096]{1,0:T(8,128)(2,1)S(1)}, bf16[128,4096]{1,0:T(8,128)(2,1)S(1)}, u32[]{:S(2)}, u32[]{:S(2)}) collective-permute-start(bf16[128,4096]{1,0:T(8,128)(2,1)S(1)} %copy.32), channel_id=1, source_target_pairs={{0,8},{8,0},{1,9},{9,1},{2,10},{10,2},{3,11},{11,3},{4,12},{12,4},... | collective-permute-start | bytes 3145736 | tf_op jit(solution)/shard_map/ppermute | solution.py:54
  139.2 28.6 %all-to-all-start.4 = ((bf16[8,128,512]{1,2,0:T(8,128)(2,1)}), bf16[8,128,512]{1,2,0:T(8,128)(2,1)}, u32[]{:S(2)}, u32[]{:S(2)}) async-start(bf16[8,128,512]{1,2,0:T(8,128)(2,1)} %all-to-all-done.3), calls=%async_computation.4 | async-start | bytes 2097152 | tf_op jit(solution)/shard_map/all_to_all | solution.py:58
  144.8 6.8 %copy-start.1 = (bf16[128,4096]{1,0:T(8,128)(2,1)}, bf16[128,4096]{1,0:T(8,128)(2,1)S(1)}, u32[]{:S(2)}) copy-start(bf16[128,4096]{1,0:T(8,128)(2,1)S(1)} %get-tuple-element.92) | copy-start | bytes 3145732
  151.7 23.4 %collective-permute-start.13 = (bf16[256,1024]{1,0:T(8,128)(2,1)S(1)}, bf16[256,1024]{1,0:T(8,128)(2,1)}, u32[]{:S(2)}, u32[]{:S(2)}) collective-permute-start(bf16[256,1024]{1,0:T(8,128)(2,1)S(1)} %fusion.2.grad_ref), channel_id=1, source_target_pairs={{0,1},{1,0},{2,3},{3,2},{4,5},{5,4},{6,7},{7,6},{8,9},{9,8},{10,11... | collective-permute-start | bytes 1572872 | tf_op jit(solution)/shard_map/ppermute | solution.py:54
  153.5 30.7 %collective-permute-start.14 = (bf16[256,1024]{1,0:T(8,128)(2,1)S(1)}, bf16[256,1024]{1,0:T(8,128)(2,1)}, u32[]{:S(2)}, u32[]{:S(2)}) collective-permute-start(bf16[256,1024]{1,0:T(8,128)(2,1)S(1)} %fusion.2.grad_ref), channel_id=1, source_target_pairs={{0,2},{1,3},{2,0},{3,1},{4,6},{5,7},{6,4},{7,5},{8,10},{9,11},{10,... | collective-permute-start | bytes 1572872 | tf_op jit(solution)/shard_map/ppermute | solution.py:54
  156.1 31.9 %collective-permute-start.12 = (bf16[768,512]{1,0:T(8,128)(2,1)S(1)}, bf16[768,512]{1,0:T(8,128)(2,1)}, u32[]{:S(2)}, u32[]{:S(2)}) collective-permute-start(bf16[768,512]{1,0:T(8,128)(2,1)S(1)} %pad_maximum_fusion.7), channel_id=1, source_target_pairs={{0,8},{8,0},{1,9},{9,1},{2,10},{10,2},{3,11},{11,3},{4,12},{12,4},... | collective-permute-start | bytes 2359304 | tf_op jit(solution)/shard_map/ppermute | solution.py:54
  158.0 28.1 %collective-permute-start.15 = (bf16[256,1024]{1,0:T(8,128)(2,1)S(1)}, bf16[256,1024]{1,0:T(8,128)(2,1)}, u32[]{:S(2)}, u32[]{:S(2)}) collective-permute-start(bf16[256,1024]{1,0:T(8,128)(2,1)S(1)} %fusion.2.grad_ref), channel_id=1, source_target_pairs={{0,3},{1,2},{2,1},{3,0},{4,7},{5,6},{6,5},{7,4},{8,11},{9,10},{10,... | collective-permute-start | bytes 1572872 | tf_op jit(solution)/shard_map/ppermute | solution.py:54
  166.7 29.2 %collective-permute-start.17 = (bf16[8,256,256]{2,1,0:T(8,128)(2,1)}, bf16[8,256,256]{2,1,0:T(8,128)(2,1)}, u32[]{:S(2)}, u32[]{:S(2)}) collective-permute-start(bf16[8,256,256]{2,1,0:T(8,128)(2,1)} %get-tuple-element.70), channel_id=1, source_target_pairs={{0,8},{8,0},{1,9},{9,1},{2,10},{10,2},{3,11},{11,3},{4,12},{12,4},... | collective-permute-start | bytes 3145736 | tf_op jit(solution)/shard_map/ppermute | solution.py:54
  167.8 25.8 %all-to-all-start.5 = ((bf16[8,128,512]{1,2,0:T(8,128)(2,1)}), bf16[8,128,512]{1,2,0:T(8,128)(2,1)}, u32[]{:S(2)}, u32[]{:S(2)}) async-start(bf16[8,128,512]{1,2,0:T(8,128)(2,1)} %bitcast.47), calls=%async_computation.6 | async-start | bytes 2097152 | tf_op jit(solution)/shard_map/all_to_all | solution.py:58
  175.1 23.2 %collective-permute-start.18 = (bf16[8,128,512]{1,2,0:T(8,128)(2,1)}, bf16[8,128,512]{1,2,0:T(8,128)(2,1)}, u32[]{:S(2)}, u32[]{:S(2)}) collective-permute-start(bf16[8,128,512]{1,2,0:T(8,128)(2,1)} %all-to-all-done.4), channel_id=1, source_target_pairs={{0,8},{8,0},{1,9},{9,1},{2,10},{10,2},{3,11},{11,3},{4,12},{12,4},... | collective-permute-start | bytes 3145736 | tf_op jit(solution)/shard_map/ppermute | solution.py:54
  192.6 32.7 %collective-permute-start.16 = (bf16[512,1024]{1,0:T(8,128)(2,1)}, bf16[512,1024]{1,0:T(8,128)(2,1)}, u32[]{:S(2)}, u32[]{:S(2)}) collective-permute-start(bf16[512,1024]{1,0:T(8,128)(2,1)} %convolution_convert_fusion.1), channel_id=1, source_target_pairs={{0,4},{4,0},{1,5},{5,1},{2,6},{6,2},{3,7},{7,3},{8,12},{12,8},{9,1... | collective-permute-start | bytes 3145736 | tf_op jit(solution)/shard_map/ppermute | solution.py:54
  212.5 18.8 %all-to-all-start.6 = ((bf16[8,256,256]{2,1,0:T(8,128)(2,1)}), bf16[8,256,256]{2,1,0:T(8,128)(2,1)S(1)}, u32[]{:S(2)}, u32[]{:S(2)}) async-start(bf16[8,256,256]{2,1,0:T(8,128)(2,1)} %add_convert_fusion.1), calls=%async_computation.7 | async-start | bytes 2097152 | tf_op jit(solution)/shard_map/all_to_all | solution.py:58
  220.4 1.9 collective-permute-start.19
  (16 other events, 52.8 us)
Sparse Core Ops, SparseCore 0:
  9.6 73.8 all-gather.1
  105.3 96.4 reduce-scatter.1

commit v6 on v5

--- a/solution.py
+++ b/solution.py
@@ -85,7 +85,7 @@
     )
     first, second = part[:, :half], part[:, half:]
     even = core_ref[0] == 0
-    keep_ref[0] = jnp.where(even, first, second)
+    keep_ref[0] = jnp.where(even, first, second).astype(BF16)
     send_ref[0] = jnp.where(even, second, first).astype(BF16)
 
 
@@ -105,7 +105,7 @@
             ],
             out_specs=[block, block],
         ),
-        out_shape=[jax.ShapeDtypeStruct(shape, F32), jax.ShapeDtypeStruct(shape, BF16)],
+        out_shape=[jax.ShapeDtypeStruct(shape, BF16)] * 2,
         cost_estimate=pl.CostEstimate(
             flops=4 * count * rows * half * depth,
             bytes_accessed=4 * count * half * depth,
@@ -203,7 +203,7 @@
     grad_rows = z_rows(wide_pre_grad)
     term_keep, term_send = term_blocks(wide_pre_grad, wide_up, core, half)
     term_send, in_blocks = gate(term_send, in_blocks)
-    term_chip = (term_keep + flip(term_send, "c").astype(F32)).astype(BF16)
+    term_chip = (term_keep.astype(F32) + flip(term_send, "c").astype(F32)).astype(BF16)
     in_own = exchange(in_blocks, CHIPS).reshape(n_d * tokens, side)
     term_chip, bound_other, narrow_down_grad = gate(term_chip, flip(bound, "c"), narrow_down_grad)
     term_all = exchange(term_chip, CHIPS)

time: 240 us -> 240 us (level)
  no operation moved by 1% of the time
where the time goes in v6:
time: 240 us; the launch traced here: 239 us
  waiting for transfers between devices  84.8 us (35%)
  starting transfers between devices  60.7 us (25%)
  local copies, waits for them, and re-layouts  33 us (14%)
  matrix products  27.6 us (12%)
  other arithmetic  14.5 us (6%)
  between operations  14.5 us (6%)
  Pallas kernels  3.85 us (2%)
    all_to_all x7, waiting for transfers between devices, exchange(): return lax.all_to_all(value, axes, 0, 0, tiled=True)  52.5 us
    all_to_all x7, starting transfers between devices, exchange(): return lax.all_to_all(value, axes, 0, 0, tiled=True)  41.4 us
    ppermute x19, waiting for transfers between devices, flip(): return lax.ppermute(value, axis, [(i, i ^ by) for i in range(size)])  29 us
    dot_general x7, matrix products, dot(): lax.dot_general(left, right, (dims, ((), ())), preferred_element_type=F32)  25.9 us
    ppermute x19, starting transfers between devices, flip(): return lax.ppermute(value, axis, [(i, i ^ by) for i in range(size)])  18.6 us
    unnamed x53, local copies, waits for them, and re-layouts  15.2 us
  transfers between devices with their start and end apart: 29, of which 12 were waited for; matrix products, arithmetic and copies ran while one was open for 27% of the time, Pallas kernels for 2%

profile of v6, /device:TPU:0, one launch (start us, length us, event | category | flops | bytes accessed | tf_op | source)
XLA Modules:
  0.0 238.9 jit_solution(18415098545216354752)
XLA Ops:
  7.2 2.2 fusion.9
  9.4 3.4 %collective-permute-start = (bf16[512,256]{1,0:T(8,128)(2,1)}, bf16[512,256]{1,0:T(8,128)(2,1)}, u32[]{:S(2)}, u32[]{:S(2)}) collective-permute-start(bf16[512,256]{1,0:T(8,128)(2,1)} %param.12), channel_id=1, source_target_pairs={{0,16},{16,0},{1,17},{17,1},{2,18},{18,2},{3,19},{19,3},{4,20},{20... | collective-permute-start | bytes 786440 | tf_op jit(solution)/shard_map/ppermute | solution.py:54
  12.7 6.6 %collective-permute-done = bf16[512,256]{1,0:T(8,128)(2,1)} collective-permute-done((bf16[512,256]{1,0:T(8,128)(2,1)}, bf16[512,256]{1,0:T(8,128)(2,1)}, u32[]{:S(2)}, u32[]{:S(2)}) %collective-permute-start) | collective-permute-done | bytes 262176 | tf_op jit(solution)/shard_map/ppermute | solution.py:54
  21.5 6.4 %all-to-all-start = ((bf16[8,128,512]{1,2,0:T(8,128)(2,1)}), bf16[8,128,512]{1,2,0:T(8,128)(2,1)S(1)}, u32[]{:S(2)}, u32[]{:S(2)}) async-start(bf16[8,128,512]{1,2,0:T(8,128)(2,1)} %broadcast_in_dim.6), calls=%async_computation | async-start | bytes 2097152 | tf_op jit(solution)/shard_map/all_to_all | solution.py:58
  29.7 2.8 %collective-permute-start.3 = (bf16[2,512,256]{2,1,0:T(8,128)(2,1)}, bf16[2,512,256]{2,1,0:T(8,128)(2,1)}, u32[]{:S(2)}, u32[]{:S(2)}) collective-permute-start(bf16[2,512,256]{2,1,0:T(8,128)(2,1)} %pad_maximum_fusion.8), channel_id=1, source_target_pairs={{0,96},{32,64},{64,32},{96,0},{1,97},{33,65},{65,33},{97,1},{2,98}... | collective-permute-start | bytes 1572872 | tf_op jit(solution)/shard_map/ppermute | solution.py:54
  33.8 21.5 %all-to-all-done = bf16[8,128,512]{1,2,0:T(8,128)(2,1)S(1)} async-done(((bf16[8,128,512]{1,2,0:T(8,128)(2,1)}), bf16[8,128,512]{1,2,0:T(8,128)(2,1)S(1)}, u32[]{:S(2)}, u32[]{:S(2)}) %all-to-all-start) | async-done | bytes 1048608 | tf_op jit(solution)/shard_map/all_to_all | solution.py:58
  64.5 6.6 %all-to-all-start.1 = ((bf16[8,128,512]{2,1,0:T(8,128)(2,1)}), bf16[8,128,512]{2,1,0:T(8,128)(2,1)S(1)}, u32[]{:S(2)}, u32[]{:S(2)}) async-start(bf16[8,128,512]{2,1,0:T(8,128)(2,1)} %broadcast_in_dim.7), calls=%async_computation.1 | async-start | bytes 2097152 | tf_op jit(solution)/shard_map/all_to_all | solution.py:58
  71.2 3.3 %convolution_convert_fusion = bf16[512,4096]{1,0:T(8,128)(2,1)} fusion(bf16[128,4096]{0,1:T(8,128)(2,1)S(1)} %bitcast.46, bf16[128,512]{1,0:T(8,128)(2,1)S(1)} %copy-done.12), kind=kOutput, calls=%fused_computation | convolution fusion | flops 539361280 | bytes 5373952 | tf_op jit(solution)/shard_map/dot_general | solution.py:20
  75.3 15.5 %all-to-all-done.1 = bf16[8,128,512]{2,1,0:T(8,128)(2,1)S(1)} async-done(((bf16[8,128,512]{2,1,0:T(8,128)(2,1)}), bf16[8,128,512]{2,1,0:T(8,128)(2,1)S(1)}, u32[]{:S(2)}, u32[]{:S(2)}) %all-to-all-start.1) | async-done | bytes 1048608 | tf_op jit(solution)/shard_map/all_to_all | solution.py:58
  92.5 7.4 %all-to-all-start.2 = ((bf16[8,128,512]{2,1,0:T(8,128)(2,1)}), bf16[8,128,512]{2,1,0:T(8,128)(2,1)S(1)}, u32[]{:S(2)}, u32[]{:S(2)}) async-start(bf16[8,128,512]{2,1,0:T(8,128)(2,1)} %bitcast.7), calls=%async_computation.2 | async-start | bytes 2097152 | tf_op jit(solution)/shard_map/all_to_all | solution.py:58
  100.6 13.8 %all-to-all-done.2 = bf16[8,128,512]{2,1,0:T(8,128)(2,1)S(1)} async-done(((bf16[8,128,512]{2,1,0:T(8,128)(2,1)}), bf16[8,128,512]{2,1,0:T(8,128)(2,1)S(1)}, u32[]{:S(2)}, u32[]{:S(2)}) %all-to-all-start.2) | async-done | bytes 1048608 | tf_op jit(solution)/shard_map/all_to_all | solution.py:58
  115.8 4.7 %all-to-all-start.3 = ((bf16[8,128,512]{1,2,0:T(8,128)(2,1)}), bf16[8,128,512]{1,2,0:T(8,128)(2,1)}, u32[]{:S(2)}, u32[]{:S(2)}) async-start(bf16[8,128,512]{1,2,0:T(8,128)(2,1)} %broadcast_in_dim.8), calls=%async_computation.3 | async-start | bytes 2097152 | tf_op jit(solution)/shard_map/all_to_all | solution.py:58
  127.2 9.1 %collective-permute-done.10 = bf16[256,512]{1,0:T(8,128)(2,1)S(1)} collective-permute-done((bf16[256,512]{1,0:T(8,128)(2,1)S(1)}, bf16[256,512]{1,0:T(8,128)(2,1)S(1)}, u32[]{:S(2)}, u32[]{:S(2)}) %collective-permute-start.10) | collective-permute-done | bytes 262176 | tf_op jit(solution)/shard_map/ppermute | solution.py:54
  139.2 4.4 %all-to-all-start.4 = ((bf16[8,128,512]{1,2,0:T(8,128)(2,1)}), bf16[8,128,512]{1,2,0:T(8,128)(2,1)}, u32[]{:S(2)}, u32[]{:S(2)}) async-start(bf16[8,128,512]{1,2,0:T(8,128)(2,1)} %all-to-all-done.3), calls=%async_computation.4 | async-start | bytes 2097152 | tf_op jit(solution)/shard_map/all_to_all | solution.py:58
  145.7 6.0 %fusion.2.grad_ref = bf16[256,1024]{1,0:T(8,128)(2,1)S(1)} fusion(bf16[1024,4096]{1,0:T(8,128)(2,1)} %param.10, bf16[128,4096]{1,0:T(8,128)(2,1)S(1)} %get-tuple-element.93, bf16[128,4096]{1,0:T(8,128)(2,1)S(1)} %get-tuple-element.92, bf16[256,1024]{1,0:T(8,128)(2,1)S(1)} %copy-done.11), kind=kOutput, calls=%fused_computation.17 | convolution fusion | flops 2154299392 | bytes 11534336 | tf_op jit(solution)/shard_map/dot_general | solution.py:20
  153.5 2.7 %collective-permute-start.14 = (bf16[256,1024]{1,0:T(8,128)(2,1)S(1)}, bf16[256,1024]{1,0:T(8,128)(2,1)}, u32[]{:S(2)}, u32[]{:S(2)}) collective-permute-start(bf16[256,1024]{1,0:T(8,128)(2,1)S(1)} %fusion.2.grad_ref), channel_id=1, source_target_pairs={{0,2},{1,3},{2,0},{3,1},{4,6},{5,7},{6,4},{7,5},{8,10},{9,11},{10,... | collective-permute-start | bytes 1572872 | tf_op jit(solution)/shard_map/ppermute | solution.py:54
  158.3 3.4 %copy-done = bf16[4096,1024]{1,0:T(8,128)(2,1)S(1)} copy-done((bf16[4096,1024]{1,0:T(8,128)(2,1)S(1)}, bf16[4096,1024]{1,0:T(8,128)(2,1)}, u32[]{:S(2)}) %copy-start) | copy-done | bytes 8388632
  161.7 3.8 %term.1 = (bf16[8,256,256]{2,1,0:T(8,128)(2,1)S(1)}, bf16[8,256,256]{2,1,0:T(8,128)(2,1)S(1)}) custom-call(s32[1]{0:T(128)} %bitcast.12.core_ref, bf16[256,1024]{1,0:T(8,128)(2,1)S(1)} %fusion.2.grad_ref, bf16[4096,1024]{1,0:T(8,128)(2,1)S(1)} %copy-done), custom_call_target="tpu_custom_call" | custom-call | flops 2147483648 | bytes 8388608 | tf_op jit(solution)/shard_map/term/pallas_call | solution.py:97
  166.7 7.3 %all-to-all-start.5 = ((bf16[8,128,512]{1,2,0:T(8,128)(2,1)}), bf16[8,128,512]{1,2,0:T(8,128)(2,1)}, u32[]{:S(2)}, u32[]{:S(2)}) async-start(bf16[8,128,512]{1,2,0:T(8,128)(2,1)} %bitcast.47), calls=%async_computation.6 | async-start | bytes 2097152 | tf_op jit(solution)/shard_map/all_to_all | solution.py:58
  176.0 8.1 %collective-permute-done.14 = bf16[256,1024]{1,0:T(8,128)(2,1)} collective-permute-done((bf16[256,1024]{1,0:T(8,128)(2,1)S(1)}, bf16[256,1024]{1,0:T(8,128)(2,1)}, u32[]{:S(2)}, u32[]{:S(2)}) %collective-permute-start.14) | collective-permute-done | bytes 524320 | tf_op jit(solution)/shard_map/ppermute | solution.py:54
  184.1 1.9 constant_dynamic-update-slice_fusion.6
  186.1 1.9 constant_dynamic-update-slice_fusion.5
  188.0 2.3 broadcast_select_fusion.3
  190.3 2.2 convolution_convert_fusion.1
  193.6 2.3 copy.35
  195.9 2.5 %add_convert_fusion.1 = bf16[8,256,256]{2,1,0:T(8,128)(2,1)} fusion(bf16[8,256,256]{2,1,0:T(8,128)(2,1)} %collective-permute-done.17, bf16[8,256,256]{2,1,0:T(8,128)(2,1)S(1)} %get-tuple-element.67), kind=kLoop, calls=%fused_computation.8 | loop fusion | flops 2097152 | bytes 3145728 | tf_op jit(solution)/shard_map/convert_element_type | solution.py:206
  198.3 2.5 %reduce-scatter.2.cloned.1.call-done = bf16[512,256]{1,0:T(8,128)(2,1)} async-done(((bf16[512,4096]{1,0:T(8,128)(2,1)}), bf16[512,256]{1,0:T(8,128)(2,1)}) %reduce-scatter.2.cloned.1.call-update) | async-done | bytes 262160 | tf_op jit(solution)/shard_map/reduce_scatter | solution.py:177
  202.7 2.6 %copy.34 = bf16[8,2,128,512]{3,2,1,0:T(8,128)(2,1)} copy(bf16[8,2,128,512]{2,3,0,1:T(8,128)(2,1)S(1)} %pad_maximum_fusion.2) | data formatting | bytes 4194304 | tf_op jit(solution)/shard_map/stack | solution.py:219
  205.3 6.2 %convolution_convert_fusion.3 = bf16[1024,512]{1,0:T(8,128)(2,1)} fusion(bf16[2048,1024]{1,0:T(8,128)(2,1)} %all-gather.2.cloned.1.call-done, bf16[2048,512]{1,0:T(8,128)(2,1)} %bitcast.48), kind=kOutput, calls=%fused_computation.15 | convolution fusion | flops 2148007936 | bytes 7340032 | tf_op jit(solution)/shard_map/dot_general | solution.py:20
  211.5 4.5 %all-to-all-start.6 = ((bf16[8,256,256]{2,1,0:T(8,128)(2,1)}), bf16[8,256,256]{2,1,0:T(8,128)(2,1)S(1)}, u32[]{:S(2)}, u32[]{:S(2)}) async-start(bf16[8,256,256]{2,1,0:T(8,128)(2,1)} %add_convert_fusion.1), calls=%async_computation.7 | async-start | bytes 2097152 | tf_op jit(solution)/shard_map/all_to_all | solution.py:58
  216.0 2.4 %fusion.31 = f32[512,512]{1,0:T(8,128)S(1)} fusion(bf16[1024,512]{1,0:T(8,128)(2,1)} %bitcast.51, bf16[1024,512]{1,0:T(8,128)(2,1)} %bitcast.50), kind=kOutput, calls=%fused_computation.89 | convolution fusion | flops 536870912 | bytes 3145728 | tf_op jit(solution)/shard_map/dot_general | solution.py:20
  225.4 4.1 %add_convert_fusion = bf16[512,1024]{1,0:T(8,128)(2,1)} fusion(bf16[512,1024]{1,0:T(8,128)(2,1)} %collective-permute-done.16, bf16[1024,1024]{1,0:T(8,128)(2,1)} %constant_dynamic-update-slice_fusion.5, bf16[768,512]{1,0:T(8,128)(2,1)S(1)} %copy-done.8, bf16[256,512]{1,0:T(8,128)(2,1)S(1)} %copy-done.13), kind=kOutput, calls=%fused_computation.7 | convolution fusion | flops 1077411840 | bytes 5242880 | tf_op jit(solution)/shard_map/dot_general | solution.py:20
  (122 shorter events, 50.1 us)
Async XLA Ops:
  7.2 83.6 %all-gather.2.cloned.1.call-start = ((), (), s32[]{:S(2)}) async-start(), calls=%async_computation.8 | async-start | bytes 4718592 | tf_op jit(solution)/shard_map/all_gather | solution.py:142
  9.4 18.5 %copy-start.7 = (bf16[512,256]{1,0:T(8,128)(2,1)S(1)}, bf16[512,256]{1,0:T(8,128)(2,1)}, u32[]{:S(2)}) copy-start(bf16[512,256]{1,0:T(8,128)(2,1)} %param.12) | copy-start | bytes 786436
  9.4 10.0 %collective-permute-start = (bf16[512,256]{1,0:T(8,128)(2,1)}, bf16[512,256]{1,0:T(8,128)(2,1)}, u32[]{:S(2)}, u32[]{:S(2)}) collective-permute-start(bf16[512,256]{1,0:T(8,128)(2,1)} %param.12), channel_id=1, source_target_pairs={{0,16},{16,0},{1,17},{17,1},{2,18},{18,2},{3,19},{19,3},{4,20},{20... | collective-permute-start | bytes 786440 | tf_op jit(solution)/shard_map/ppermute | solution.py:54
  21.5 33.8 %all-to-all-start = ((bf16[8,128,512]{1,2,0:T(8,128)(2,1)}), bf16[8,128,512]{1,2,0:T(8,128)(2,1)S(1)}, u32[]{:S(2)}, u32[]{:S(2)}) async-start(bf16[8,128,512]{1,2,0:T(8,128)(2,1)} %broadcast_in_dim.6), calls=%async_computation | async-start | bytes 2097152 | tf_op jit(solution)/shard_map/all_to_all | solution.py:58
  29.7 29.2 %collective-permute-start.3 = (bf16[2,512,256]{2,1,0:T(8,128)(2,1)}, bf16[2,512,256]{2,1,0:T(8,128)(2,1)}, u32[]{:S(2)}, u32[]{:S(2)}) collective-permute-start(bf16[2,512,256]{2,1,0:T(8,128)(2,1)} %pad_maximum_fusion.8), channel_id=1, source_target_pairs={{0,96},{32,64},{64,32},{96,0},{1,97},{33,65},{65,33},{97,1},{2,98}... | collective-permute-start | bytes 1572872 | tf_op jit(solution)/shard_map/ppermute | solution.py:54
  32.5 25.3 %collective-permute-start.2 = (bf16[2,512,256]{2,1,0:T(8,128)(2,1)}, bf16[2,512,256]{2,1,0:T(8,128)(2,1)}, u32[]{:S(2)}, u32[]{:S(2)}) collective-permute-start(bf16[2,512,256]{2,1,0:T(8,128)(2,1)} %pad_maximum_fusion.8), channel_id=1, source_target_pairs={{0,64},{32,96},{64,0},{96,32},{1,65},{33,97},{65,1},{97,33},{2,66}... | collective-permute-start | bytes 1572872 | tf_op jit(solution)/shard_map/ppermute | solution.py:54
  33.3 23.4 %collective-permute-start.1 = (bf16[2,512,256]{2,1,0:T(8,128)(2,1)}, bf16[2,512,256]{2,1,0:T(8,128)(2,1)}, u32[]{:S(2)}, u32[]{:S(2)}) collective-permute-start(bf16[2,512,256]{2,1,0:T(8,128)(2,1)} %pad_maximum_fusion.8), channel_id=1, source_target_pairs={{0,32},{32,0},{64,96},{96,64},{1,33},{33,1},{65,97},{97,65},{2,34}... | collective-permute-start | bytes 1572872 | tf_op jit(solution)/shard_map/ppermute | solution.py:54
  33.8 26.2 %collective-permute-start.5 = (bf16[256,512]{1,0:T(8,128)(2,1)}, bf16[256,512]{1,0:T(8,128)(2,1)S(1)}, u32[]{:S(2)}, u32[]{:S(2)}) collective-permute-start(bf16[256,512]{1,0:T(8,128)(2,1)} %param.11), channel_id=1, source_target_pairs={{0,8},{8,0},{1,9},{9,1},{2,10},{10,2},{3,11},{11,3},{4,12},{12,4},... | collective-permute-start | bytes 786440 | tf_op jit(solution)/shard_map/ppermute | solution.py:54
  55.6 4.4 %collective-permute-start.4 = (bf16[8,128,256]{1,2,0:T(8,128)(2,1)S(1)}, bf16[8,128,256]{1,2,0:T(8,128)(2,1)S(1)}, u32[]{:S(2)}, u32[]{:S(2)}) collective-permute-start(bf16[8,128,256]{1,2,0:T(8,128)(2,1)S(1)} %get-tuple-element.100), channel_id=1, source_target_pairs={{0,8},{8,0},{1,9},{9,1},{2,10},{10,2},{3,11},{11,3},{4,12},{12,4},... | collective-permute-start | bytes 1572872 | tf_op jit(solution)/shard_map/ppermute | solution.py:54
  60.9 1.7 collective-permute-start.6
  64.5 26.2 %all-to-all-start.1 = ((bf16[8,128,512]{2,1,0:T(8,128)(2,1)}), bf16[8,128,512]{2,1,0:T(8,128)(2,1)S(1)}, u32[]{:S(2)}, u32[]{:S(2)}) async-start(bf16[8,128,512]{2,1,0:T(8,128)(2,1)} %broadcast_in_dim.7), calls=%async_computation.1 | async-start | bytes 2097152 | tf_op jit(solution)/shard_map/all_to_all | solution.py:58
  74.5 0.8 collective-permute-start.7
  92.5 21.9 %all-to-all-start.2 = ((bf16[8,128,512]{2,1,0:T(8,128)(2,1)}), bf16[8,128,512]{2,1,0:T(8,128)(2,1)S(1)}, u32[]{:S(2)}, u32[]{:S(2)}) async-start(bf16[8,128,512]{2,1,0:T(8,128)(2,1)} %bitcast.7), calls=%async_computation.2 | async-start | bytes 2097152 | tf_op jit(solution)/shard_map/all_to_all | solution.py:58
  99.9 100.9 %reduce-scatter.2.cloned.1.call-start = ((), (), s32[]{:S(2)}) async-start(), calls=%async_computation.9 | async-start | bytes 4456448 | tf_op jit(solution)/shard_map/reduce_scatter | solution.py:177
  115.8 10.1 %copy-start.5 = (bf16[128,4096]{1,0:T(8,128)(2,1)S(1)}, bf16[128,4096]{1,0:T(8,128)(2,1)}, u32[]{:S(2)}) copy-start(bf16[128,4096]{1,0:T(8,128)(2,1)} %param.15) | copy-start | bytes 3145732
  115.8 21.1 %all-to-all-start.3 = ((bf16[8,128,512]{1,2,0:T(8,128)(2,1)}), bf16[8,128,512]{1,2,0:T(8,128)(2,1)}, u32[]{:S(2)}, u32[]{:S(2)}) async-start(bf16[8,128,512]{1,2,0:T(8,128)(2,1)} %broadcast_in_dim.8), calls=%async_computation.3 | async-start | bytes 2097152 | tf_op jit(solution)/shard_map/all_to_all | solution.py:58
  121.7 14.5 %collective-permute-start.10 = (bf16[256,512]{1,0:T(8,128)(2,1)S(1)}, bf16[256,512]{1,0:T(8,128)(2,1)S(1)}, u32[]{:S(2)}, u32[]{:S(2)}) collective-permute-start(bf16[256,512]{1,0:T(8,128)(2,1)S(1)} %get-tuple-element.94), channel_id=1, source_target_pairs={{0,3},{1,2},{2,1},{3,0},{4,7},{5,6},{6,5},{7,4},{8,11},{9,10},{10,... | collective-permute-start | bytes 786440 | tf_op jit(solution)/shard_map/ppermute | solution.py:54
  123.3 13.0 %collective-permute-start.9 = (bf16[256,512]{1,0:T(8,128)(2,1)S(1)}, bf16[256,512]{1,0:T(8,128)(2,1)S(1)}, u32[]{:S(2)}, u32[]{:S(2)}) collective-permute-start(bf16[256,512]{1,0:T(8,128)(2,1)S(1)} %get-tuple-element.95), channel_id=1, source_target_pairs={{0,2},{1,3},{2,0},{3,1},{4,6},{5,7},{6,4},{7,5},{8,10},{9,11},{10,... | collective-permute-start | bytes 786440 | tf_op jit(solution)/shard_map/ppermute | solution.py:54
  124.7 12.2 %collective-permute-start.8 = (bf16[256,512]{1,0:T(8,128)(2,1)S(1)}, bf16[256,512]{1,0:T(8,128)(2,1)S(1)}, u32[]{:S(2)}, u32[]{:S(2)}) collective-permute-start(bf16[256,512]{1,0:T(8,128)(2,1)S(1)} %get-tuple-element.96), channel_id=1, source_target_pairs={{0,1},{1,0},{2,3},{3,2},{4,5},{5,4},{6,7},{7,6},{8,9},{9,8},{10,11... | collective-permute-start | bytes 786440 | tf_op jit(solution)/shard_map/ppermute | solution.py:54
  139.1 5.6 %collective-permute-start.11 = (bf16[128,4096]{1,0:T(8,128)(2,1)S(1)}, bf16[128,4096]{1,0:T(8,128)(2,1)S(1)}, u32[]{:S(2)}, u32[]{:S(2)}) collective-permute-start(bf16[128,4096]{1,0:T(8,128)(2,1)S(1)} %copy.32), channel_id=1, source_target_pairs={{0,8},{8,0},{1,9},{9,1},{2,10},{10,2},{3,11},{11,3},{4,12},{12,4},... | collective-permute-start | bytes 3145736 | tf_op jit(solution)/shard_map/ppermute | solution.py:54
  139.2 27.5 %all-to-all-start.4 = ((bf16[8,128,512]{1,2,0:T(8,128)(2,1)}), bf16[8,128,512]{1,2,0:T(8,128)(2,1)}, u32[]{:S(2)}, u32[]{:S(2)}) async-start(bf16[8,128,512]{1,2,0:T(8,128)(2,1)} %all-to-all-done.3), calls=%async_computation.4 | async-start | bytes 2097152 | tf_op jit(solution)/shard_map/all_to_all | solution.py:58
  144.8 6.8 %copy-start.1 = (bf16[128,4096]{1,0:T(8,128)(2,1)}, bf16[128,4096]{1,0:T(8,128)(2,1)S(1)}, u32[]{:S(2)}) copy-start(bf16[128,4096]{1,0:T(8,128)(2,1)S(1)} %get-tuple-element.92) | copy-start | bytes 3145732
  151.7 22.4 %collective-permute-start.13 = (bf16[256,1024]{1,0:T(8,128)(2,1)S(1)}, bf16[256,1024]{1,0:T(8,128)(2,1)}, u32[]{:S(2)}, u32[]{:S(2)}) collective-permute-start(bf16[256,1024]{1,0:T(8,128)(2,1)S(1)} %fusion.2.grad_ref), channel_id=1, source_target_pairs={{0,1},{1,0},{2,3},{3,2},{4,5},{5,4},{6,7},{7,6},{8,9},{9,8},{10,11... | collective-permute-start | bytes 1572872 | tf_op jit(solution)/shard_map/ppermute | solution.py:54
  153.5 30.7 %collective-permute-start.14 = (bf16[256,1024]{1,0:T(8,128)(2,1)S(1)}, bf16[256,1024]{1,0:T(8,128)(2,1)}, u32[]{:S(2)}, u32[]{:S(2)}) collective-permute-start(bf16[256,1024]{1,0:T(8,128)(2,1)S(1)} %fusion.2.grad_ref), channel_id=1, source_target_pairs={{0,2},{1,3},{2,0},{3,1},{4,6},{5,7},{6,4},{7,5},{8,10},{9,11},{10,... | collective-permute-start | bytes 1572872 | tf_op jit(solution)/shard_map/ppermute | solution.py:54
  156.1 31.9 %collective-permute-start.12 = (bf16[768,512]{1,0:T(8,128)(2,1)S(1)}, bf16[768,512]{1,0:T(8,128)(2,1)}, u32[]{:S(2)}, u32[]{:S(2)}) collective-permute-start(bf16[768,512]{1,0:T(8,128)(2,1)S(1)} %pad_maximum_fusion.7), channel_id=1, source_target_pairs={{0,8},{8,0},{1,9},{9,1},{2,10},{10,2},{3,11},{11,3},{4,12},{12,4},... | collective-permute-start | bytes 2359304 | tf_op jit(solution)/shard_map/ppermute | solution.py:54
  158.0 28.1 %collective-permute-start.15 = (bf16[256,1024]{1,0:T(8,128)(2,1)S(1)}, bf16[256,1024]{1,0:T(8,128)(2,1)}, u32[]{:S(2)}, u32[]{:S(2)}) collective-permute-start(bf16[256,1024]{1,0:T(8,128)(2,1)S(1)} %fusion.2.grad_ref), channel_id=1, source_target_pairs={{0,3},{1,2},{2,1},{3,0},{4,7},{5,6},{6,5},{7,4},{8,11},{9,10},{10,... | collective-permute-start | bytes 1572872 | tf_op jit(solution)/shard_map/ppermute | solution.py:54
  165.5 30.3 %collective-permute-start.17 = (bf16[8,256,256]{2,1,0:T(8,128)(2,1)S(1)}, bf16[8,256,256]{2,1,0:T(8,128)(2,1)}, u32[]{:S(2)}, u32[]{:S(2)}) collective-permute-start(bf16[8,256,256]{2,1,0:T(8,128)(2,1)S(1)} %get-tuple-element.70), channel_id=1, source_target_pairs={{0,8},{8,0},{1,9},{9,1},{2,10},{10,2},{3,11},{11,3},{4,12},{12,4},... | collective-permute-start | bytes 3145736 | tf_op jit(solution)/shard_map/ppermute | solution.py:54
  166.7 26.8 %all-to-all-start.5 = ((bf16[8,128,512]{1,2,0:T(8,128)(2,1)}), bf16[8,128,512]{1,2,0:T(8,128)(2,1)}, u32[]{:S(2)}, u32[]{:S(2)}) async-start(bf16[8,128,512]{1,2,0:T(8,128)(2,1)} %bitcast.47), calls=%async_computation.6 | async-start | bytes 2097152 | tf_op jit(solution)/shard_map/all_to_all | solution.py:58
  174.0 24.3 %collective-permute-start.18 = (bf16[8,128,512]{1,2,0:T(8,128)(2,1)}, bf16[8,128,512]{1,2,0:T(8,128)(2,1)}, u32[]{:S(2)}, u32[]{:S(2)}) collective-permute-start(bf16[8,128,512]{1,2,0:T(8,128)(2,1)} %all-to-all-done.4), channel_id=1, source_target_pairs={{0,8},{8,0},{1,9},{9,1},{2,10},{10,2},{3,11},{11,3},{4,12},{12,4},... | collective-permute-start | bytes 3145736 | tf_op jit(solution)/shard_map/ppermute | solution.py:54
  192.6 32.8 %collective-permute-start.16 = (bf16[512,1024]{1,0:T(8,128)(2,1)}, bf16[512,1024]{1,0:T(8,128)(2,1)}, u32[]{:S(2)}, u32[]{:S(2)}) collective-permute-start(bf16[512,1024]{1,0:T(8,128)(2,1)} %convolution_convert_fusion.1), channel_id=1, source_target_pairs={{0,4},{4,0},{1,5},{5,1},{2,6},{6,2},{3,7},{7,3},{8,12},{12,8},{9,1... | collective-permute-start | bytes 3145736 | tf_op jit(solution)/shard_map/ppermute | solution.py:54
  211.5 19.7 %all-to-all-start.6 = ((bf16[8,256,256]{2,1,0:T(8,128)(2,1)}), bf16[8,256,256]{2,1,0:T(8,128)(2,1)S(1)}, u32[]{:S(2)}, u32[]{:S(2)}) async-start(bf16[8,256,256]{2,1,0:T(8,128)(2,1)} %add_convert_fusion.1), calls=%async_computation.7 | async-start | bytes 2097152 | tf_op jit(solution)/shard_map/all_to_all | solution.py:58
  220.1 1.9 collective-permute-start.19
  (16 other events, 53.5 us)
Sparse Core Ops, SparseCore 0:
  9.6 73.8 all-gather.1
  105.3 95.3 reduce-scatter.1
